TPU v7x, 32 devices: a whole 2x2x4 slice. The times are simulated.
32 devices in a mesh: dof: 16 (over z, x, core), snap: 2 (over y).
Axes of the slice: x: 2, y: 2, z: 4, core: 2. Of those that a mesh axis runs over, the one named last changes fastest.
Arguments:
- snapshots: float32 [65536, 1024], P('dof', 'snap'), may hold values from -19 to 19
Outputs:
- basis: float32 [65536, 1024], P('dof', 'snap')
- factor: float32 [1024, 1024], P(None, 'snap')
All inputs are finite; a program needn't handle non-finite values.
Results may differ from a plain program's by a relative error of at most 0.00024.
Values sent between devices are 32-bit elements; how exact they have to be, the bound alone decides.
No kernel may reach another device: no remote copies, remote signals or barrier semaphores. Data moves between devices by JAX's collectives and lax.ppermute only.
A program may use at most 128 MiB of HBM per device.

v0:
```python
import jax
import jax.numpy as jnp
from jax import lax
from jax.sharding import PartitionSpec as P


def whiten(gram):
    order = gram.shape[0]
    lower = jnp.linalg.cholesky(gram)
    identity = jnp.eye(order, dtype=jnp.float32)
    inverse = jax.scipy.linalg.solve_triangular(lower, identity, lower=True).T
    return (lower, inverse)


def on_device(snapshots):
    width = snapshots.shape[1]
    offset = lax.axis_index("snap") * width
    root_rows = jnp.sqrt(jnp.float32(snapshots.shape[0] * lax.axis_size("dof")))
    gathered = lax.all_gather(snapshots, "snap", axis=1, tiled=True)
    partial_gram = jnp.dot(
        gathered.T, snapshots, preferred_element_type=jnp.float32, precision=lax.Precision.HIGHEST
    )
    gram_accumulated = lax.psum(partial_gram, "dof")
    gram = lax.all_gather(gram_accumulated, "snap", axis=1, tiled=True)
    lower, inverse = whiten(gram)
    own_inverse = lax.dynamic_slice_in_dim(inverse, offset, width, 1)
    basis = (
        jnp.dot(
            gathered,
            own_inverse,
            preferred_element_type=jnp.float32,
            precision=lax.Precision.HIGHEST,
        )
        * root_rows
    )
    factor = lax.dynamic_slice_in_dim(lower.T, offset, width, 1) / root_rows
    return (basis, factor)


def solution(mesh):
    in_specs = (P("dof", "snap"),)
    out_specs = (P("dof", "snap"), P(None, "snap"))
    return jax.shard_map(
        on_device, mesh=mesh, in_specs=in_specs, out_specs=out_specs, check_vma=False
    )
```

profile of v0, /device:TPU:0, one launch (start us, length us, event | category | flops | bytes accessed | tf_op | source)
XLA Modules:
  0.0 795.6 jit_solution(8438589093578754183)
XLA Ops:
  7.9 203.2 %all-gather.3.cloned.1.call-done = f32[4096,1024]{1,0:T(8,128)} async-done(((f32[4096,512]{1,0:T(8,128)}), f32[4096,1024]{1,0:T(8,128)}) %all-gather.3.cloned.1.call-update) | async-done | bytes 16777232 | tf_op jit(solution)/shard_map/all_gather | solution.py:19
  211.2 31.4 %fusion.74 = f32[1024,512]{0,1:T(8,128)} fusion(f32[4096,1024]{1,0:T(8,128)} %all-gather.3.cloned.1.call-done, f32[4096,512]{1,0:T(8,128)} %param.1), kind=kOutput, calls=%fused_computation.164 | convolution fusion | flops 25769803776 | bytes 27262976 | tf_op jit(solution)/shard_map/dot_general | solution.py:20
  242.7 97.9 %all-reduce.3.cloned.1.call-done = f32[1024,512]{0,1:T(8,128)} async-done(((f32[1024,512]{0,1:T(8,128)}), f32[1024,512]{0,1:T(8,128)}) %all-reduce.3.cloned.1.call-update) | async-done | bytes 2097168 | tf_op jit(solution)/shard_map/psum | solution.py:23
  343.4 54.9 %all-gather.5.cloned.1.call-done = f32[1024,1024]{0,1:T(8,128)} async-done(((f32[1024,512]{0,1:T(8,128)}), f32[1024,1024]{0,1:T(8,128)}) %all-gather.5.cloned.1.call-update) | async-done | bytes 4194320 | tf_op jit(solution)/shard_map/all_gather | solution.py:24
  398.2 5.5 copy.4
  403.8 4.4 fusion
  410.2 11.7 %cholesky.223 = f32[128,128]{1,0:T(8,128)S(1)} custom-call(f32[128,128]{1,0:T(8,128)S(1)} %cholesky.580), custom_call_target="Cholesky" | custom-call | tf_op jit(solution)/shard_map/jit(cholesky)/cholesky | solution.py:9
  421.9 9.8 %custom-call.63 = f32[1,128,128]{1,2,0:T(8,128)S(1)} custom-call(f32[1,128,128]{2,1,0:T(8,128)S(1)} %get-tuple-element.70), custom_call_target="InvertDiagBlocksLowerTriangular" | custom-call | tf_op jit(solution)/shard_map/jit(cholesky)/cholesky | solution.py:9
  438.2 12.1 %cholesky.244 = f32[128,128]{1,0:T(8,128)S(1)} custom-call(f32[128,128]{1,0:T(8,128)S(1)} %cholesky.584), custom_call_target="Cholesky" | custom-call | tf_op jit(solution)/shard_map/jit(cholesky)/cholesky | solution.py:9
  450.9 9.8 %custom-call.64 = f32[1,128,128]{1,2,0:T(8,128)S(1)} custom-call(f32[1,128,128]{2,1,0:T(8,128)S(1)} %get-tuple-element.67), custom_call_target="InvertDiagBlocksLowerTriangular" | custom-call | tf_op jit(solution)/shard_map/jit(cholesky)/cholesky | solution.py:9
  464.0 11.7 %cholesky.468 = f32[128,128]{1,0:T(8,128)S(1)} custom-call(f32[128,128]{1,0:T(8,128)S(1)} %cholesky.589), custom_call_target="Cholesky" | custom-call | tf_op jit(solution)/shard_map/jit(cholesky)/cholesky | solution.py:9
  477.0 9.8 %custom-call.65 = f32[1,128,128]{1,2,0:T(8,128)S(1)} custom-call(f32[1,128,128]{2,1,0:T(8,128)S(1)} %get-tuple-element.64), custom_call_target="InvertDiagBlocksLowerTriangular" | custom-call | tf_op jit(solution)/shard_map/jit(cholesky)/cholesky | solution.py:9
  490.3 11.8 %cholesky.487 = f32[128,128]{1,0:T(8,128)S(1)} custom-call(f32[128,128]{1,0:T(8,128)S(1)} %cholesky.594), custom_call_target="Cholesky" | custom-call | tf_op jit(solution)/shard_map/jit(cholesky)/cholesky | solution.py:9
  503.5 9.8 %custom-call.66 = f32[1,128,128]{1,2,0:T(8,128)S(1)} custom-call(f32[1,128,128]{2,1,0:T(8,128)S(1)} %get-tuple-element.61), custom_call_target="InvertDiagBlocksLowerTriangular" | custom-call | tf_op jit(solution)/shard_map/jit(cholesky)/cholesky | solution.py:9
  516.7 11.7 %cholesky.506 = f32[128,128]{1,0:T(8,128)S(1)} custom-call(f32[128,128]{1,0:T(8,128)S(1)} %cholesky.599), custom_call_target="Cholesky" | custom-call | tf_op jit(solution)/shard_map/jit(cholesky)/cholesky | solution.py:9
  529.7 10.0 %custom-call.67 = f32[1,128,128]{1,2,0:T(8,128)S(1)} custom-call(f32[1,128,128]{2,1,0:T(8,128)S(1)} %get-tuple-element.58), custom_call_target="InvertDiagBlocksLowerTriangular" | custom-call | tf_op jit(solution)/shard_map/jit(cholesky)/cholesky | solution.py:9
  543.1 11.7 %cholesky.526 = f32[128,128]{1,0:T(8,128)S(1)} custom-call(f32[128,128]{1,0:T(8,128)S(1)} %cholesky.604), custom_call_target="Cholesky" | custom-call | tf_op jit(solution)/shard_map/jit(cholesky)/cholesky | solution.py:9
  556.1 9.8 %custom-call.68 = f32[1,128,128]{1,2,0:T(8,128)S(1)} custom-call(f32[1,128,128]{2,1,0:T(8,128)S(1)} %get-tuple-element.55), custom_call_target="InvertDiagBlocksLowerTriangular" | custom-call | tf_op jit(solution)/shard_map/jit(cholesky)/cholesky | solution.py:9
  568.9 12.2 %cholesky.546 = f32[128,128]{1,0:T(8,128)S(1)} custom-call(f32[128,128]{1,0:T(8,128)S(1)} %cholesky.609), custom_call_target="Cholesky" | custom-call | tf_op jit(solution)/shard_map/jit(cholesky)/cholesky | solution.py:9
  582.4 9.8 %custom-call.69 = f32[1,128,128]{1,2,0:T(8,128)S(1)} custom-call(f32[1,128,128]{2,1,0:T(8,128)S(1)} %get-tuple-element.52), custom_call_target="InvertDiagBlocksLowerTriangular" | custom-call | tf_op jit(solution)/shard_map/jit(cholesky)/cholesky | solution.py:9
  594.8 11.7 %cholesky.564 = f32[128,128]{1,0:T(8,128)S(1)} custom-call(f32[128,128]{1,0:T(8,128)S(1)} %convolution_subtract_fusion.11), custom_call_target="Cholesky" | custom-call | tf_op jit(solution)/shard_map/jit(cholesky)/cholesky | solution.py:9
  613.3 4.9 fusion.1
  620.2 27.7 %while.1 = (s32[]{:T(128)}, f32[1024,1024]{1,0:T(8,128)}, s32[8,2]{0,1:T(2,128)S(1)}, f32[8,128,128]{2,1,0:T(8,128)}, s32[]{:T(128)}) while((s32[]{:T(128)}, f32[1024,1024]{1,0:T(8,128)}, s32[8,2]{0,1:T(2,128)S(1)}, f32[8,128,128]{2,1,0:T(8,128)}, s32[]{:T(128)}) %tuple.63), condition=%wide.while_cond, body=%wide.while_body.sunk | while | flops 2 | bytes 132205 | solution.py:11
  620.8 2.8 bitcast_dynamic-update-slice_fusion.2
  627.8 2.8 bitcast_dynamic-update-slice_fusion.2
  634.7 2.8 bitcast_dynamic-update-slice_fusion.2
  638.2 2.8 bitcast_dynamic-update-slice_fusion.2
  641.7 2.8 bitcast_dynamic-update-slice_fusion.2
  647.9 79.6 %custom-call.70 = f32[8,128,128]{1,2,0:T(8,128)S(1)} custom-call(f32[8,128,128]{2,1,0:T(8,128)} %get-tuple-element.9), custom_call_target="InvertDiagBlocksLowerTriangular" | custom-call | tf_op jit(solution)/shard_map/jit(_solve_triangular)/triangular_solve | solution.py:11
  746.1 3.6 convolution_subtract_fusion.3
  750.4 29.3 %multiply_bitcast_fusion = f32[4096,512]{0,1:T(8,128)} fusion(f32[4096,1024]{1,0:T(8,128)S(1)} %bitcast.109, f32[1024,1024]{1,0:T(8,128)S(1)} %convolution_dynamic-update-slice_fusion, s32[]{:T(128)S(6)} %select_n.9), kind=kOutput, calls=%fused_computation.2 | convolution fusion | flops 25771900928 | bytes 27262980 | tf_op jit(solution)/shard_map/dot_general | solution.py:28
  779.7 8.9 %copy.5 = f32[4096,512]{1,0:T(8,128)} copy(f32[4096,512]{0,1:T(8,128)} %multiply_bitcast_fusion) | data formatting | bytes 16777216
  (96 shorter events, 74.7 us)
Async XLA Ops:
  7.2 204.0 %all-gather.3.cloned.1.call-start = ((), (), s32[]{:S(2)}) async-start(), calls=%async_computation | async-start | bytes 25165824 | tf_op jit(solution)/shard_map/all_gather | solution.py:19
  7.9 332.7 %all-reduce.3.cloned.1.call-start = ((), (), s32[]{:S(2)}) async-start(), calls=%async_computation.1 | async-start | bytes 4194304 | tf_op jit(solution)/shard_map/psum | solution.py:23
  242.6 155.6 %all-gather.5.cloned.1.call-start = ((), (), s32[]{:S(2)}) async-start(), calls=%async_computation.2 | async-start | bytes 6291456 | tf_op jit(solution)/shard_map/all_gather | solution.py:24
  408.2 2.0 copy-start.1
  727.5 3.2 copy-start
  733.1 17.3 %slice-start = ((s8[16777216]{0:T(1024)(128)(4,1)}), s8[4194304]{0:T(1024)(128)(4,1)S(1)}, s32[]{:S(2)}) async-start(s8[16777216]{0:T(1024)(128)(4,1)} %bitcast.108), calls=%async_computation.3 | async-start | bytes 8388608
  736.0 14.3 %slice-start.1 = ((s8[16777216]{0:T(1024)(128)(4,1)}), s8[4194304]{0:T(1024)(128)(4,1)S(1)}, s32[]{:S(2)}) async-start(s8[16777216]{0:T(1024)(128)(4,1)} %bitcast.108), calls=%async_computation.4 | async-start | bytes 8388608
  739.2 11.2 %slice-start.2 = ((s8[16777216]{0:T(1024)(128)(4,1)}), s8[4194304]{0:T(1024)(128)(4,1)S(1)}, s32[]{:S(2)}) async-start(s8[16777216]{0:T(1024)(128)(4,1)} %bitcast.108), calls=%async_computation.5 | async-start | bytes 8388608
  745.5 4.9 slice-start.3
Sparse Core Ops, SparseCore 0:
  9.6 201.5 all-gather.2
  242.7 97.7 all-reduce.2
  342.2 55.9 all-gather.4
where the time goes:
time: 803 us; the launch traced here: 796 us
  waiting for transfers between devices  357 us (44%)
  other arithmetic  264 us (33%)
  matrix products  106 us (13%)
  local copies, waits for them, and re-layouts  48.5 us (6%)
  between operations  19.4 us (2%)
    all_gather x1, waiting for transfers between devices, on_device(): gathered = lax.all_gather(snapshots, 'snap', axis=1, tiled=True)  203 us
    another operation x30, other arithmetic, whiten(): lower = jnp.linalg.cholesky(gram)  173 us
    psum x1, waiting for transfers between devices, on_device(): gram_accumulated = lax.psum(partial_gram, 'dof')  97.9 us
    another operation x3, other arithmetic, whiten(): inverse = jax.scipy.linalg.solve_triangular(lower, identity, lower=True).T  84.5 us
    all_gather x1, waiting for transfers between devices, on_device(): gram = lax.all_gather(gram_accumulated, 'snap', axis=1, tiled=True)  54.9 us
    dot_general x1, matrix products, on_device(): jnp.dot(gathered.T, snapshots, preferred_element_type=jnp.float32, precis...  31.4 us
    dot_general x1, matrix products, on_device(): jnp.dot(gathered, own_inverse, preferred_element_type=jnp.float32, precis...  29.3 us
    another operation x24, local copies, waits for them, and re-layouts  27.7 us
  transfers between devices with their start and end apart: 3, of which 3 were waited for; matrix products, arithmetic and copies ran while one was open for 0% of the time, Pallas kernels for 0%

commit v1 on v0

v1 whole, which is shorter than its diff:
```python
import functools

import jax
import jax.numpy as jnp
from jax import lax
from jax.experimental import pallas as pl
from jax.experimental.pallas import tpu as pltpu
from jax.sharding import PartitionSpec as P

F32 = jnp.float32
BF16 = jnp.bfloat16
HIGHEST = lax.Precision.HIGHEST
VMEM = pltpu.VMEM
BLOCK = 128
GROUP = 8
TILE = 512


def params(megabytes):
    return pltpu.CompilerParams(vmem_limit_bytes=megabytes * 1024 * 1024)


def whole(count):
    return [pl.BlockSpec(memory_space=VMEM)] * count


def dot(a, b, contract, precision=None):
    return lax.dot_general(
        a, b, ((contract[:1], contract[1:]), ((), ())), precision=precision, preferred_element_type=F32
    )


def split(x):
    high = x.astype(BF16)
    return high, (x - high.astype(F32)).astype(BF16)


def dot3(a, b, contract):
    ah, al = split(a)
    bh, bl = split(b)
    return dot(ah, bh, contract) + (dot(ah, bl, contract) + dot(al, bh, contract))


def own_gram_kernel(scale, s_ref, g_ref, high_acc, mixed_acc):
    step = pl.program_id(0)

    @pl.when(step == 0)
    def _():
        high_acc[...] = jnp.zeros_like(high_acc)
        mixed_acc[...] = jnp.zeros_like(mixed_acc)

    high, low = split(s_ref[...])
    high_acc[...] += dot(high, high, (0, 0)) + dot(low, low, (0, 0))
    mixed_acc[...] += dot(high, low, (0, 0))

    @pl.when(step == pl.num_programs(0) - 1)
    def _():
        mixed = mixed_acc[...]
        g_ref[...] = (high_acc[...] + (mixed + mixed.T)) * scale


def own_gram(s, scale):
    rows, width = s.shape
    square = (width, width)
    return pl.pallas_call(
        functools.partial(own_gram_kernel, scale),
        grid=(rows // TILE,),
        out_shape=jax.ShapeDtypeStruct(square, F32),
        in_specs=[pl.BlockSpec((TILE, width), lambda i: (i, 0))],
        out_specs=pl.BlockSpec(square, lambda i: (0, 0)),
        scratch_shapes=[pltpu.VMEM(square, F32), pltpu.VMEM(square, F32)],
        compiler_params=params(40),
        cost_estimate=pl.CostEstimate(
            flops=6 * rows * width * width, bytes_accessed=4 * rows * width, transcendentals=0
        ),
        name="own_gram",
    )(s)


def cross_gram_kernel(scale, side_ref, own_ref, other_ref, before_ref, g_ref):
    step = pl.program_id(0)

    @pl.when(step == 0)
    def _():
        g_ref[...] = before_ref[...]

    first = side_ref[0] == 0
    own, other = own_ref[...], other_ref[...]
    left = jnp.where(first, own, other)
    right = jnp.where(first, other, own)
    lh, ll = split(left)
    rh, rl = split(right * scale)
    g_ref[...] += (dot(lh, rh, (0, 0)) + dot(ll, rl, (0, 0))) + (dot(lh, rl, (0, 0)) + dot(ll, rh, (0, 0)))


def cross_gram(side, own, other, before, offset, scale):
    width = own.shape[1]
    rows = other.shape[0]
    square = (width, width)
    tile = min(TILE, rows)
    half = own.shape[0] // 2 // tile
    start = offset // tile
    return pl.pallas_call(
        functools.partial(cross_gram_kernel, scale),
        grid_spec=pltpu.PrefetchScalarGridSpec(
            num_scalar_prefetch=1,
            grid=(rows // tile,),
            in_specs=[
                pl.BlockSpec((tile, width), lambda i, side: (i + start + (1 - side[0]) * half, 0)),
                pl.BlockSpec((tile, width), lambda i, side: (i, 0)),
                pl.BlockSpec(square, lambda i, side: (0, 0)),
            ],
            out_specs=pl.BlockSpec(square, lambda i, side: (0, 0)),
        ),
        out_shape=jax.ShapeDtypeStruct(square, F32),
        compiler_params=params(40),
        cost_estimate=pl.CostEstimate(
            flops=8 * rows * width * width, bytes_accessed=8 * rows * width, transcendentals=0
        ),
        name="cross_gram",
    )(side, own, other, before)


def factor_block(a, x):
    count, width = len(a), a[0].shape[1]
    shape = (GROUP, width)
    row = lax.broadcasted_iota(jnp.int32, shape, 0)
    lane = lax.broadcasted_iota(jnp.int32, shape, 1)
    upper, inverse = [], []
    for p in range(count):
        c = GROUP * p
        pa = [jnp.broadcast_to(a[p][k : k + 1, :], shape) for k in range(GROUP)]
        px = [jnp.broadcast_to(x[p][k : k + 1, :], shape) for k in range(GROUP)]
        s = [
            [jnp.broadcast_to(pa[k][:, c + l : c + l + 1], shape) if l >= k else None for l in range(GROUP)]
            for k in range(GROUP)
        ]
        reciprocal = []
        for k in range(GROUP):
            reciprocal.append(1.0 / s[k][k])
            for l in range(k + 1, GROUP):
                m = s[k][l] * reciprocal[k]
                for t in range(l, GROUP):
                    s[l][t] = s[l][t] - m * s[k][t]
                pa[l] = pa[l] - m * pa[k]
                px[l] = px[l] - m * px[k]
        for r in range(p + 1, count):
            columns = [jnp.broadcast_to(a[r][:, c + l : c + l + 1], shape) for l in range(GROUP)]
            for k in range(GROUP):
                m = columns[k] * reciprocal[k]
                for t in range(k + 1, GROUP):
                    columns[t] = columns[t] - m * s[k][t]
                a[r] = a[r] - m * pa[k]
                x[r] = x[r] - m * px[k]
        ua, ux = None, None
        for k in range(GROUP):
            root = lax.rsqrt(s[k][k])
            va, vx = pa[k] * root, px[k] * root
            ua = va if k == 0 else jnp.where(row == k, va, ua)
            ux = vx if k == 0 else jnp.where(row == k, vx, ux)
        upper.append(jnp.where(lane >= row + c, ua, 0.0))
        inverse.append(ux)
    return upper, inverse


def factor_whole(a_ref, r_ref, x_ref, e_ref):
    order = a_ref.shape[0]
    blocks = order // BLOCK
    groups = BLOCK // GROUP
    r_ref[...] = jnp.zeros_like(r_ref)
    x_ref[...] = jnp.zeros_like(x_ref)
    row = lax.broadcasted_iota(jnp.int32, (GROUP, BLOCK), 0)
    lane = lax.broadcasted_iota(jnp.int32, (GROUP, BLOCK), 1)

    def body(b, carry):
        start = pl.multiple_of(b * BLOCK, BLOCK)
        here = pl.ds(start, BLOCK)
        a = [a_ref[pl.ds(start + GROUP * i, GROUP), here] for i in range(groups)]
        x = [jnp.where(lane == row + GROUP * i, 1.0, 0.0) for i in range(groups)]
        upper, inverse = factor_block(a, x)
        for i in range(groups):
            r_ref[pl.ds(start + GROUP * i, GROUP), here] = upper[i]
            e_ref[pl.ds(GROUP * i, GROUP), :] = inverse[i]
        for k in range(blocks):

            @pl.when(b == k)
            def _():
                lo, hi = k * BLOCK, (k + 1) * BLOCK
                e = e_ref[...]
                x_ref[lo:hi, lo:hi] = e
                if k > 0:
                    x_ref[lo:hi, :lo] = dot(e, x_ref[lo:hi, :lo], (1, 0), HIGHEST)
                if hi < order:
                    strip = dot(e, a_ref[lo:hi, hi:], (1, 0), HIGHEST)
                    r_ref[lo:hi, hi:] = strip
                    a_ref[hi:, hi:] -= dot(strip, strip, (0, 0), HIGHEST)
                    x_ref[hi:, :hi] -= dot(strip, x_ref[lo:hi, :hi], (0, 0), HIGHEST)

        return carry

    lax.fori_loop(0, blocks, body, 0)


def first_factor_kernel(g_ref, r_ref, x_ref, a_ref, e_ref):
    a_ref[...] = g_ref[...]
    factor_whole(a_ref, r_ref, x_ref, e_ref)


def first_factor(gram):
    order = gram.shape[0]
    square = jax.ShapeDtypeStruct((order, order), F32)
    return pl.pallas_call(
        first_factor_kernel,
        out_shape=[square, square],
        in_specs=whole(1),
        out_specs=whole(2),
        scratch_shapes=[pltpu.VMEM((order, order), F32), pltpu.VMEM((BLOCK, BLOCK), F32)],
        compiler_params=params(40),
        cost_estimate=pl.CostEstimate(flops=30 * order**3, bytes_accessed=12 * order * order, transcendentals=0),
        name="first_factor",
    )(gram)


def second_factor_kernel(cross_ref, gram_ref, x0_ref, r01_ref, r_ref, x_ref, w01_ref, a_ref, e_ref):
    x0 = x0_ref[...]
    r01 = dot(x0, cross_ref[...], (1, 0), HIGHEST)
    r01_ref[...] = r01
    a_ref[...] = gram_ref[...] - dot(r01, r01, (0, 0), HIGHEST)
    factor_whole(a_ref, r_ref, x_ref, e_ref)
    u = dot(x0, r01_ref[...], (0, 0), HIGHEST)
    w01_ref[...] = -dot(u, x_ref[...], (1, 1), HIGHEST)


def second_factor(cross, gram, x0):
    order = gram.shape[0]
    square = jax.ShapeDtypeStruct((order, order), F32)
    return pl.pallas_call(
        second_factor_kernel,
        out_shape=[square] * 4,
        in_specs=whole(3),
        out_specs=whole(4),
        scratch_shapes=[pltpu.VMEM((order, order), F32), pltpu.VMEM((BLOCK, BLOCK), F32)],
        compiler_params=params(40),
        cost_estimate=pl.CostEstimate(flops=60 * order**3, bytes_accessed=28 * order * order, transcendentals=0),
        name="second_factor",
    )(cross, gram, x0)


def basis_kernel(counts, side_ref, own_ref, *refs):
    chunks = refs[: len(counts)]
    x0_ref, x1_ref, w01_ref, out_ref, oh, ol, ch, cl = refs[len(counts) :]
    step = pl.program_id(0)

    @pl.when(step == 0)
    def _():
        first = side_ref[0] == 0
        own = jnp.where(first, x0_ref[...], x1_ref[...]).T
        oh[...], ol[...] = split(own)
        cross = jnp.where(first, 0.0, w01_ref[...])
        ch[...], cl[...] = split(cross)

    def product(x, high, low):
        xh, xl = split(x)
        return dot(xh, high[...], (1, 0)) + (dot(xh, low[...], (1, 0)) + dot(xl, high[...], (1, 0)))

    start = 0
    for chunk, count in zip(chunks, counts):

        @pl.when((step >= start) & (step < start + count))
        def _():
            out_ref[...] = product(own_ref[...], oh, ol) + product(chunk[...], ch, cl)

        start += count


def whitened(side, own, chunks, x0, x1, w01):
    rows, width = own.shape
    counts = tuple(c.shape[0] // TILE for c in chunks)
    starts = [sum(counts[:i]) for i in range(len(counts))]
    square = (width, width)

    def chunk_spec(start, count):
        return pl.BlockSpec((TILE, width), lambda i, side: (jnp.clip(i - start, 0, count - 1), 0))

    fixed = pl.BlockSpec(square, lambda i, side: (0, 0))
    return pl.pallas_call(
        functools.partial(basis_kernel, counts),
        grid_spec=pltpu.PrefetchScalarGridSpec(
            num_scalar_prefetch=1,
            grid=(rows // TILE,),
            in_specs=[pl.BlockSpec((TILE, width), lambda i, side: (i, 0))]
            + [chunk_spec(s, c) for s, c in zip(starts, counts)]
            + [fixed] * 3,
            out_specs=pl.BlockSpec((TILE, width), lambda i, side: (i, 0)),
            scratch_shapes=[pltpu.VMEM(square, BF16)] * 4,
        ),
        out_shape=jax.ShapeDtypeStruct((rows, width), F32),
        compiler_params=params(48),
        cost_estimate=pl.CostEstimate(
            flops=12 * rows * width * width, bytes_accessed=12 * rows * width, transcendentals=0
        ),
        name="whitened",
    )(side, own, *chunks, x0, x1, w01)


def flip(x, bit):
    count = lax.axis_size("dof")
    return lax.ppermute(x, "dof", [(i, i ^ bit) for i in range(count)])


def flip_side(x, bit):
    count = lax.axis_size("dof") * 2
    return lax.ppermute(x, ("dof", "snap"), [(i, i ^ (2 * bit + 1)) for i in range(count)])


def halve(x, upper, send):
    half = x.shape[0] // 2
    low, high = x[:half], x[half:]
    return jnp.where(upper, high, low) + send(jnp.where(upper, low, high))


def double(x, upper, send):
    other = send(x)
    return jnp.concatenate([jnp.where(upper, other, x), jnp.where(upper, x, other)])


def on_device(snapshots):
    rows, width = snapshots.shape
    count = lax.axis_size("dof")
    scale = 1.0 / (rows * count)
    me, side = lax.axis_index("dof"), lax.axis_index("snap")
    side_operand = jnp.full((1,), side, jnp.int32)
    across = 2
    outer = [1] + [1 << i for i in range(2, count.bit_length() - 1)]

    def bit(k):
        return (me & k) != 0

    half = rows // 2
    quarter = half // 2
    swap = [(0, 1), (1, 0)]
    sent = [lax.dynamic_slice_in_dim(snapshots, side * half + j * quarter, quarter, 0) for j in range(2)]
    arrived = [lax.ppermute(x, "snap", swap) for x in sent]
    rest = lax.ppermute(snapshots[half:], "snap", [(0, 1)])

    own = own_gram(snapshots, scale)
    second = lax.psum(own, "dof")
    shard = own
    for k in outer + [across]:
        shard = halve(shard, bit(k), functools.partial(flip, bit=k))
    received = flip_side(shard, across)
    shard = jnp.where(side == 0, shard, received)
    shard = double(shard, bit(across) ^ (side == 1), functools.partial(flip, bit=across))
    for k in outer[::-1]:
        shard = double(shard, bit(k), functools.partial(flip, bit=k))
    r00, x00 = first_factor(shard)

    cross = jnp.zeros((width, width), F32)
    for j in range(2):
        cross = cross_gram(side_operand, snapshots, arrived[j], cross, j * quarter, scale)
    for k in outer:
        cross = halve(cross, bit(k), functools.partial(flip, bit=k))
    cross = halve(cross, side == 1, functools.partial(flip_side, bit=across))
    cross = cross + flip(cross, across)
    cross = double(cross, side == 1, functools.partial(flip_side, bit=across))
    for k in outer[::-1]:
        cross = double(cross, bit(k), functools.partial(flip, bit=k))

    r01, r11, x11, w01 = second_factor(cross, second, x00)
    basis = whitened(side_operand, snapshots, arrived + [rest], x00, x11, w01)
    factor = jnp.concatenate([jnp.where(side == 0, r00, r01), jnp.where(side == 0, 0.0, r11)])
    return (basis, factor)


def solution(mesh):
    in_specs = (P("dof", "snap"),)
    out_specs = (P("dof", "snap"), P(None, "snap"))
    return jax.shard_map(
        on_device, mesh=mesh, in_specs=in_specs, out_specs=out_specs, check_vma=False
    )
```

time: 803 us -> 314 us (0.39)
  other arithmetic: 264 us -> 5.65 us
  waiting for transfers between devices: 357 us -> 169 us
  matrix products: 106 us -> 0 us
  Pallas kernels: 0 us -> 82.2 us
  local copies, waits for them, and re-layouts: 48.5 us -> 12.2 us
  starting transfers between devices: 0.12 us -> 29.5 us
    all_gather x2 -> x0, waiting for transfers between devices: 258 us -> none  [the longest x1 203 us: on_device(): gathered = lax.all_gather(snapshots, 'snap', axis=1, tiled=True)]
    another operation x33 -> x0, other arithmetic: 257 us -> none  [the longest x30 173 us: whiten(): lower = jnp.linalg.cholesky(gram)]
    ppermute x0 -> x21, waiting for transfers between devices: none -> 102 us  [the longest x2 64.8 us: on_device(): arrived = [lax.ppermute(x, 'snap', swap) for x in sent]]
    pallas_call x0 -> x6, Pallas kernels: none -> 82.2 us  [the longest x1 26.9 us: second_factor(): pl.pallas_call(second_factor_kernel, out_shape=[square] * 4, in_specs=who...]
    dot_general x2 -> x0, matrix products: 60.7 us -> none  [the longest x1 31.4 us: on_device(): jnp.dot(gathered.T, snapshots, preferred_element_type=jnp.float32, precis...]
    another operation x29 -> x0, matrix products: 45.6 us -> none  [the longest x14 22.9 us: whiten(): lower = jnp.linalg.cholesky(gram)]
    another operation x33 -> x0, local copies, waits for them, and re-layouts: 30.3 us -> none
    psum x1, waiting for transfers between devices: 97.9 us -> 67.8 us  [on_device(): second = lax.psum(own, 'dof')]
  transfers between devices with their start and end apart: 3 -> 22, of which waited for: 3 -> 14; matrix products, arithmetic and copies ran while one was open for 0% -> 3% of each run, Pallas kernels for 0% -> 20%
where the time goes in v1:
time: 314 us; the launch traced here: 313 us
  waiting for transfers between devices  169 us (54%)
  Pallas kernels  82.2 us (26%)
  starting transfers between devices  29.5 us (9%)
  between operations  14.4 us (5%)
  local copies, waits for them, and re-layouts  12.2 us (4%)
  other arithmetic  5.65 us (2%)
    psum x1, waiting for transfers between devices, on_device(): second = lax.psum(own, 'dof')  67.8 us
    ppermute x2, waiting for transfers between devices, on_device(): arrived = [lax.ppermute(x, 'snap', swap) for x in sent]  64.8 us
    ppermute x15, waiting for transfers between devices, flip(): return lax.ppermute(x, 'dof', [(i, i ^ bit) for i in range(count)])  29 us
    pallas_call x1, Pallas kernels, second_factor(): pl.pallas_call(second_factor_kernel, out_shape=[square] * 4, in_specs=who...  26.9 us
    pallas_call x1, Pallas kernels, first_factor(): pl.pallas_call(first_factor_kernel, out_shape=[square, square], in_specs=...  19.6 us
    ppermute x15, starting transfers between devices, flip(): return lax.ppermute(x, 'dof', [(i, i ^ bit) for i in range(count)])  18.7 us
    pallas_call x1, Pallas kernels, whitened(): pl.pallas_call(functools.partial(basis_kernel, counts), grid_spec=pltpu.P...  18.7 us
    pallas_call x1, Pallas kernels, own_gram(): pl.pallas_call(functools.partial(own_gram_kernel, scale), grid=(rows // T...  9.75 us
  transfers between devices with their start and end apart: 22, of which 14 were waited for; matrix products, arithmetic and copies ran while one was open for 3% of the time, Pallas kernels for 20%

profile of v1, /device:TPU:0, one launch (start us, length us, event | category | flops | bytes accessed | tf_op | source)
XLA Modules:
  0.0 313.2 jit_solution(7768575357209697224)
XLA Ops:
  7.2 5.0 %constant_dynamic-slice_fusion = (f32[1024,512]{1,0:T(8,128)}, f32[1024,512]{1,0:T(8,128)}) fusion(f32[4096,512]{1,0:T(8,128)} %own_ref.5, s32[]{:T(128)S(6)} %select_n.175, s32[]{:T(128)S(6)} %select_n.174), kind=kLoop, calls=%fused_computation.44 | loop fusion | bytes 8388616 | tf_op jit(solution)/shard_map/dynamic_slice | solution.py:342
  12.2 3.0 collective-permute-start.1
  15.2 9.8 %own_gram.1 = f32[512,512]{1,0:T(8,128)} custom-call(f32[4096,512]{1,0:T(8,128)S(1)} %copy-done), custom_call_target="tpu_custom_call" | custom-call | flops 6442450944 | bytes 8388608 | tf_op jit(solution)/shard_map/own_gram/pallas_call | solution.py:65
  26.3 1.9 collective-permute-done.3
  29.6 2.1 collective-permute-start.4
  31.7 6.6 %collective-permute-done.4 = f32[128,512]{1,0:T(8,128)S(1)} collective-permute-done((f32[128,512]{1,0:T(8,128)S(1)}, f32[128,512]{1,0:T(8,128)S(1)}, u32[]{:S(2)}, u32[]{:S(2)}) %collective-permute-start.4) | collective-permute-done | bytes 262176 | tf_op jit(solution)/shard_map/ppermute | solution.py:308
  38.4 2.8 collective-permute-start.5
  41.2 64.8 %collective-permute-done.other_ref.refs_0_ = f32[1024,512]{1,0:T(8,128)} collective-permute-done((f32[1024,512]{1,0:T(8,128)}, f32[1024,512]{1,0:T(8,128)}, u32[]{:S(2)}, u32[]{:S(2)}) %collective-permute-start) | collective-permute-done | bytes 2097184 | tf_op jit(solution)/shard_map/ppermute | solution.py:343
  106.1 3.4 %copy-done.1 = f32[4096,512]{1,0:T(8,128)S(1)} copy-done((f32[4096,512]{1,0:T(8,128)S(1)}, f32[4096,512]{1,0:T(8,128)}, u32[]{:S(2)}) %copy-start.1) | copy-done | bytes 8388632
  109.5 4.2 %cross_gram.2.before_ref = f32[512,512]{1,0:T(8,128)S(1)} custom-call(s32[1]{0:T(128)} %bitcast.side_ref, f32[4096,512]{1,0:T(8,128)S(1)} %copy-done.1, f32[1024,512]{1,0:T(8,128)} %collective-permute-done.other_ref.refs_0_, f32[512,512]{1,0:T(8,128)S(1)} %broadcast_in_dim.9.before_ref), custom_call_target="tpu_custom_call" | custom-call | flops 2147483648 | bytes 4194304 | tf_op jit(solution)/shard_map/cross_gram/pallas_call | solution.py:103
  113.8 3.0 cross_gram.3
  117.0 1.8 collective-permute-start.6
  118.8 2.8 collective-permute-done.6
  121.6 2.7 collective-permute-start.7
  124.5 1.6 collective-permute-start.13
  126.2 2.5 slice.51
  128.6 4.4 %collective-permute-start.2 = (f32[2048,512]{1,0:T(8,128)}, f32[2048,512]{1,0:T(8,128)}, u32[]{:S(2)}, u32[]{:S(2)}) collective-permute-start(f32[2048,512]{1,0:T(8,128)} %slice.51), channel_id=1, source_target_pairs={{0,1},{2,3},{4,5},{6,7},{8,9},{10,11},{12,13},{14,15},{16,17},{18,... | collective-permute-start | bytes 12582920 | tf_op jit(solution)/shard_map/ppermute | solution.py:344
  133.7 2.7 collective-permute-start.14
  137.4 3.9 %collective-permute-done.14 = f32[64,512]{1,0:T(8,128)S(1)} collective-permute-done((f32[64,512]{1,0:T(8,128)S(1)}, f32[64,512]{1,0:T(8,128)S(1)}, u32[]{:S(2)}, u32[]{:S(2)}) %collective-permute-start.14) | collective-permute-done | bytes 131104 | tf_op jit(solution)/shard_map/ppermute | solution.py:308
  142.6 4.1 %collective-permute-done.15 = f32[32,512]{1,0:T(8,128)S(1)} collective-permute-done((f32[32,512]{1,0:T(8,128)S(1)}, f32[32,512]{1,0:T(8,128)S(1)}, u32[]{:S(2)}, u32[]{:S(2)}) %collective-permute-start.15) | collective-permute-done | bytes 65568 | tf_op jit(solution)/shard_map/ppermute | solution.py:313
  146.6 2.1 collective-permute-start.16
  149.3 1.7 collective-permute-done.16
  152.6 3.7 %collective-permute-done.17 = f32[32,512]{1,0:T(8,128)S(1)} collective-permute-done((f32[32,512]{1,0:T(8,128)S(1)}, f32[32,512]{1,0:T(8,128)S(1)}, u32[]{:S(2)}, u32[]{:S(2)}) %collective-permute-start.17) | collective-permute-done | bytes 65568 | tf_op jit(solution)/shard_map/ppermute | solution.py:313
  156.3 1.4 collective-permute-start.18
  157.7 1.7 collective-permute-done.10
  159.5 3.8 %collective-permute-done.18 = f32[64,512]{1,0:T(8,128)S(1)} collective-permute-done((f32[64,512]{1,0:T(8,128)S(1)}, f32[64,512]{1,0:T(8,128)S(1)}, u32[]{:S(2)}, u32[]{:S(2)}) %collective-permute-start.18) | collective-permute-done | bytes 131104 | tf_op jit(solution)/shard_map/ppermute | solution.py:308
  164.8 5.0 %collective-permute-done.19 = f32[128,512]{1,0:T(8,128)S(1)} collective-permute-done((f32[128,512]{1,0:T(8,128)S(1)}, f32[128,512]{1,0:T(8,128)S(1)}, u32[]{:S(2)}, u32[]{:S(2)}) %collective-permute-start.19) | collective-permute-done | bytes 262176 | tf_op jit(solution)/shard_map/ppermute | solution.py:308
  170.2 19.6 %first_factor.1 = (f32[512,512]{1,0:T(8,128)S(1)}, f32[512,512]{1,0:T(8,128)S(1)}) custom-call(f32[512,512]{1,0:T(8,128)S(1)} %pad_maximum_fusion.1.g_ref), custom_call_target="tpu_custom_call" | custom-call | flops 4026531840 | bytes 3145728 | tf_op jit(solution)/shard_map/first_factor/pallas_call | solution.py:212
  190.0 67.8 %all-reduce.2.cloned.1.call-done.gram_ref = f32[512,512]{1,0:T(8,128)} async-done(((f32[512,512]{1,0:T(8,128)}), f32[512,512]{1,0:T(8,128)}) %all-reduce.2.cloned.1.call-update) | async-done | bytes 1048592 | tf_op jit(solution)/shard_map/psum | solution.py:347
  259.0 26.9 %second_factor.1 = (f32[512,512]{1,0:T(8,128)S(1)}, f32[512,512]{1,0:T(8,128)S(1)}, f32[512,512]{1,0:T(8,128)S(1)}, f32[512,512]{1,0:T(8,128)S(1)}) custom-call(f32[512,512]{1,0:T(8,128)S(1)} %pad_maximum_fusion.2.cross_ref, f32[512,512]{1,0:T(8,128)S(1)} %copy-done.3, f32[512,512]{1,0:T(8,128)S(1)} %get-tuple-element.8.x0_ref.refs_3_), custom_call_target="tpu_custom_call" | custom-call | flops 8053063680 | bytes 7340032 | tf_op jit(solution)/shard_map/second_factor/pallas_call | solution.py:237
  286.2 1.5 pad_maximum_fusion
  287.7 18.7 %whitened.1 = f32[4096,512]{1,0:T(8,128)} custom-call(s32[1]{0:T(128)} %bitcast.side_ref, f32[4096,512]{1,0:T(8,128)} %own_ref.5, f32[1024,512]{1,0:T(8,128)} %collective-permute-done.other_ref.refs_0_, f32[1024,512]{1,0:T(8,128)} %copy-done.2, f32[2048,512]{1,0:T(8,128)} %collective-permute-done.2.refs_2_, f32[512,512]{1,0:T(8,128)S(1)} %get-tuple-element.8.x0_ref.refs_3_, ...), custom_call_target="tpu_custom_call" | custom-call | flops 12884901888 | bytes 25165824 | tf_op jit(solution)/shard_map/whitened/pallas_call | solution.py:286
  (66 shorter events, 12.0 us)
Async XLA Ops:
  7.2 8.0 %copy-start = (f32[4096,512]{1,0:T(8,128)S(1)}, f32[4096,512]{1,0:T(8,128)}, u32[]{:S(2)}) copy-start(f32[4096,512]{1,0:T(8,128)} %own_ref.5) | copy-start | bytes 25165828
  12.2 101.6 %collective-permute-start.1 = (f32[1024,512]{1,0:T(8,128)}, f32[1024,512]{1,0:T(8,128)S(1)}, u32[]{:S(2)}, u32[]{:S(2)}) collective-permute-start(f32[1024,512]{1,0:T(8,128)} %get-tuple-element.14), channel_id=1, source_target_pairs={{0,1},{1,0},{2,3},{3,2},{4,5},{5,4},{6,7},{7,6},{8,9},{9,8},{10,11... | collective-permute-start | bytes 6291464 | tf_op jit(solution)/shard_map/ppermute | solution.py:343
  15.1 90.9 %collective-permute-start = (f32[1024,512]{1,0:T(8,128)}, f32[1024,512]{1,0:T(8,128)}, u32[]{:S(2)}, u32[]{:S(2)}) collective-permute-start(f32[1024,512]{1,0:T(8,128)} %get-tuple-element.15), channel_id=1, source_target_pairs={{0,1},{1,0},{2,3},{3,2},{4,5},{5,4},{6,7},{7,6},{8,9},{9,8},{10,11... | collective-permute-start | bytes 6291464 | tf_op jit(solution)/shard_map/ppermute | solution.py:343
  26.2 2.0 collective-permute-start.3
  29.5 228.2 %all-reduce.2.cloned.1.call-start = ((), (), s32[]{:S(2)}) async-start(), calls=%async_computation | async-start | bytes 2097152 | tf_op jit(solution)/shard_map/psum | solution.py:347
  29.6 8.7 %collective-permute-start.4 = (f32[128,512]{1,0:T(8,128)S(1)}, f32[128,512]{1,0:T(8,128)S(1)}, u32[]{:S(2)}, u32[]{:S(2)}) collective-permute-start(f32[128,512]{1,0:T(8,128)S(1)} %slice_select_fusion.3), channel_id=1, source_target_pairs={{0,8},{2,10},{4,12},{6,14},{8,0},{10,2},{12,4},{14,6},{16,24},{18,... | collective-permute-start | bytes 786440 | tf_op jit(solution)/shard_map/ppermute | solution.py:308
  38.4 78.6 %collective-permute-start.5 = (f32[64,512]{1,0:T(8,128)S(1)}, f32[64,512]{1,0:T(8,128)S(1)}, u32[]{:S(2)}, u32[]{:S(2)}) collective-permute-start(f32[64,512]{1,0:T(8,128)S(1)} %slice_select_fusion.5), channel_id=1, source_target_pairs={{0,16},{2,18},{4,20},{6,22},{8,24},{10,26},{12,28},{14,30},{16,0},... | collective-permute-start | bytes 393224 | tf_op jit(solution)/shard_map/ppermute | solution.py:308
  106.1 3.4 %copy-start.1 = (f32[4096,512]{1,0:T(8,128)S(1)}, f32[4096,512]{1,0:T(8,128)}, u32[]{:S(2)}) copy-start(f32[4096,512]{1,0:T(8,128)} %own_ref.5) | copy-start | bytes 25165828
  113.8 3.0 copy-start.2
  116.9 7.5 %collective-permute-start.12 = (f32[256,512]{1,0:T(8,128)S(1)}, f32[256,512]{1,0:T(8,128)S(1)}, u32[]{:S(2)}, u32[]{:S(2)}) collective-permute-start(f32[256,512]{1,0:T(8,128)S(1)} %slice_select_fusion), channel_id=1, source_target_pairs={{0,2},{2,0},{4,6},{6,4},{8,10},{10,8},{12,14},{14,12},{16,18},{18,... | collective-permute-start | bytes 1572872 | tf_op jit(solution)/shard_map/ppermute | solution.py:308
  117.0 4.5 %collective-permute-start.6 = (f32[32,512]{1,0:T(8,128)S(1)}, f32[32,512]{1,0:T(8,128)S(1)}, u32[]{:S(2)}, u32[]{:S(2)}) collective-permute-start(f32[32,512]{1,0:T(8,128)S(1)} %slice_select_fusion.7), channel_id=1, source_target_pairs={{0,4},{2,6},{4,0},{6,2},{8,12},{10,14},{12,8},{14,10},{16,20},{18,... | collective-permute-start | bytes 196616 | tf_op jit(solution)/shard_map/ppermute | solution.py:308
  121.6 11.4 %collective-permute-start.7 = (f32[32,512]{1,0:T(8,128)S(1)}, f32[32,512]{1,0:T(8,128)S(1)}, u32[]{:S(2)}, u32[]{:S(2)}) collective-permute-start(f32[32,512]{1,0:T(8,128)S(1)} %select_add_fusion.7), channel_id=1, source_target_pairs={{0,5},{1,4},{2,7},{3,6},{4,1},{5,0},{6,3},{7,2},{8,13},{9,12},{10,... | collective-permute-start | bytes 196616 | tf_op jit(solution)/shard_map/ppermute | solution.py:313
  124.5 9.1 %collective-permute-start.13 = (f32[128,512]{1,0:T(8,128)S(1)}, f32[128,512]{1,0:T(8,128)S(1)}, u32[]{:S(2)}, u32[]{:S(2)}) collective-permute-start(f32[128,512]{1,0:T(8,128)S(1)} %slice_select_fusion.2), channel_id=1, source_target_pairs={{0,8},{2,10},{4,12},{6,14},{8,0},{10,2},{12,4},{14,6},{16,24},{18,... | collective-permute-start | bytes 786440 | tf_op jit(solution)/shard_map/ppermute | solution.py:308
  128.6 159.1 %collective-permute-start.2 = (f32[2048,512]{1,0:T(8,128)}, f32[2048,512]{1,0:T(8,128)}, u32[]{:S(2)}, u32[]{:S(2)}) collective-permute-start(f32[2048,512]{1,0:T(8,128)} %slice.51), channel_id=1, source_target_pairs={{0,1},{2,3},{4,5},{6,7},{8,9},{10,11},{12,13},{14,15},{16,17},{18,... | collective-permute-start | bytes 12582920 | tf_op jit(solution)/shard_map/ppermute | solution.py:344
  133.0 4.3 %collective-permute-start.8 = (f32[32,512]{1,0:T(8,128)S(1)}, f32[32,512]{1,0:T(8,128)S(1)}, u32[]{:S(2)}, u32[]{:S(2)}) collective-permute-start(f32[32,512]{1,0:T(8,128)S(1)} %broadcast_select_fusion.16), channel_id=1, source_target_pairs={{0,4},{2,6},{4,0},{6,2},{8,12},{10,14},{12,8},{14,10},{16,20},{18,... | collective-permute-start | bytes 196616 | tf_op jit(solution)/shard_map/ppermute | solution.py:308
  133.7 7.6 %collective-permute-start.14 = (f32[64,512]{1,0:T(8,128)S(1)}, f32[64,512]{1,0:T(8,128)S(1)}, u32[]{:S(2)}, u32[]{:S(2)}) collective-permute-start(f32[64,512]{1,0:T(8,128)S(1)} %slice_select_fusion.4), channel_id=1, source_target_pairs={{0,16},{2,18},{4,20},{6,22},{8,24},{10,26},{12,28},{14,30},{16,0},... | collective-permute-start | bytes 393224 | tf_op jit(solution)/shard_map/ppermute | solution.py:308
  141.4 5.2 %collective-permute-start.15 = (f32[32,512]{1,0:T(8,128)S(1)}, f32[32,512]{1,0:T(8,128)S(1)}, u32[]{:S(2)}, u32[]{:S(2)}) collective-permute-start(f32[32,512]{1,0:T(8,128)S(1)} %slice_select_fusion.6), channel_id=1, source_target_pairs={{0,5},{1,4},{2,7},{3,6},{4,1},{5,0},{6,3},{7,2},{8,13},{9,12},{10,... | collective-permute-start | bytes 196616 | tf_op jit(solution)/shard_map/ppermute | solution.py:313
  141.5 7.8 %collective-permute-start.9 = (f32[64,512]{1,0:T(8,128)S(1)}, f32[64,512]{1,0:T(8,128)S(1)}, u32[]{:S(2)}, u32[]{:S(2)}) collective-permute-start(f32[64,512]{1,0:T(8,128)S(1)} %pad_maximum_fusion.7), channel_id=1, source_target_pairs={{0,16},{2,18},{4,20},{6,22},{8,24},{10,26},{12,28},{14,30},{16,0},... | collective-permute-start | bytes 393224 | tf_op jit(solution)/shard_map/ppermute | solution.py:308
  146.6 4.4 %collective-permute-start.16 = (f32[32,512]{1,0:T(8,128)S(1)}, f32[32,512]{1,0:T(8,128)S(1)}, u32[]{:S(2)}, u32[]{:S(2)}) collective-permute-start(f32[32,512]{1,0:T(8,128)S(1)} %select_add_fusion.6), channel_id=1, source_target_pairs={{0,4},{2,6},{4,0},{6,2},{8,12},{10,14},{12,8},{14,10},{16,20},{18,... | collective-permute-start | bytes 196616 | tf_op jit(solution)/shard_map/ppermute | solution.py:308
  151.0 5.2 %collective-permute-start.17 = (f32[32,512]{1,0:T(8,128)S(1)}, f32[32,512]{1,0:T(8,128)S(1)}, u32[]{:S(2)}, u32[]{:S(2)}) collective-permute-start(f32[32,512]{1,0:T(8,128)S(1)} %add.51), channel_id=1, source_target_pairs={{0,5},{1,4},{2,7},{3,6},{4,1},{5,0},{6,3},{7,2},{8,13},{9,12},{10,... | collective-permute-start | bytes 196616 | tf_op jit(solution)/shard_map/ppermute | solution.py:313
  151.6 7.8 %collective-permute-start.10 = (f32[128,512]{1,0:T(8,128)S(1)}, f32[128,512]{1,0:T(8,128)S(1)}, u32[]{:S(2)}, u32[]{:S(2)}) collective-permute-start(f32[128,512]{1,0:T(8,128)S(1)} %pad_maximum_fusion.5), channel_id=1, source_target_pairs={{0,8},{2,10},{4,12},{6,14},{8,0},{10,2},{12,4},{14,6},{16,24},{18,... | collective-permute-start | bytes 786440 | tf_op jit(solution)/shard_map/ppermute | solution.py:308
  156.3 7.0 %collective-permute-start.18 = (f32[64,512]{1,0:T(8,128)S(1)}, f32[64,512]{1,0:T(8,128)S(1)}, u32[]{:S(2)}, u32[]{:S(2)}) collective-permute-start(f32[64,512]{1,0:T(8,128)S(1)} %pad_maximum_fusion.8), channel_id=1, source_target_pairs={{0,16},{2,18},{4,20},{6,22},{8,24},{10,26},{12,28},{14,30},{16,0},... | collective-permute-start | bytes 393224 | tf_op jit(solution)/shard_map/ppermute | solution.py:308
  163.4 6.4 %collective-permute-start.19 = (f32[128,512]{1,0:T(8,128)S(1)}, f32[128,512]{1,0:T(8,128)S(1)}, u32[]{:S(2)}, u32[]{:S(2)}) collective-permute-start(f32[128,512]{1,0:T(8,128)S(1)} %pad_maximum_fusion.6), channel_id=1, source_target_pairs={{0,8},{2,10},{4,12},{6,14},{8,0},{10,2},{12,4},{14,6},{16,24},{18,... | collective-permute-start | bytes 786440 | tf_op jit(solution)/shard_map/ppermute | solution.py:308
  164.7 5.3 %collective-permute-start.11 = (f32[256,512]{1,0:T(8,128)S(1)}, f32[256,512]{1,0:T(8,128)S(1)}, u32[]{:S(2)}, u32[]{:S(2)}) collective-permute-start(f32[256,512]{1,0:T(8,128)S(1)} %pad_maximum_fusion.3), channel_id=1, source_target_pairs={{0,2},{2,0},{4,6},{6,4},{8,10},{10,8},{12,14},{14,12},{16,18},{18,... | collective-permute-start | bytes 1572872 | tf_op jit(solution)/shard_map/ppermute | solution.py:308
  169.9 19.9 %collective-permute-start.20 = (f32[256,512]{1,0:T(8,128)S(1)}, f32[256,512]{1,0:T(8,128)S(1)}, u32[]{:S(2)}, u32[]{:S(2)}) collective-permute-start(f32[256,512]{1,0:T(8,128)S(1)} %pad_maximum_fusion.4), channel_id=1, source_target_pairs={{0,2},{2,0},{4,6},{6,4},{8,10},{10,8},{12,14},{14,12},{16,18},{18,... | collective-permute-start | bytes 1572872 | tf_op jit(solution)/shard_map/ppermute | solution.py:308
  257.7 1.2 copy-start.3
Sparse Core Ops, SparseCore 0:
  164.9 92.8 all-reduce.1

commit v2 on v1

v2 whole, which is shorter than its diff:
```python
import functools
import math

import jax
import jax.numpy as jnp
from jax import lax
from jax.experimental import pallas as pl
from jax.experimental.pallas import tpu as pltpu
from jax.sharding import PartitionSpec as P

F32 = jnp.float32
BF16 = jnp.bfloat16
HIGHEST = lax.Precision.HIGHEST
VMEM = pltpu.VMEM
BLOCK = 128
GROUP = 8
TILE = 512
COST = pl.CostEstimate(flops=1, bytes_accessed=1, transcendentals=0)


def params(megabytes):
    return pltpu.CompilerParams(vmem_limit_bytes=megabytes * 1024 * 1024)


def whole(count):
    return [pl.BlockSpec(memory_space=VMEM)] * count


def dot(a, b, contract, precision=None):
    return lax.dot_general(
        a, b, ((contract[:1], contract[1:]), ((), ())), precision=precision, preferred_element_type=F32
    )


def split(x):
    high = x.astype(BF16)
    return high, (x - high.astype(F32)).astype(BF16)


def dot3(a, b, contract):
    ah, al = split(a)
    bh, bl = split(b)
    return dot(ah, bh, contract) + (dot(ah, bl, contract) + dot(al, bh, contract))


def block_pairs(blocks):
    return [(i, j) for i in range(blocks) for j in range(i, blocks)]


def own_gram_kernel(scale, spans, side_ref, s_ref, g_ref, *refs):
    copies, (high_acc, mixed_acc) = refs[:-2], refs[-2:]
    step = pl.program_id(0)
    half = high_acc.shape[0] // 2

    @pl.when(step == 0)
    def _():
        high_acc[...] = jnp.zeros_like(high_acc)
        mixed_acc[...] = jnp.zeros_like(mixed_acc)

    block = s_ref[...]
    for copy, (start, shift, count) in zip(copies, spans):
        begin = start + shift * side_ref[0]

        @pl.when((step >= begin) & (step < begin + count))
        def _():
            copy[...] = block

    high, low = split(block)
    high_acc[:half] += dot(high[:, :half], high, (0, 0)) + dot(low[:, :half], low, (0, 0))
    high_acc[half:, half:] += dot(high[:, half:], high[:, half:], (0, 0)) + dot(low[:, half:], low[:, half:], (0, 0))
    mixed_acc[...] += dot(high, low, (0, 0))

    @pl.when(step == pl.num_programs(0) - 1)
    def _():
        for k, (i, j) in enumerate(block_pairs(high_acc.shape[0] // BLOCK)):
            rows, columns = pl.ds(i * BLOCK, BLOCK), pl.ds(j * BLOCK, BLOCK)
            mixed = mixed_acc[rows, columns] + mixed_acc[columns, rows].T
            g_ref[pl.ds(k * BLOCK, BLOCK), :] = (high_acc[rows, columns] + mixed) * scale


def own_gram(side, s, scale, spans):
    rows, width = s.shape
    square = (width, width)
    packed = (len(block_pairs(width // BLOCK)) * BLOCK, BLOCK)

    def copy_spec(start, shift, count):
        return pl.BlockSpec((TILE, width), lambda i, side: (jnp.clip(i - start - shift * side[0], 0, count - 1), 0))

    return pl.pallas_call(
        functools.partial(own_gram_kernel, scale, spans),
        grid_spec=pltpu.PrefetchScalarGridSpec(
            num_scalar_prefetch=1,
            grid=(rows // TILE,),
            in_specs=[pl.BlockSpec((TILE, width), lambda i, side: (i, 0))],
            out_specs=[pl.BlockSpec(packed, lambda i, side: (0, 0))] + [copy_spec(*span) for span in spans],
            scratch_shapes=[pltpu.VMEM(square, F32), pltpu.VMEM(square, F32)],
        ),
        out_shape=[jax.ShapeDtypeStruct(packed, F32)]
        + [jax.ShapeDtypeStruct((count * TILE, width), F32) for _, _, count in spans],
        compiler_params=params(60),
        cost_estimate=COST,
        name="own_gram",
    )(side, s)


def cross_gram_kernel(scale, resume, counts, side_ref, own_ref, *refs):
    chunks, before_ref, g_ref = refs[: len(counts)], refs[len(counts)], refs[-1]
    step = pl.program_id(0)
    first = side_ref[0] == 0

    @pl.when(step == 0)
    def _():
        g_ref[...] = before_ref[...] if resume else jnp.zeros_like(g_ref)

    begin = 0
    for chunk, count in zip(chunks, counts):

        @pl.when((step >= begin) & (step < begin + count))
        def _():
            own, other = own_ref[...], chunk[...]
            left = jnp.where(first, own, other)
            right = jnp.where(first, other, own)
            lh, ll = split(left)
            rh, rl = split(right * scale)
            g_ref[...] += (dot(lh, rh, (0, 0)) + dot(ll, rl, (0, 0))) + (dot(lh, rl, (0, 0)) + dot(ll, rh, (0, 0)))

        begin += count


def cross_gram(side, own, chunks, before, after, offset, scale):
    rows, width = own.shape
    counts = tuple(c.shape[0] // TILE for c in chunks)
    starts = [sum(counts[:i]) for i in range(len(counts))]
    square = (width, width)
    half = rows // 2 // TILE
    start = offset // TILE

    def chunk_spec(begin, count):
        return pl.BlockSpec((TILE, width), lambda i, side: (jnp.clip(i - begin, 0, count - 1), 0))

    in_specs = [pl.BlockSpec((TILE, width), lambda i, side: (i + start + (1 - side[0]) * half, 0))]
    in_specs += [chunk_spec(b, c) for b, c in zip(starts, counts)]
    in_specs += [pl.BlockSpec(square, lambda i, side: (0, 0))] * (before is not None)
    in_specs += [pl.BlockSpec(memory_space=pl.ANY)] * len(after)
    return pl.pallas_call(
        functools.partial(cross_gram_kernel, scale, before is not None, counts),
        grid_spec=pltpu.PrefetchScalarGridSpec(
            num_scalar_prefetch=1,
            grid=(sum(counts),),
            in_specs=in_specs,
            out_specs=pl.BlockSpec(square, lambda i, side: (0, 0)),
        ),
        out_shape=jax.ShapeDtypeStruct(square, F32),
        compiler_params=params(60),
        cost_estimate=COST,
        name="cross_gram",
    )(side, own, *chunks, *([] if before is None else [before]), *after)


def factor_block(a, x):
    count, width = len(a), a[0].shape[1]
    shape = (GROUP, width)
    row = lax.broadcasted_iota(jnp.int32, shape, 0)
    lane = lax.broadcasted_iota(jnp.int32, shape, 1)
    upper, inverse = [], []
    for p in range(count):
        c = GROUP * p
        pa = [jnp.broadcast_to(a[p][k : k + 1, :], shape) for k in range(GROUP)]
        px = [jnp.broadcast_to(x[p][k : k + 1, :], shape) for k in range(GROUP)]
        s = [
            [jnp.broadcast_to(pa[k][:, c + l : c + l + 1], shape) if l >= k else None for l in range(GROUP)]
            for k in range(GROUP)
        ]
        reciprocal = []
        for k in range(GROUP):
            reciprocal.append(1.0 / s[k][k])
            for l in range(k + 1, GROUP):
                m = s[k][l] * reciprocal[k]
                for t in range(l, GROUP):
                    s[l][t] = s[l][t] - m * s[k][t]
                pa[l] = pa[l] - m * pa[k]
                px[l] = px[l] - m * px[k]
        for r in range(p + 1, count):
            columns = [jnp.broadcast_to(a[r][:, c + l : c + l + 1], shape) for l in range(GROUP)]
            for k in range(GROUP):
                m = columns[k] * reciprocal[k]
                for t in range(k + 1, GROUP):
                    columns[t] = columns[t] - m * s[k][t]
                a[r] = a[r] - m * pa[k]
                x[r] = x[r] - m * px[k]
        ua, ux = None, None
        for k in range(GROUP):
            root = lax.rsqrt(s[k][k])
            va, vx = pa[k] * root, px[k] * root
            ua = va if k == 0 else jnp.where(row == k, va, ua)
            ux = vx if k == 0 else jnp.where(row == k, vx, ux)
        upper.append(jnp.where(lane >= row + c, ua, 0.0))
        inverse.append(ux)
    return upper, inverse


def factor_whole(a_ref, r_ref, x_ref, e_ref):
    order = a_ref.shape[0]
    blocks = order // BLOCK
    groups = BLOCK // GROUP
    r_ref[...] = jnp.zeros_like(r_ref)
    x_ref[...] = jnp.zeros_like(x_ref)
    row = lax.broadcasted_iota(jnp.int32, (GROUP, BLOCK), 0)
    lane = lax.broadcasted_iota(jnp.int32, (GROUP, BLOCK), 1)

    def body(b, carry):
        start = pl.multiple_of(b * BLOCK, BLOCK)
        here = pl.ds(start, BLOCK)
        a = [a_ref[pl.ds(start + GROUP * i, GROUP), here] for i in range(groups)]
        x = [jnp.where(lane == row + GROUP * i, 1.0, 0.0) for i in range(groups)]
        upper, inverse = factor_block(a, x)
        for i in range(groups):
            r_ref[pl.ds(start + GROUP * i, GROUP), here] = upper[i]
            e_ref[pl.ds(GROUP * i, GROUP), :] = inverse[i]
        for k in range(blocks):

            @pl.when(b == k)
            def _():
                lo, hi = k * BLOCK, (k + 1) * BLOCK
                e = e_ref[...]
                x_ref[lo:hi, lo:hi] = e
                if k > 0:
                    x_ref[lo:hi, :lo] = dot(e, x_ref[lo:hi, :lo], (1, 0), HIGHEST)
                if hi < order:
                    strip = dot(e, a_ref[lo:hi, hi:], (1, 0), HIGHEST)
                    r_ref[lo:hi, hi:] = strip
                    a_ref[hi:, hi:] -= dot(strip, strip, (0, 0), HIGHEST)
                    x_ref[hi:, :hi] -= dot(strip, x_ref[lo:hi, :hi], (0, 0), HIGHEST)

        return carry

    lax.fori_loop(0, blocks, body, 0)


def unpack(packed_ref, a_ref):
    for k, (i, j) in enumerate(block_pairs(a_ref.shape[0] // BLOCK)):
        a_ref[pl.ds(i * BLOCK, BLOCK), pl.ds(j * BLOCK, BLOCK)] = packed_ref[pl.ds(k * BLOCK, BLOCK), :]


def first_factor_kernel(g_ref, r_ref, x_ref, a_ref, e_ref):
    unpack(g_ref, a_ref)
    factor_whole(a_ref, r_ref, x_ref, e_ref)


def first_factor(packed, order):
    square = jax.ShapeDtypeStruct((order, order), F32)
    return pl.pallas_call(
        first_factor_kernel,
        out_shape=[square, square],
        in_specs=whole(1),
        out_specs=whole(2),
        scratch_shapes=[pltpu.VMEM((order, order), F32), pltpu.VMEM((BLOCK, BLOCK), F32)],
        compiler_params=params(40),
        cost_estimate=COST,
        name="first_factor",
    )(packed)


def second_factor_kernel(side_ref, cross_ref, g_ref, r00_ref, x0_ref, f_ref, *refs):
    own_high, own_low, other_high, other_low, a_ref, r_ref, x_ref, e_ref = refs
    order = a_ref.shape[0]
    first = side_ref[0] == 0
    x0 = x0_ref[...]
    r01 = dot(x0, cross_ref[...], (1, 0), HIGHEST)
    unpack(g_ref, a_ref)
    a_ref[...] -= dot(r01, r01, (0, 0), HIGHEST)
    u = dot3(x0, r01, (0, 0))
    f_ref[:order] = jnp.where(first, r00_ref[...], r01)
    factor_whole(a_ref, r_ref, x_ref, e_ref)
    f_ref[order:] = jnp.where(first, 0.0, r_ref[...])
    x1 = x_ref[...]
    own_high[...], own_low[...] = split(jnp.where(first, x0, x1).T)
    other_high[...], other_low[...] = split(jnp.where(first, 0.0, -dot3(u, x1, (1, 1))))


def second_factor(side, cross, packed, r00, x0):
    order = cross.shape[0]
    square = (order, order)
    return pl.pallas_call(
        second_factor_kernel,
        out_shape=[jax.ShapeDtypeStruct((2 * order, order), F32)] + [jax.ShapeDtypeStruct(square, BF16)] * 4,
        in_specs=[pl.BlockSpec(memory_space=pltpu.SMEM)] + whole(4),
        out_specs=whole(5),
        scratch_shapes=[pltpu.VMEM(square, F32)] * 3 + [pltpu.VMEM((BLOCK, BLOCK), F32)],
        compiler_params=params(40),
        cost_estimate=COST,
        name="second_factor",
    )(side, cross, packed, r00, x0)


def basis_kernel(counts, own_ref, *refs):
    chunks = refs[: len(counts)]
    own_high, own_low, other_high, other_low = refs[len(counts) : len(counts) + 4]
    out_ref = refs[-1]
    step = pl.program_id(0)

    def product(x, high, low):
        xh, xl = split(x)
        return dot(xh, high[...], (1, 0)) + (dot(xh, low[...], (1, 0)) + dot(xl, high[...], (1, 0)))

    begin = 0
    for chunk, count in zip(chunks, counts):

        @pl.when((step >= begin) & (step < begin + count))
        def _():
            out_ref[...] = product(own_ref[...], own_high, own_low) + product(chunk[...], other_high, other_low)

        begin += count


def whitened(own, chunks, factors, row, before):
    rows, width = own.shape
    counts = tuple(c.shape[0] // TILE for c in chunks)
    starts = [sum(counts[:i]) for i in range(len(counts))]
    offset = row // TILE

    def chunk_spec(begin, count):
        return pl.BlockSpec((TILE, width), lambda i: (jnp.clip(i - begin, 0, count - 1), 0))

    in_specs = [pl.BlockSpec((TILE, width), lambda i: (i + offset, 0))]
    in_specs += [chunk_spec(b, c) for b, c in zip(starts, counts)]
    in_specs += [pl.BlockSpec((width, width), lambda i: (0, 0))] * 4
    operands = [own, *chunks, *factors]
    aliases = {}
    if before is not None:
        aliases = {len(operands): 0}
        in_specs.append(pl.BlockSpec(memory_space=pl.ANY))
        operands.append(before)
    return pl.pallas_call(
        functools.partial(basis_kernel, counts),
        grid=(sum(counts),),
        in_specs=in_specs,
        out_specs=pl.BlockSpec((TILE, width), lambda i: (i + offset, 0)),
        out_shape=jax.ShapeDtypeStruct((rows, width), F32),
        input_output_aliases=aliases,
        compiler_params=params(60),
        cost_estimate=COST,
        name="whitened",
    )(*operands)


def flip(x, order, step):
    count = lax.axis_size("dof")
    return lax.ppermute(x, "dof", [(i, i ^ order[i % 2][step]) for i in range(count)])


def flip_side(x, order):
    count = lax.axis_size("dof")
    pairs = [(2 * i + j, 2 * (i ^ order[i % 2][-1]) + 1 - j) for i in range(count) for j in range(2)]
    return lax.ppermute(x, ("dof", "snap"), pairs)


def halve(x, upper, send):
    half = x.shape[0] // 2
    low, high = x[:half], x[half:]
    return jnp.where(upper, high, low) + send(jnp.where(upper, low, high))


def double_with(x, other, upper, axis=0):
    return jnp.concatenate([jnp.where(upper, other, x), jnp.where(upper, x, other)], axis)


def double(x, upper, send, axis=0):
    return double_with(x, send(x), upper, axis)


def on_device(snapshots):
    rows, width = snapshots.shape
    count = lax.axis_size("dof")
    scale = 1.0 / (rows * count)
    me, side = lax.axis_index("dof"), lax.axis_index("snap")
    side_operand = jnp.full((1,), side, jnp.int32)
    bits = [1 << i for i in range(1, count.bit_length() - 1)]
    order = ([1] + bits[1:] + bits[:1], [1] + bits)
    steps = list(range(len(order[0])))

    def bit(step):
        return (me & jnp.where(me % 2 == 0, order[0][step], order[1][step])) != 0

    def send(step):
        return lambda x: flip(x, order, step)

    def send_side(x):
        return flip_side(x, order)

    def reduce_own(i, carry):
        shard = carry[0]
        for k in steps:
            shard = halve(shard, bit(k), send(k))
        received = send_side(shard)
        upper = bit(steps[-1]) ^ (side == 1)
        first = jnp.where(side == 0, shard, received)
        second = jnp.where(side == 0, received, shard)
        first = double(first, upper, send(steps[-1]))
        second = double(second, ~upper, send(steps[-1]))
        for k in steps[-2::-1]:
            first = double(first, bit(k), send(k))
            second = double(second, bit(k), send(k))
        return first, second

    def reduce_cross(i, cross):
        for k in steps[:-1]:
            cross = halve(cross, bit(k), send(k))
        cross = halve(cross, side == 1, send_side)
        cross = cross + send(steps[-1])(cross)
        cross = double(cross, side == 1, send_side)
        for k in steps[-2::-1]:
            cross = double(cross, bit(k), send(k))
        return cross

    half = rows // 2 // TILE
    parts = [half // 4, half // 2, half - half // 4 - half // 2]
    rests = [3 * half // 4, half - 3 * half // 4]
    spans = [(parts[0], half, parts[1]), (parts[0] + parts[1], half, parts[2])]
    spans += [(half, 0, rests[0]), (half + rests[0], 0, rests[1])]

    def swap(x):
        return lax.ppermute(x, "snap", [(0, 1), (1, 0)])

    def one_way(x):
        return lax.ppermute(x, "snap", [(0, 1)])

    def late(x, after):
        return lax.optimization_barrier((x, after))[0]

    once = 1 + jnp.minimum(side, 0)
    arrived = [swap(lax.dynamic_slice_in_dim(snapshots, side * half * TILE, parts[0] * TILE, 0))]
    own, send1, send2, send3, send4 = own_gram(side_operand, snapshots, scale, spans)
    arrived.append(swap(send1))
    first, second = lax.fori_loop(0, once, reduce_own, (own, own))
    arrived.append(swap(late(send2, first)))
    r00, x00 = first_factor(first, width)
    arrived.append(one_way(late(send3, r00)))
    early = parts[0] + parts[1]
    cross = cross_gram(side_operand, snapshots, arrived[:2], None, [x00, second], 0, scale)
    arrived.append(one_way(late(send4, cross)))
    cross = cross_gram(side_operand, snapshots, arrived[2:3], cross, [], early * TILE, scale)
    cross = lax.fori_loop(0, once, reduce_cross, cross)
    factor, *factors = second_factor(side_operand, cross, second, r00, x00)
    basis = whitened(snapshots, arrived[:-1], factors, 0, None)
    basis = whitened(snapshots, arrived[-1:], factors, (half + rests[0]) * TILE, basis)
    return (basis, factor)


def solution(mesh):
    in_specs = (P("dof", "snap"),)
    out_specs = (P("dof", "snap"), P(None, "snap"))
    return jax.shard_map(
        on_device, mesh=mesh, in_specs=in_specs, out_specs=out_specs, check_vma=False
    )
```

time: 314 us -> 203 us (0.65)
  waiting for transfers between devices: 169 us -> 47.9 us
  starting transfers between devices: 29.5 us -> 49.1 us
  between operations: 14.4 us -> 0.7 us
  Pallas kernels: 82.2 us -> 93.6 us
  local copies, waits for them, and re-layouts: 12.2 us -> 7.35 us
    psum x1 -> x0, waiting for transfers between devices: 67.8 us -> none  [on_device(): second = lax.psum(own, 'dof')]
    ppermute x21 -> x27, waiting for transfers between devices: 102 us -> 47.9 us  [the longest x19 41.1 us: flip(): lax.ppermute(x, 'dof', [(i, i ^ order[i % 2][step]) for i in range(count)])]
    ppermute x21 -> x27, starting transfers between devices: 29.5 us -> 49.1 us  [the longest x19 28.5 us: flip(): lax.ppermute(x, 'dof', [(i, i ^ order[i % 2][step]) for i in range(count)])]
    pallas_call x5 -> x6, Pallas kernels: 62.6 us -> 73.9 us  [the longest x1 27.9 us: second_factor(): pl.pallas_call(second_factor_kernel, out_shape=[jax.ShapeDtypeStruct((2 *...]
  transfers between devices with their start and end apart: 22 -> 27, of which waited for: 14 -> 20; matrix products, arithmetic and copies ran while one was open for 3% -> 2% of each run, Pallas kernels for 20% -> 44%
where the time goes in v2:
time: 203 us; the launch traced here: 202 us
  Pallas kernels  93.6 us (46%)
  starting transfers between devices  49.1 us (24%)
  waiting for transfers between devices  47.9 us (24%)
  local copies, waits for them, and re-layouts  7.35 us (4%)
  other arithmetic  2.91 us (1%)
    ppermute x19, waiting for transfers between devices, flip(): lax.ppermute(x, 'dof', [(i, i ^ order[i % 2][step]) for i in range(count)])  41.1 us
    ppermute x19, starting transfers between devices, flip(): lax.ppermute(x, 'dof', [(i, i ^ order[i % 2][step]) for i in range(count)])  28.5 us
    pallas_call x1, Pallas kernels, second_factor(): pl.pallas_call(second_factor_kernel, out_shape=[jax.ShapeDtypeStruct((2 *...  27.9 us
    pallas_call x2, Pallas kernels, whitened(): pl.pallas_call(functools.partial(basis_kernel, counts), grid=(sum(counts)...  22 us
    pallas_call x1, Pallas kernels, first_factor(): pl.pallas_call(first_factor_kernel, out_shape=[square, square], in_specs=...  19.6 us
    pallas_call x1, Pallas kernels, own_gram(): pl.pallas_call(functools.partial(own_gram_kernel, scale, spans), grid_spe...  13.4 us
    pallas_call x2, Pallas kernels, cross_gram(): pl.pallas_call(functools.partial(cross_gram_kernel, scale, before is not...  10.7 us
    ppermute x3, starting transfers between devices, flip_side(): return lax.ppermute(x, ('dof', 'snap'), pairs)  9.76 us
  transfers between devices with their start and end apart: 27, of which 20 were waited for; matrix products, arithmetic and copies ran while one was open for 2% of the time, Pallas kernels for 44%

profile of v2, /device:TPU:0, one launch (start us, length us, event | category | flops | bytes accessed | tf_op | source)
XLA Modules:
  0.0 201.8 jit_solution(9582368576038954728)
XLA Ops:
  0.6 2.3 %constant_dynamic-slice_fusion = f32[512,512]{1,0:T(8,128)} fusion(f32[4096,512]{1,0:T(8,128)} %own_ref.7, s32[]{:T(128)S(6)} %select_n.396), kind=kLoop, calls=%fused_computation.54 | loop fusion | bytes 2097156 | tf_op jit(solution)/shard_map/dynamic_slice | solution.py:432
  2.9 3.0 %collective-permute-start.22 = (f32[512,512]{1,0:T(8,128)}, f32[512,512]{1,0:T(8,128)}, u32[]{:S(2)}, u32[]{:S(2)}) collective-permute-start(f32[512,512]{1,0:T(8,128)} %constant_dynamic-slice_fusion), channel_id=1, source_target_pairs={{0,1},{1,0},{2,3},{3,2},{4,5},{5,4},{6,7},{7,6},{8,9},{9,8},{10,11... | collective-permute-start | bytes 3145736 | tf_op jit(solution)/shard_map/ppermute | solution.py:423
  5.9 13.4 %own_gram.1 = (f32[1280,128]{1,0:T(8,128)S(1)}, f32[1024,512]{1,0:T(8,128)}, f32[512,512]{1,0:T(8,128)}, f32[1536,512]{1,0:T(8,128)}, f32[512,512]{1,0:T(8,128)}) custom-call(s32[1]{0:T(128)} %bitcast.side_ref, f32[4096,512]{1,0:T(8,128)} %own_ref.7), custom_call_target="tpu_custom_call" | custom-call | flops 1 | bytes 1 | tf_op jit(solution)/shard_map/own_gram/pallas_call | solution.py:89
  20.2 43.0 %while.26 = (s32[]{:T(128)}, f32[1280,128]{1,0:T(8,128)S(1)}, f32[1280,128]{1,0:T(8,128)}, s32[]{:T(128)}, pred[]{:T(512)}, /*index=5*/pred[]{:T(512)}, pred[]{:...) while((s32[]{:T(128)}, f32[1280,128]{1,0:T(8,128)S(1)}, ...), condition=%wide.region_1.2_spmd, body=%wide.region_0.1_spmd.sunk | while | flops 1996802 | bytes 21832332 | solution.py:435
  24.1 3.3 %collective-permute-done.1 = f32[320,128]{1,0:T(8,128)S(1)} collective-permute-done((f32[320,128]{1,0:T(8,128)S(1)}, f32[320,128]{1,0:T(8,128)S(1)}, u32[]{:S(2)}, u32[]{:S(2)}) %collective-permute-start.1) | collective-permute-done | bytes 163872 | tf_op jit(solution)/shard_map/while/body/ppermute | solution.py:349
  27.5 3.1 %collective-permute-start.2 = (f32[160,128]{1,0:T(8,128)S(1)}, f32[160,128]{1,0:T(8,128)S(1)}, u32[]{:S(2)}, u32[]{:S(2)}) collective-permute-start(f32[160,128]{1,0:T(8,128)S(1)} %slice_select_fusion.18), channel_id=1, source_target_pairs={{0,16},{2,10},{4,20},{6,14},{8,24},{10,2},{12,28},{14,6},{16,0},{1... | collective-permute-start | bytes 245768 | tf_op jit(solution)/shard_map/while/body/ppermute | solution.py:349
  30.6 2.4 %collective-permute-done.2 = f32[160,128]{1,0:T(8,128)S(1)} collective-permute-done((f32[160,128]{1,0:T(8,128)S(1)}, f32[160,128]{1,0:T(8,128)S(1)}, u32[]{:S(2)}, u32[]{:S(2)}) %collective-permute-start.2) | collective-permute-done | bytes 81952 | tf_op jit(solution)/shard_map/while/body/ppermute | solution.py:349
  37.1 2.8 %collective-permute-start.4 = (f32[80,128]{1,0:T(8,128)S(1)}, f32[80,128]{1,0:T(8,128)S(1)}, u32[]{:S(2)}, u32[]{:S(2)}) collective-permute-start(f32[80,128]{1,0:T(8,128)S(1)} %select_add_fusion.19), channel_id=1, source_target_pairs={{0,5},{1,4},{2,19},{3,18},{4,1},{5,0},{6,23},{7,22},{8,13},{9,12},... | collective-permute-start | bytes 122888 | tf_op jit(solution)/shard_map/while/body/ppermute | solution.py:355
  39.9 2.3 %collective-permute-done.4 = f32[80,128]{1,0:T(8,128)S(1)} collective-permute-done((f32[80,128]{1,0:T(8,128)S(1)}, f32[80,128]{1,0:T(8,128)S(1)}, u32[]{:S(2)}, u32[]{:S(2)}) %collective-permute-start.4) | collective-permute-done | bytes 40992 | tf_op jit(solution)/shard_map/while/body/ppermute | solution.py:355
  46.3 3.1 %collective-permute-start.6 = (f32[160,128]{1,0:T(8,128)S(1)}, f32[160,128]{1,0:T(8,128)S(1)}, u32[]{:S(2)}, u32[]{:S(2)}) collective-permute-start(f32[160,128]{1,0:T(8,128)S(1)} %pad_maximum_fusion.24), channel_id=1, source_target_pairs={{0,16},{2,10},{4,20},{6,14},{8,24},{10,2},{12,28},{14,6},{16,0},{1... | collective-permute-start | bytes 245768 | tf_op jit(solution)/shard_map/while/body/ppermute | solution.py:349
  51.8 2.3 %collective-permute-start.7 = (f32[320,128]{1,0:T(8,128)S(1)}, f32[320,128]{1,0:T(8,128)S(1)}, u32[]{:S(2)}, u32[]{:S(2)}) collective-permute-start(f32[320,128]{1,0:T(8,128)S(1)} %pad_maximum_fusion.25), channel_id=1, source_target_pairs={{0,8},{2,6},{4,12},{6,2},{8,0},{10,14},{12,4},{14,10},{16,24},{18,... | collective-permute-start | bytes 491528 | tf_op jit(solution)/shard_map/while/body/ppermute | solution.py:349
  54.8 2.3 %collective-permute-start.11 = (f32[320,128]{1,0:T(8,128)S(1)}, f32[320,128]{1,0:T(8,128)S(1)}, u32[]{:S(2)}, u32[]{:S(2)}) collective-permute-start(f32[320,128]{1,0:T(8,128)S(1)} %pad_maximum_fusion.29), channel_id=1, source_target_pairs={{0,8},{2,6},{4,12},{6,2},{8,0},{10,14},{12,4},{14,10},{16,24},{18,... | collective-permute-start | bytes 491528 | tf_op jit(solution)/shard_map/while/body/ppermute | solution.py:349
  57.6 2.9 %collective-permute-done.11 = f32[320,128]{1,0:T(8,128)S(1)} collective-permute-done((f32[320,128]{1,0:T(8,128)S(1)}, f32[320,128]{1,0:T(8,128)S(1)}, u32[]{:S(2)}, u32[]{:S(2)}) %collective-permute-start.11) | collective-permute-done | bytes 163872 | tf_op jit(solution)/shard_map/while/body/ppermute | solution.py:349
  64.6 19.6 %first_factor.1 = (f32[512,512]{1,0:T(8,128)S(1)}, f32[512,512]{1,0:T(8,128)S(1)}) custom-call(f32[1280,128]{1,0:T(8,128)S(1)} %get-tuple-element.227.g_ref), custom_call_target="tpu_custom_call" | custom-call | flops 1 | bytes 1 | tf_op jit(solution)/shard_map/first_factor/pallas_call | solution.py:252
  85.2 4.1 %collective-permute-start.26 = (f32[1536,512]{1,0:T(8,128)}, f32[1536,512]{1,0:T(8,128)}, u32[]{:S(2)}, u32[]{:S(2)}) collective-permute-start(f32[1536,512]{1,0:T(8,128)} %get-tuple-element.240), channel_id=1, source_target_pairs={{0,1},{2,3},{4,5},{6,7},{8,9},{10,11},{12,13},{14,15},{16,17},{18,... | collective-permute-start | bytes 9437192 | tf_op jit(solution)/shard_map/ppermute | solution.py:426
  89.3 7.4 %cross_gram.2.refs_1_ = f32[512,512]{1,0:T(8,128)} custom-call(s32[1]{0:T(128)} %bitcast.side_ref, f32[4096,512]{1,0:T(8,128)} %own_ref.7, f32[512,512]{1,0:T(8,128)} %collective-permute-done.22.refs_0_, f32[1024,512]{1,0:T(8,128)} %collective-permute-done.23.refs_1_, f32[512,512]{1,0:T(8,128)} %copy-done, f32[1280,128]{1,0:T(8,128)} %get-tuple-element.229.refs_3_.g_ref), custom_call_target="tpu_custom_call" | custom-call | flops 1 | bytes 1 | tf_op jit(solution)/shard_map/cross_gram/pallas_call | solution.py:145
  96.7 2.3 %collective-permute-start.24 = (f32[512,512]{1,0:T(8,128)}, f32[512,512]{1,0:T(8,128)}, u32[]{:S(2)}, u32[]{:S(2)}) collective-permute-start(f32[512,512]{1,0:T(8,128)} %get-tuple-element.230), channel_id=1, source_target_pairs={{0,1},{2,3},{4,5},{6,7},{8,9},{10,11},{12,13},{14,15},{16,17},{18,... | collective-permute-start | bytes 3145736 | tf_op jit(solution)/shard_map/ppermute | solution.py:426
  99.0 3.3 %cross_gram.3 = f32[512,512]{1,0:T(8,128)S(1)} custom-call(s32[1]{0:T(128)} %bitcast.side_ref, f32[4096,512]{1,0:T(8,128)} %own_ref.7, f32[512,512]{1,0:T(8,128)} %collective-permute-done.25.refs_0_.refs_2_, f32[512,512]{1,0:T(8,128)} %cross_gram.2.refs_1_), custom_call_target="tpu_custom_call" | custom-call | flops 1 | bytes 1 | tf_op jit(solution)/shard_map/cross_gram/pallas_call | solution.py:145
  102.3 46.4 %while.27 = (s32[]{:T(128)}, f32[512,512]{1,0:T(8,128)S(1)}, s32[]{:T(128)}, pred[]{:T(512)}, pred[]{:T(512)}, /*index=5*/pred[]{:T(512)}, pred[]{:T(512)}, s32[]{:T(128)}) while((s32[]{:T(128)}, f32[512,512]{1,0:T(8,128)S(1)}, s32[]{:T(128)}, pred[]{:T(512)}, pred[]{:T(512)}, /*index=5*/pred[]{:T(512)}, pred[]{:T(512)}, s32[]{:T(128)}) %tuple.97), condition=%wide.region_3.4_spmd, body=%wide.region_2.3_spmd.sunk | while | flops 1966082 | bytes 23069128 | solution.py:443
  106.6 4.4 %collective-permute-done.14 = f32[128,512]{1,0:T(8,128)S(1)} collective-permute-done((f32[128,512]{1,0:T(8,128)S(1)}, f32[128,512]{1,0:T(8,128)S(1)}, u32[]{:S(2)}, u32[]{:S(2)}) %collective-permute-start.14) | collective-permute-done | bytes 262176 | tf_op jit(solution)/shard_map/while/body/ppermute | solution.py:349
  111.1 3.1 %collective-permute-start.15 = (f32[64,512]{1,0:T(8,128)S(1)}, f32[64,512]{1,0:T(8,128)S(1)}, u32[]{:S(2)}, u32[]{:S(2)}) collective-permute-start(f32[64,512]{1,0:T(8,128)S(1)} %slice_select_fusion.22), channel_id=1, source_target_pairs={{0,16},{2,10},{4,20},{6,14},{8,24},{10,2},{12,28},{14,6},{16,0},{1... | collective-permute-start | bytes 393224 | tf_op jit(solution)/shard_map/while/body/ppermute | solution.py:349
  114.1 3.0 %collective-permute-done.15 = f32[64,512]{1,0:T(8,128)S(1)} collective-permute-done((f32[64,512]{1,0:T(8,128)S(1)}, f32[64,512]{1,0:T(8,128)S(1)}, u32[]{:S(2)}, u32[]{:S(2)}) %collective-permute-start.15) | collective-permute-done | bytes 131104 | tf_op jit(solution)/shard_map/while/body/ppermute | solution.py:349
  117.1 3.9 %collective-permute-start.16 = (f32[32,512]{1,0:T(8,128)S(1)}, f32[32,512]{1,0:T(8,128)S(1)}, u32[]{:S(2)}, u32[]{:S(2)}) collective-permute-start(f32[32,512]{1,0:T(8,128)S(1)} %slice_select_fusion.23), channel_id=1, source_target_pairs={{0,5},{1,4},{2,19},{3,18},{4,1},{5,0},{6,23},{7,22},{8,13},{9,12},... | collective-permute-start | bytes 196616 | tf_op jit(solution)/shard_map/while/body/ppermute | solution.py:355
  121.1 2.2 %collective-permute-done.16 = f32[32,512]{1,0:T(8,128)S(1)} collective-permute-done((f32[32,512]{1,0:T(8,128)S(1)}, f32[32,512]{1,0:T(8,128)S(1)}, u32[]{:S(2)}, u32[]{:S(2)}) %collective-permute-start.16) | collective-permute-done | bytes 65568 | tf_op jit(solution)/shard_map/while/body/ppermute | solution.py:355
  123.9 3.7 %collective-permute-done.17 = f32[32,512]{1,0:T(8,128)S(1)} collective-permute-done((f32[32,512]{1,0:T(8,128)S(1)}, f32[32,512]{1,0:T(8,128)S(1)}, u32[]{:S(2)}, u32[]{:S(2)}) %collective-permute-start.17) | collective-permute-done | bytes 65568 | tf_op jit(solution)/shard_map/while/body/ppermute | solution.py:349
  127.7 3.1 %collective-permute-start.18 = (f32[32,512]{1,0:T(8,128)S(1)}, f32[32,512]{1,0:T(8,128)S(1)}, u32[]{:S(2)}, u32[]{:S(2)}) collective-permute-start(f32[32,512]{1,0:T(8,128)S(1)} %add.117), channel_id=1, source_target_pairs={{0,5},{1,4},{2,19},{3,18},{4,1},{5,0},{6,23},{7,22},{8,13},{9,12},... | collective-permute-start | bytes 196616 | tf_op jit(solution)/shard_map/while/body/ppermute | solution.py:355
  130.8 2.2 %collective-permute-done.18 = f32[32,512]{1,0:T(8,128)S(1)} collective-permute-done((f32[32,512]{1,0:T(8,128)S(1)}, f32[32,512]{1,0:T(8,128)S(1)}, u32[]{:S(2)}, u32[]{:S(2)}) %collective-permute-start.18) | collective-permute-done | bytes 65568 | tf_op jit(solution)/shard_map/while/body/ppermute | solution.py:355
  135.1 3.9 %collective-permute-done.19 = f32[64,512]{1,0:T(8,128)S(1)} collective-permute-done((f32[64,512]{1,0:T(8,128)S(1)}, f32[64,512]{1,0:T(8,128)S(1)}, u32[]{:S(2)}, u32[]{:S(2)}) %collective-permute-start.19) | collective-permute-done | bytes 131104 | tf_op jit(solution)/shard_map/while/body/ppermute | solution.py:349
  141.0 4.4 %collective-permute-done.20 = f32[128,512]{1,0:T(8,128)S(1)} collective-permute-done((f32[128,512]{1,0:T(8,128)S(1)}, f32[128,512]{1,0:T(8,128)S(1)}, u32[]{:S(2)}, u32[]{:S(2)}) %collective-permute-start.20) | collective-permute-done | bytes 262176 | tf_op jit(solution)/shard_map/while/body/ppermute | solution.py:349
  148.7 27.9 %second_factor.1 = (f32[1024,512]{1,0:T(8,128)}, bf16[512,512]{1,0:T(8,128)(2,1)S(1)}, bf16[512,512]{1,0:T(8,128)(2,1)S(1)}, bf16[512,512]{1,0:T(8,128)(2,1)S(1)}, bf16[512,512]{1,0:T(8,128)(2,1)S(1)}) custom-call(s32[1]{0:T(128)} %bitcast.side_ref, f32[512,512]{1,0:T(8,128)S(1)} %get-tuple-element.233.cross_ref, ...), custom_call_target="tpu_custom_call" | custom-call | flops 1 | bytes 1 | tf_op jit(solution)/shard_map/second_factor/pallas_call | solution.py:284
  179.8 17.1 %whitened.2.refs_5_ = f32[4096,512]{1,0:T(8,128)} custom-call(f32[4096,512]{1,0:T(8,128)} %own_ref.7, f32[512,512]{1,0:T(8,128)} %collective-permute-done.22.refs_0_, f32[1024,512]{1,0:T(8,128)} %collective-permute-done.23.refs_1_, f32[512,512]{1,0:T(8,128)} %collective-permute-done.25.refs_0_.refs_2_, f32[1536,512]{1,0:T(8,128)} %collective-permute-done.26.refs_3_, ...), custom_call_target="tpu_custom_call" | custom-call | flops 1 | bytes 1 | tf_op jit(solution)/shard_map/whitened/pallas_call | solution.py:334
  196.9 4.9 %whitened.3 = f32[4096,512]{1,0:T(8,128)} custom-call(f32[4096,512]{1,0:T(8,128)} %own_ref.7, f32[512,512]{1,0:T(8,128)} %collective-permute-done.24.refs_0_, bf16[512,512]{1,0:T(8,128)(2,1)} %copy-done.2, bf16[512,512]{1,0:T(8,128)(2,1)} %copy-done.3, bf16[512,512]{1,0:T(8,128)(2,1)} %copy-done.4, ...), custom_call_target="tpu_custom_call", output_to_operand_aliasing={{}: (6, {})} | custom-call | flops 1 | bytes 1 | tf_op jit(solution)/shard_map/whitened/pallas_call | solution.py:334
  (87 shorter events, 37.3 us)
Async XLA Ops:
  2.9 86.4 %collective-permute-start.22 = (f32[512,512]{1,0:T(8,128)}, f32[512,512]{1,0:T(8,128)}, u32[]{:S(2)}, u32[]{:S(2)}) collective-permute-start(f32[512,512]{1,0:T(8,128)} %constant_dynamic-slice_fusion), channel_id=1, source_target_pairs={{0,1},{1,0},{2,3},{3,2},{4,5},{5,4},{6,7},{7,6},{8,9},{9,8},{10,11... | collective-permute-start | bytes 3145736 | tf_op jit(solution)/shard_map/ppermute | solution.py:423
  19.3 70.1 %collective-permute-start.23 = (f32[1024,512]{1,0:T(8,128)}, f32[1024,512]{1,0:T(8,128)}, u32[]{:S(2)}, u32[]{:S(2)}) collective-permute-start(f32[1024,512]{1,0:T(8,128)} %get-tuple-element.225), channel_id=1, source_target_pairs={{0,1},{1,0},{2,3},{3,2},{4,5},{5,4},{6,7},{7,6},{8,9},{9,8},{10,11... | collective-permute-start | bytes 6291464 | tf_op jit(solution)/shard_map/ppermute | solution.py:423
  20.2 1.7 collective-permute-start
  22.0 5.4 %collective-permute-start.1 = (f32[320,128]{1,0:T(8,128)S(1)}, f32[320,128]{1,0:T(8,128)S(1)}, u32[]{:S(2)}, u32[]{:S(2)}) collective-permute-start(f32[320,128]{1,0:T(8,128)S(1)} %slice_select_fusion.17), channel_id=1, source_target_pairs={{0,8},{2,6},{4,12},{6,2},{8,0},{10,14},{12,4},{14,10},{16,24},{18,... | collective-permute-start | bytes 491528 | tf_op jit(solution)/shard_map/while/body/ppermute | solution.py:349
  27.5 5.5 %collective-permute-start.2 = (f32[160,128]{1,0:T(8,128)S(1)}, f32[160,128]{1,0:T(8,128)S(1)}, u32[]{:S(2)}, u32[]{:S(2)}) collective-permute-start(f32[160,128]{1,0:T(8,128)S(1)} %slice_select_fusion.18), channel_id=1, source_target_pairs={{0,16},{2,10},{4,20},{6,14},{8,24},{10,2},{12,28},{14,6},{16,0},{1... | collective-permute-start | bytes 245768 | tf_op jit(solution)/shard_map/while/body/ppermute | solution.py:349
  33.0 4.1 %collective-permute-start.3 = (f32[80,128]{1,0:T(8,128)S(1)}, f32[80,128]{1,0:T(8,128)S(1)}, u32[]{:S(2)}, u32[]{:S(2)}) collective-permute-start(f32[80,128]{1,0:T(8,128)S(1)} %slice_select_fusion.19), channel_id=1, source_target_pairs={{0,4},{2,18},{4,0},{6,22},{8,12},{10,26},{12,8},{14,30},{16,20},{1... | collective-permute-start | bytes 122888 | tf_op jit(solution)/shard_map/while/body/ppermute | solution.py:349
  37.1 5.1 %collective-permute-start.4 = (f32[80,128]{1,0:T(8,128)S(1)}, f32[80,128]{1,0:T(8,128)S(1)}, u32[]{:S(2)}, u32[]{:S(2)}) collective-permute-start(f32[80,128]{1,0:T(8,128)S(1)} %select_add_fusion.19), channel_id=1, source_target_pairs={{0,5},{1,4},{2,19},{3,18},{4,1},{5,0},{6,23},{7,22},{8,13},{9,12},... | collective-permute-start | bytes 122888 | tf_op jit(solution)/shard_map/while/body/ppermute | solution.py:355
  42.2 4.1 %collective-permute-start.5 = (f32[80,128]{1,0:T(8,128)S(1)}, f32[80,128]{1,0:T(8,128)S(1)}, u32[]{:S(2)}, u32[]{:S(2)}) collective-permute-start(f32[80,128]{1,0:T(8,128)S(1)} %get-tuple-element.433), channel_id=1, source_target_pairs={{0,4},{2,18},{4,0},{6,22},{8,12},{10,26},{12,8},{14,30},{16,20},{1... | collective-permute-start | bytes 122888 | tf_op jit(solution)/shard_map/while/body/ppermute | solution.py:349
  44.1 5.3 %collective-permute-start.9 = (f32[80,128]{1,0:T(8,128)S(1)}, f32[80,128]{1,0:T(8,128)S(1)}, u32[]{:S(2)}, u32[]{:S(2)}) collective-permute-start(f32[80,128]{1,0:T(8,128)S(1)} %get-tuple-element.442), channel_id=1, source_target_pairs={{0,4},{2,18},{4,0},{6,22},{8,12},{10,26},{12,8},{14,30},{16,20},{1... | collective-permute-start | bytes 122888 | tf_op jit(solution)/shard_map/while/body/ppermute | solution.py:349
  46.3 5.5 %collective-permute-start.6 = (f32[160,128]{1,0:T(8,128)S(1)}, f32[160,128]{1,0:T(8,128)S(1)}, u32[]{:S(2)}, u32[]{:S(2)}) collective-permute-start(f32[160,128]{1,0:T(8,128)S(1)} %pad_maximum_fusion.24), channel_id=1, source_target_pairs={{0,16},{2,10},{4,20},{6,14},{8,24},{10,2},{12,28},{14,6},{16,0},{1... | collective-permute-start | bytes 245768 | tf_op jit(solution)/shard_map/while/body/ppermute | solution.py:349
  49.4 5.4 %collective-permute-start.10 = (f32[160,128]{1,0:T(8,128)S(1)}, f32[160,128]{1,0:T(8,128)S(1)}, u32[]{:S(2)}, u32[]{:S(2)}) collective-permute-start(f32[160,128]{1,0:T(8,128)S(1)} %pad_maximum_fusion.28), channel_id=1, source_target_pairs={{0,16},{2,10},{4,20},{6,14},{8,24},{10,2},{12,28},{14,6},{16,0},{1... | collective-permute-start | bytes 245768 | tf_op jit(solution)/shard_map/while/body/ppermute | solution.py:349
  51.8 5.6 %collective-permute-start.7 = (f32[320,128]{1,0:T(8,128)S(1)}, f32[320,128]{1,0:T(8,128)S(1)}, u32[]{:S(2)}, u32[]{:S(2)}) collective-permute-start(f32[320,128]{1,0:T(8,128)S(1)} %pad_maximum_fusion.25), channel_id=1, source_target_pairs={{0,8},{2,6},{4,12},{6,2},{8,0},{10,14},{12,4},{14,10},{16,24},{18,... | collective-permute-start | bytes 491528 | tf_op jit(solution)/shard_map/while/body/ppermute | solution.py:349
  54.8 5.6 %collective-permute-start.11 = (f32[320,128]{1,0:T(8,128)S(1)}, f32[320,128]{1,0:T(8,128)S(1)}, u32[]{:S(2)}, u32[]{:S(2)}) collective-permute-start(f32[320,128]{1,0:T(8,128)S(1)} %pad_maximum_fusion.29), channel_id=1, source_target_pairs={{0,8},{2,6},{4,12},{6,2},{8,0},{10,14},{12,4},{14,10},{16,24},{18,... | collective-permute-start | bytes 491528 | tf_op jit(solution)/shard_map/while/body/ppermute | solution.py:349
  57.5 3.1 %collective-permute-start.8 = (f32[640,128]{1,0:T(8,128)S(1)}, f32[640,128]{1,0:T(8,128)S(1)}, u32[]{:S(2)}, u32[]{:S(2)}) collective-permute-start(f32[640,128]{1,0:T(8,128)S(1)} %pad_maximum_fusion.26), channel_id=1, source_target_pairs={{0,2},{2,0},{4,6},{6,4},{8,10},{10,8},{12,14},{14,12},{16,18},{18,... | collective-permute-start | bytes 983048 | tf_op jit(solution)/shard_map/while/body/ppermute | solution.py:349
  60.5 1.7 collective-permute-start.12
  63.2 35.8 %collective-permute-start.25 = (f32[512,512]{1,0:T(8,128)}, f32[512,512]{1,0:T(8,128)}, u32[]{:S(2)}, u32[]{:S(2)}) collective-permute-start(f32[512,512]{1,0:T(8,128)} %get-tuple-element.232), channel_id=1, source_target_pairs={{0,1},{1,0},{2,3},{3,2},{4,5},{5,4},{6,7},{7,6},{8,9},{9,8},{10,11... | collective-permute-start | bytes 3145736 | tf_op jit(solution)/shard_map/ppermute | solution.py:423
  84.2 1.0 copy-start
  85.2 94.6 %collective-permute-start.26 = (f32[1536,512]{1,0:T(8,128)}, f32[1536,512]{1,0:T(8,128)}, u32[]{:S(2)}, u32[]{:S(2)}) collective-permute-start(f32[1536,512]{1,0:T(8,128)} %get-tuple-element.240), channel_id=1, source_target_pairs={{0,1},{2,3},{4,5},{6,7},{8,9},{10,11},{12,13},{14,15},{16,17},{18,... | collective-permute-start | bytes 9437192 | tf_op jit(solution)/shard_map/ppermute | solution.py:426
  96.7 100.2 %collective-permute-start.24 = (f32[512,512]{1,0:T(8,128)}, f32[512,512]{1,0:T(8,128)}, u32[]{:S(2)}, u32[]{:S(2)}) collective-permute-start(f32[512,512]{1,0:T(8,128)} %get-tuple-element.230), channel_id=1, source_target_pairs={{0,1},{2,3},{4,5},{6,7},{8,9},{10,11},{12,13},{14,15},{16,17},{18,... | collective-permute-start | bytes 3145736 | tf_op jit(solution)/shard_map/ppermute | solution.py:426
  102.3 46.4 %copy-start.1 = (f32[512,512]{1,0:T(8,128)S(1)}, f32[512,512]{1,0:T(8,128)}, u32[]{:S(2)}) copy-start(f32[512,512]{1,0:T(8,128)} %copy-done) | copy-start | bytes 3145732
  102.4 2.0 collective-permute-start.13
  104.5 6.4 %collective-permute-start.14 = (f32[128,512]{1,0:T(8,128)S(1)}, f32[128,512]{1,0:T(8,128)S(1)}, u32[]{:S(2)}, u32[]{:S(2)}) collective-permute-start(f32[128,512]{1,0:T(8,128)S(1)} %slice_select_fusion.21), channel_id=1, source_target_pairs={{0,8},{2,6},{4,12},{6,2},{8,0},{10,14},{12,4},{14,10},{16,24},{18,... | collective-permute-start | bytes 786440 | tf_op jit(solution)/shard_map/while/body/ppermute | solution.py:349
  111.1 6.0 %collective-permute-start.15 = (f32[64,512]{1,0:T(8,128)S(1)}, f32[64,512]{1,0:T(8,128)S(1)}, u32[]{:S(2)}, u32[]{:S(2)}) collective-permute-start(f32[64,512]{1,0:T(8,128)S(1)} %slice_select_fusion.22), channel_id=1, source_target_pairs={{0,16},{2,10},{4,20},{6,14},{8,24},{10,2},{12,28},{14,6},{16,0},{1... | collective-permute-start | bytes 393224 | tf_op jit(solution)/shard_map/while/body/ppermute | solution.py:349
  117.1 6.2 %collective-permute-start.16 = (f32[32,512]{1,0:T(8,128)S(1)}, f32[32,512]{1,0:T(8,128)S(1)}, u32[]{:S(2)}, u32[]{:S(2)}) collective-permute-start(f32[32,512]{1,0:T(8,128)S(1)} %slice_select_fusion.23), channel_id=1, source_target_pairs={{0,5},{1,4},{2,19},{3,18},{4,1},{5,0},{6,23},{7,22},{8,13},{9,12},... | collective-permute-start | bytes 196616 | tf_op jit(solution)/shard_map/while/body/ppermute | solution.py:355
  123.3 4.3 %collective-permute-start.17 = (f32[32,512]{1,0:T(8,128)S(1)}, f32[32,512]{1,0:T(8,128)S(1)}, u32[]{:S(2)}, u32[]{:S(2)}) collective-permute-start(f32[32,512]{1,0:T(8,128)S(1)} %select_add_fusion.23), channel_id=1, source_target_pairs={{0,4},{2,18},{4,0},{6,22},{8,12},{10,26},{12,8},{14,30},{16,20},{1... | collective-permute-start | bytes 196616 | tf_op jit(solution)/shard_map/while/body/ppermute | solution.py:349
  127.7 5.3 %collective-permute-start.18 = (f32[32,512]{1,0:T(8,128)S(1)}, f32[32,512]{1,0:T(8,128)S(1)}, u32[]{:S(2)}, u32[]{:S(2)}) collective-permute-start(f32[32,512]{1,0:T(8,128)S(1)} %add.117), channel_id=1, source_target_pairs={{0,5},{1,4},{2,19},{3,18},{4,1},{5,0},{6,23},{7,22},{8,13},{9,12},... | collective-permute-start | bytes 196616 | tf_op jit(solution)/shard_map/while/body/ppermute | solution.py:355
  133.0 5.9 %collective-permute-start.19 = (f32[64,512]{1,0:T(8,128)S(1)}, f32[64,512]{1,0:T(8,128)S(1)}, u32[]{:S(2)}, u32[]{:S(2)}) collective-permute-start(f32[64,512]{1,0:T(8,128)S(1)} %pad_maximum_fusion.32), channel_id=1, source_target_pairs={{0,16},{2,10},{4,20},{6,14},{8,24},{10,2},{12,28},{14,6},{16,0},{1... | collective-permute-start | bytes 393224 | tf_op jit(solution)/shard_map/while/body/ppermute | solution.py:349
  139.0 6.4 %collective-permute-start.20 = (f32[128,512]{1,0:T(8,128)S(1)}, f32[128,512]{1,0:T(8,128)S(1)}, u32[]{:S(2)}, u32[]{:S(2)}) collective-permute-start(f32[128,512]{1,0:T(8,128)S(1)} %pad_maximum_fusion.33), channel_id=1, source_target_pairs={{0,8},{2,6},{4,12},{6,2},{8,0},{10,14},{12,4},{14,10},{16,24},{18,... | collective-permute-start | bytes 786440 | tf_op jit(solution)/shard_map/while/body/ppermute | solution.py:349
  146.3 2.1 %collective-permute-start.21 = (f32[256,512]{1,0:T(8,128)}, f32[256,512]{1,0:T(8,128)S(1)}, u32[]{:S(2)}, u32[]{:S(2)}) collective-permute-start(f32[256,512]{1,0:T(8,128)} %pad_maximum_fusion.34), channel_id=1, source_target_pairs={{0,2},{2,0},{4,6},{6,4},{8,10},{10,8},{12,14},{14,12},{16,18},{18,... | collective-permute-start | bytes 1572872 | tf_op jit(solution)/shard_map/while/body/ppermute | solution.py:349
  176.5 0.8 copy-start.2
  177.4 0.8 copy-start.3
  179.0 0.8 copy-start.5
  (1 other events, 0.8 us)

commit v3 on v2

--- a/solution.py
+++ b/solution.py
@@ -66,8 +66,9 @@
             copy[...] = block
 
     high, low = split(block)
-    high_acc[:half] += dot(high[:, :half], high, (0, 0)) + dot(low[:, :half], low, (0, 0))
-    high_acc[half:, half:] += dot(high[:, half:], high[:, half:], (0, 0)) + dot(low[:, half:], low[:, half:], (0, 0))
+    both = jnp.concatenate([high, low])
+    high_acc[:half] += dot(both[:, :half], both, (0, 0))
+    high_acc[half:, half:] += dot(both[:, half:], both[:, half:], (0, 0))
     mixed_acc[...] += dot(high, low, (0, 0))
 
     @pl.when(step == pl.num_programs(0) - 1)
@@ -122,7 +123,9 @@
             right = jnp.where(first, other, own)
             lh, ll = split(left)
             rh, rl = split(right * scale)
-            g_ref[...] += (dot(lh, rh, (0, 0)) + dot(ll, rl, (0, 0))) + (dot(lh, rl, (0, 0)) + dot(ll, rh, (0, 0)))
+            left = jnp.concatenate([lh, ll, lh, ll])
+            right = jnp.concatenate([rh, rl, rl, rh])
+            g_ref[...] += dot(left, right, (0, 0))
 
         begin += count
 
@@ -199,7 +202,7 @@
     return upper, inverse
 
 
-def factor_whole(a_ref, r_ref, x_ref, e_ref):
+def factor_whole(a_ref, r_ref, x_ref, e_ref, beside=None):
     order = a_ref.shape[0]
     blocks = order // BLOCK
     groups = BLOCK // GROUP
@@ -213,6 +216,8 @@
         here = pl.ds(start, BLOCK)
         a = [a_ref[pl.ds(start + GROUP * i, GROUP), here] for i in range(groups)]
         x = [jnp.where(lane == row + GROUP * i, 1.0, 0.0) for i in range(groups)]
+        if beside is not None:
+            beside(b, blocks)
         upper, inverse = factor_block(a, x)
         for i in range(groups):
             r_ref[pl.ds(start + GROUP * i, GROUP), here] = upper[i]
@@ -261,87 +266,142 @@
     )(packed)
 
 
-def second_factor_kernel(side_ref, cross_ref, g_ref, r00_ref, x0_ref, f_ref, *refs):
-    own_high, own_low, other_high, other_low, a_ref, r_ref, x_ref, e_ref = refs
+def thrice(x):
+    high, low = split(x)
+    return jnp.concatenate([high, high, low], axis=1)
+
+
+def stacked(w):
+    high, low = split(w)
+    return jnp.concatenate([high, low, high], axis=0)
+
+
+def times_upper(x, left, right):
+    half = x.shape[1] // 2
+    return jnp.concatenate(
+        [dot(thrice(x[:, :half]), left, (1, 0)), dot(thrice(x), right, (1, 0))], axis=1
+    )
+
+
+def finish_kernel(counts, side_ref, cross_ref, g_ref, r00_ref, x0_ref, own_hbm, *refs):
+    chunks, refs = refs[: len(counts)], refs[len(counts) :]
+    f_ref, factor_ref, part_ref, basis_hbm = refs[:4]
+    own, other, u_ref, left_ref, right_ref, a_ref, r_ref, x_ref, e_ref, load_sems, store_sems = refs[4:]
     order = a_ref.shape[0]
+    half = order // 2
+    rows, known = own.shape[0], sum(counts)
     first = side_ref[0] == 0
+    loads = [pltpu.make_async_copy(own_hbm, own, load_sems.at[len(counts)])]
+    begin = 0
+    for k, count in enumerate(counts):
+        loads.append(pltpu.make_async_copy(chunks[k], other.at[pl.ds(begin, count)], load_sems.at[k]))
+        begin += count
+    for load in loads:
+        load.start()
     x0 = x0_ref[...]
     r01 = dot(x0, cross_ref[...], (1, 0), HIGHEST)
+    u = dot3(x0, r01, (0, 0))
+    u_ref[...] = stacked(jnp.where(first, 0.0, u))
     unpack(g_ref, a_ref)
     a_ref[...] -= dot(r01, r01, (0, 0), HIGHEST)
-    u = dot3(x0, r01, (0, 0))
     f_ref[:order] = jnp.where(first, r00_ref[...], r01)
-    factor_whole(a_ref, r_ref, x_ref, e_ref)
+    for load in loads:
+        load.wait()
+
+    def project(b, blocks):
+        size = other.shape[0] // blocks
+        tile = math.gcd(size, TILE)
+        for k in range(size // tile):
+            here = pl.ds(pl.multiple_of(b * size + k * tile, tile), tile)
+            own[here] -= dot(thrice(other[here]), u_ref[...], (1, 0))
+
+    factor_whole(a_ref, r_ref, x_ref, e_ref, project)
+    x1 = x_ref[...]
+    w = jnp.where(first, x0, x1).T
+    left_ref[...] = stacked(w[:half, :half])
+    right_ref[...] = stacked(w[:, half:])
+
+    def store(k):
+        here = pl.ds(pl.multiple_of(k * TILE, TILE), TILE)
+        return pltpu.make_async_copy(own.at[here], basis_hbm.at[here], store_sems.at[k])
+
+    def body(k, carry):
+        here = pl.ds(pl.multiple_of(k * TILE, TILE), TILE)
+        own[here] = times_upper(own[here], left_ref[...], right_ref[...])
+        store(k).start()
+        return carry
+
+    lax.fori_loop(0, known // TILE, body, 0)
+    for k in range(known, rows, TILE):
+        part_ref[k - known : k - known + TILE] = times_upper(own[k : k + TILE], left_ref[...], right_ref[...])
     f_ref[order:] = jnp.where(first, 0.0, r_ref[...])
-    x1 = x_ref[...]
-    own_high[...], own_low[...] = split(jnp.where(first, x0, x1).T)
-    other_high[...], other_low[...] = split(jnp.where(first, 0.0, -dot3(u, x1, (1, 1))))
-
-
-def second_factor(side, cross, packed, r00, x0):
+    factor_ref[...] = stacked(jnp.where(first, 0.0, -dot3(u, x1, (1, 1))))
+    for k in range(known // TILE):
+        store(k).wait()
+
+
+def finish(side, cross, packed, r00, x0, own, chunks):
     order = cross.shape[0]
+    half = order // 2
     square = (order, order)
+    counts = tuple(c.shape[0] for c in chunks)
+    anywhere = pl.BlockSpec(memory_space=pltpu.HBM)
     return pl.pallas_call(
-        second_factor_kernel,
-        out_shape=[jax.ShapeDtypeStruct((2 * order, order), F32)] + [jax.ShapeDtypeStruct(square, BF16)] * 4,
-        in_specs=[pl.BlockSpec(memory_space=pltpu.SMEM)] + whole(4),
-        out_specs=whole(5),
-        scratch_shapes=[pltpu.VMEM(square, F32)] * 3 + [pltpu.VMEM((BLOCK, BLOCK), F32)],
-        compiler_params=params(40),
-        cost_estimate=COST,
-        name="second_factor",
-    )(side, cross, packed, r00, x0)
-
-
-def basis_kernel(counts, own_ref, *refs):
-    chunks = refs[: len(counts)]
-    own_high, own_low, other_high, other_low = refs[len(counts) : len(counts) + 4]
-    out_ref = refs[-1]
-    step = pl.program_id(0)
-
-    def product(x, high, low):
-        xh, xl = split(x)
-        return dot(xh, high[...], (1, 0)) + (dot(xh, low[...], (1, 0)) + dot(xl, high[...], (1, 0)))
-
-    begin = 0
-    for chunk, count in zip(chunks, counts):
-
-        @pl.when((step >= begin) & (step < begin + count))
-        def _():
-            out_ref[...] = product(own_ref[...], own_high, own_low) + product(chunk[...], other_high, other_low)
-
-        begin += count
-
-
-def whitened(own, chunks, factors, row, before):
-    rows, width = own.shape
-    counts = tuple(c.shape[0] // TILE for c in chunks)
-    starts = [sum(counts[:i]) for i in range(len(counts))]
-    offset = row // TILE
-
-    def chunk_spec(begin, count):
-        return pl.BlockSpec((TILE, width), lambda i: (jnp.clip(i - begin, 0, count - 1), 0))
-
-    in_specs = [pl.BlockSpec((TILE, width), lambda i: (i + offset, 0))]
-    in_specs += [chunk_spec(b, c) for b, c in zip(starts, counts)]
-    in_specs += [pl.BlockSpec((width, width), lambda i: (0, 0))] * 4
-    operands = [own, *chunks, *factors]
-    aliases = {}
-    if before is not None:
-        aliases = {len(operands): 0}
-        in_specs.append(pl.BlockSpec(memory_space=pl.ANY))
-        operands.append(before)
-    return pl.pallas_call(
-        functools.partial(basis_kernel, counts),
-        grid=(sum(counts),),
-        in_specs=in_specs,
-        out_specs=pl.BlockSpec((TILE, width), lambda i: (i + offset, 0)),
-        out_shape=jax.ShapeDtypeStruct((rows, width), F32),
-        input_output_aliases=aliases,
+        functools.partial(finish_kernel, counts),
+        out_shape=[
+            jax.ShapeDtypeStruct((2 * order, order), F32),
+            jax.ShapeDtypeStruct((3 * order, order), BF16),
+            jax.ShapeDtypeStruct((own.shape[0] - sum(counts), order), F32),
+            jax.ShapeDtypeStruct(own.shape, F32),
+        ],
+        in_specs=[pl.BlockSpec(memory_space=pltpu.SMEM)] + whole(4) + [anywhere] * (1 + len(chunks)),
+        out_specs=whole(3) + [anywhere],
+        scratch_shapes=[
+            pltpu.VMEM(own.shape, F32),
+            pltpu.VMEM((sum(counts), order), F32),
+            pltpu.VMEM((3 * order, order), BF16),
+            pltpu.VMEM((3 * half, half), BF16),
+            pltpu.VMEM((3 * order, half), BF16),
+            pltpu.VMEM(square, F32),
+            pltpu.VMEM(square, F32),
+            pltpu.VMEM(square, F32),
+            pltpu.VMEM((BLOCK, BLOCK), F32),
+            pltpu.SemaphoreType.DMA((len(chunks) + 1,)),
+            pltpu.SemaphoreType.DMA((sum(counts) // TILE,)),
+        ],
         compiler_params=params(60),
         cost_estimate=COST,
-        name="whitened",
-    )(*operands)
+        name="finish",
+    )(side, cross, packed, r00, x0, own, *chunks)
+
+
+def tail_kernel(start, row, chunk_ref, factor_ref, part_ref, before_hbm, basis_hbm, out, sems):
+    copies = []
+    for k in range(out.shape[0]):
+        size = out.shape[1]
+        here = pl.ds(k * size, size)
+        out[k] = part_ref[pl.ds(start + k * size, size)] + dot(thrice(chunk_ref[here]), factor_ref[...], (1, 0))
+        copies.append(pltpu.make_async_copy(out.at[k], basis_hbm.at[pl.ds(row + k * size, size)], sems.at[k]))
+        copies[-1].start()
+    for copy in copies:
+        copy.wait()
+
+
+def tail(chunk, factor, part, start, row, basis):
+    rows, width = chunk.shape
+    tile = math.gcd(TILE // 2, rows)
+    anywhere = pl.BlockSpec(memory_space=pltpu.HBM)
+    return pl.pallas_call(
+        functools.partial(tail_kernel, start, row),
+        in_specs=whole(3) + [anywhere],
+        out_specs=anywhere,
+        out_shape=jax.ShapeDtypeStruct(basis.shape, F32),
+        scratch_shapes=[pltpu.VMEM((rows // tile, tile, width), F32), pltpu.SemaphoreType.DMA((rows // tile,))],
+        input_output_aliases={3: 0},
+        compiler_params=params(12),
+        cost_estimate=COST,
+        name="tail",
+    )(chunk, factor, part, basis)
 
 
 def flip(x, order, step):
@@ -349,9 +409,9 @@
     return lax.ppermute(x, "dof", [(i, i ^ order[i % 2][step]) for i in range(count)])
 
 
-def flip_side(x, order):
+def flip_side(x, order, sides):
     count = lax.axis_size("dof")
-    pairs = [(2 * i + j, 2 * (i ^ order[i % 2][-1]) + 1 - j) for i in range(count) for j in range(2)]
+    pairs = [(2 * i + j, 2 * (i ^ order[i % 2][-1]) + 1 - j) for i in range(count) for j in sides]
     return lax.ppermute(x, ("dof", "snap"), pairs)
 
 
@@ -385,14 +445,11 @@
     def send(step):
         return lambda x: flip(x, order, step)
 
-    def send_side(x):
-        return flip_side(x, order)
-
     def reduce_own(i, carry):
         shard = carry[0]
         for k in steps:
             shard = halve(shard, bit(k), send(k))
-        received = send_side(shard)
+        received = flip_side(shard, order, (0, 1))
         upper = bit(steps[-1]) ^ (side == 1)
         first = jnp.where(side == 0, shard, received)
         second = jnp.where(side == 0, received, shard)
@@ -406,18 +463,17 @@
     def reduce_cross(i, cross):
         for k in steps[:-1]:
             cross = halve(cross, bit(k), send(k))
-        cross = halve(cross, side == 1, send_side)
+        cross = cross + flip_side(cross, order, (0,))
         cross = cross + send(steps[-1])(cross)
-        cross = double(cross, side == 1, send_side)
         for k in steps[-2::-1]:
             cross = double(cross, bit(k), send(k))
         return cross
 
     half = rows // 2 // TILE
     parts = [half // 4, half // 2, half - half // 4 - half // 2]
-    rests = [3 * half // 4, half - 3 * half // 4]
+    rests = [half // 2, half - half // 2]
     spans = [(parts[0], half, parts[1]), (parts[0] + parts[1], half, parts[2])]
-    spans += [(half, 0, rests[0]), (half + rests[0], 0, rests[1])]
+    spans += [(half + sum(rests[:i]), 0, rests[i]) for i in range(2)]
 
     def swap(x):
         return lax.ppermute(x, "snap", [(0, 1), (1, 0)])
@@ -430,20 +486,20 @@
 
     once = 1 + jnp.minimum(side, 0)
     arrived = [swap(lax.dynamic_slice_in_dim(snapshots, side * half * TILE, parts[0] * TILE, 0))]
-    own, send1, send2, send3, send4 = own_gram(side_operand, snapshots, scale, spans)
-    arrived.append(swap(send1))
+    own, *sends = own_gram(side_operand, snapshots, scale, spans)
+    arrived.append(swap(sends[0]))
     first, second = lax.fori_loop(0, once, reduce_own, (own, own))
-    arrived.append(swap(late(send2, first)))
+    arrived.append(swap(late(sends[1], first)))
     r00, x00 = first_factor(first, width)
-    arrived.append(one_way(late(send3, r00)))
+    arrived.append(one_way(late(sends[2], r00)))
     early = parts[0] + parts[1]
     cross = cross_gram(side_operand, snapshots, arrived[:2], None, [x00, second], 0, scale)
-    arrived.append(one_way(late(send4, cross)))
+    arrived.append(one_way(late(sends[3], cross)))
     cross = cross_gram(side_operand, snapshots, arrived[2:3], cross, [], early * TILE, scale)
     cross = lax.fori_loop(0, once, reduce_cross, cross)
-    factor, *factors = second_factor(side_operand, cross, second, r00, x00)
-    basis = whitened(snapshots, arrived[:-1], factors, 0, None)
-    basis = whitened(snapshots, arrived[-1:], factors, (half + rests[0]) * TILE, basis)
+    factor, share, part, basis = finish(side_operand, cross, second, r00, x00, snapshots, arrived[:4])
+    begin = half + rests[0]
+    basis = tail(arrived[4], share, part, 0, begin * TILE, basis)
     return (basis, factor)
 
 

time: 203 us -> 196 us (0.966)
  Pallas kernels: 93.6 us -> 84.1 us
  waiting for transfers between devices: 47.9 us -> 54.6 us
  starting transfers between devices: 49.1 us -> 43.2 us
  local copies, waits for them, and re-layouts: 7.35 us -> 9.49 us
    pallas_call x3 -> x2, Pallas kernels: 49.9 us -> 40.7 us  [the longest x1 38.1 us: finish(): pl.pallas_call(functools.partial(finish_kernel, counts), out_shape=[jax.S...]
    ppermute x19, waiting for transfers between devices: 41.1 us -> 45.9 us  [flip(): lax.ppermute(x, 'dof', [(i, i ^ order[i % 2][step]) for i in range(count)])]
    ppermute x2, waiting for transfers between devices: 0.01 us -> 4.08 us  [one_way(): return lax.ppermute(x, 'snap', [(0, 1)])]
    ppermute x19, starting transfers between devices: 28.5 us -> 25.6 us  [flip(): lax.ppermute(x, 'dof', [(i, i ^ order[i % 2][step]) for i in range(count)])]
    ppermute x3 -> x2, waiting for transfers between devices: 6.8 us -> 4.6 us  [flip_side(): return lax.ppermute(x, ('dof', 'snap'), pairs)]
    unnamed x13 -> x11, local copies, waits for them, and re-layouts: 5.08 us -> 7.2 us
    ppermute x3 -> x2, starting transfers between devices: 9.76 us -> 7.89 us  [flip_side(): return lax.ppermute(x, ('dof', 'snap'), pairs)]
  transfers between devices with their start and end apart: 27 -> 26, of which waited for: 20 -> 20; matrix products, arithmetic and copies ran while one was open for 2% -> 2% of each run, Pallas kernels for 44% -> 42%
where the time goes in v3:
time: 196 us; the launch traced here: 195 us
  Pallas kernels  84.1 us (43%)
  waiting for transfers between devices  54.6 us (28%)
  starting transfers between devices  43.2 us (22%)
  local copies, waits for them, and re-layouts  9.49 us (5%)
  other arithmetic  2.89 us (1%)
    ppermute x19, waiting for transfers between devices, flip(): lax.ppermute(x, 'dof', [(i, i ^ order[i % 2][step]) for i in range(count)])  45.9 us
    pallas_call x1, Pallas kernels, finish(): pl.pallas_call(functools.partial(finish_kernel, counts), out_shape=[jax.S...  38.1 us
    ppermute x19, starting transfers between devices, flip(): lax.ppermute(x, 'dof', [(i, i ^ order[i % 2][step]) for i in range(count)])  25.6 us
    pallas_call x1, Pallas kernels, first_factor(): pl.pallas_call(first_factor_kernel, out_shape=[square, square], in_specs=...  19.6 us
    pallas_call x1, Pallas kernels, own_gram(): pl.pallas_call(functools.partial(own_gram_kernel, scale, spans), grid_spe...  13.3 us
    pallas_call x2, Pallas kernels, cross_gram(): pl.pallas_call(functools.partial(cross_gram_kernel, scale, before is not...  10.5 us
    ppermute x2, starting transfers between devices, flip_side(): return lax.ppermute(x, ('dof', 'snap'), pairs)  7.89 us
    unnamed x11, local copies, waits for them, and re-layouts  7.2 us
  transfers between devices with their start and end apart: 26, of which 20 were waited for; matrix products, arithmetic and copies ran while one was open for 2% of the time, Pallas kernels for 42%

profile of v3, /device:TPU:0, one launch (start us, length us, event | category | flops | bytes accessed | tf_op | source)
XLA Modules:
  0.0 195.4 jit_solution(2770842905494334931)
XLA Ops:
  0.6 2.3 %constant_dynamic-slice_fusion = f32[512,512]{1,0:T(8,128)} fusion(f32[4096,512]{1,0:T(8,128)} %own_hbm.1, s32[]{:T(128)S(6)} %select_n.366), kind=kLoop, calls=%fused_computation.49 | loop fusion | bytes 2097156 | tf_op jit(solution)/shard_map/dynamic_slice | solution.py:488
  2.9 3.0 %collective-permute-start.21 = (f32[512,512]{1,0:T(8,128)}, f32[512,512]{1,0:T(8,128)}, u32[]{:S(2)}, u32[]{:S(2)}) collective-permute-start(f32[512,512]{1,0:T(8,128)} %constant_dynamic-slice_fusion), channel_id=1, source_target_pairs={{0,1},{1,0},{2,3},{3,2},{4,5},{5,4},{6,7},{7,6},{8,9},{9,8},{10,11... | collective-permute-start | bytes 3145736 | tf_op jit(solution)/shard_map/ppermute | solution.py:479
  5.9 13.3 %own_gram.1 = (f32[1280,128]{1,0:T(8,128)S(1)}, f32[1024,512]{1,0:T(8,128)}, f32[512,512]{1,0:T(8,128)}, f32[1024,512]{1,0:T(8,128)}, f32[1024,512]{1,0:T(8,128)}) custom-call(s32[1]{0:T(128)} %bitcast.side_ref, f32[4096,512]{1,0:T(8,128)} %own_hbm.1), custom_call_target="tpu_custom_call" | custom-call | flops 1 | bytes 1 | tf_op jit(solution)/shard_map/own_gram/pallas_call | solution.py:90
  20.0 42.8 %while.26 = (s32[]{:T(128)}, f32[1280,128]{1,0:T(8,128)S(1)}, f32[1280,128]{1,0:T(8,128)}, s32[]{:T(128)}, pred[]{:T(512)}, /*index=5*/pred[]{:T(512)}, pred[]{:...) while((s32[]{:T(128)}, f32[1280,128]{1,0:T(8,128)S(1)}, ...), condition=%wide.region_1.2_spmd, body=%wide.region_0.1_spmd.sunk | while | flops 1996802 | bytes 21832332 | solution.py:491
  23.9 3.4 %collective-permute-done.1 = f32[320,128]{1,0:T(8,128)S(1)} collective-permute-done((f32[320,128]{1,0:T(8,128)S(1)}, f32[320,128]{1,0:T(8,128)S(1)}, u32[]{:S(2)}, u32[]{:S(2)}) %collective-permute-start.1) | collective-permute-done | bytes 163872 | tf_op jit(solution)/shard_map/while/body/ppermute | solution.py:409
  27.3 3.0 %collective-permute-start.2 = (f32[160,128]{1,0:T(8,128)S(1)}, f32[160,128]{1,0:T(8,128)S(1)}, u32[]{:S(2)}, u32[]{:S(2)}) collective-permute-start(f32[160,128]{1,0:T(8,128)S(1)} %slice_select_fusion.16), channel_id=1, source_target_pairs={{0,16},{2,10},{4,20},{6,14},{8,24},{10,2},{12,28},{14,6},{16,0},{1... | collective-permute-start | bytes 245768 | tf_op jit(solution)/shard_map/while/body/ppermute | solution.py:409
  30.3 2.4 %collective-permute-done.2 = f32[160,128]{1,0:T(8,128)S(1)} collective-permute-done((f32[160,128]{1,0:T(8,128)S(1)}, f32[160,128]{1,0:T(8,128)S(1)}, u32[]{:S(2)}, u32[]{:S(2)}) %collective-permute-start.2) | collective-permute-done | bytes 81952 | tf_op jit(solution)/shard_map/while/body/ppermute | solution.py:409
  34.6 2.2 %collective-permute-done.3 = f32[80,128]{1,0:T(8,128)S(1)} collective-permute-done((f32[80,128]{1,0:T(8,128)S(1)}, f32[80,128]{1,0:T(8,128)S(1)}, u32[]{:S(2)}, u32[]{:S(2)}) %collective-permute-start.3) | collective-permute-done | bytes 40992 | tf_op jit(solution)/shard_map/while/body/ppermute | solution.py:409
  36.8 3.0 %collective-permute-start.4 = (f32[80,128]{1,0:T(8,128)S(1)}, f32[80,128]{1,0:T(8,128)S(1)}, u32[]{:S(2)}, u32[]{:S(2)}) collective-permute-start(f32[80,128]{1,0:T(8,128)S(1)} %select_add_fusion.17), channel_id=1, source_target_pairs={{0,5},{1,4},{2,19},{3,18},{4,1},{5,0},{6,23},{7,22},{8,13},{9,12},... | collective-permute-start | bytes 122888 | tf_op jit(solution)/shard_map/while/body/ppermute | solution.py:415
  39.8 2.1 %collective-permute-done.4 = f32[80,128]{1,0:T(8,128)S(1)} collective-permute-done((f32[80,128]{1,0:T(8,128)S(1)}, f32[80,128]{1,0:T(8,128)S(1)}, u32[]{:S(2)}, u32[]{:S(2)}) %collective-permute-start.4) | collective-permute-done | bytes 40992 | tf_op jit(solution)/shard_map/while/body/ppermute | solution.py:415
  46.0 3.1 %collective-permute-start.6 = (f32[160,128]{1,0:T(8,128)S(1)}, f32[160,128]{1,0:T(8,128)S(1)}, u32[]{:S(2)}, u32[]{:S(2)}) collective-permute-start(f32[160,128]{1,0:T(8,128)S(1)} %pad_maximum_fusion.22), channel_id=1, source_target_pairs={{0,16},{2,10},{4,20},{6,14},{8,24},{10,2},{12,28},{14,6},{16,0},{1... | collective-permute-start | bytes 245768 | tf_op jit(solution)/shard_map/while/body/ppermute | solution.py:409
  51.5 2.3 %collective-permute-start.7 = (f32[320,128]{1,0:T(8,128)S(1)}, f32[320,128]{1,0:T(8,128)S(1)}, u32[]{:S(2)}, u32[]{:S(2)}) collective-permute-start(f32[320,128]{1,0:T(8,128)S(1)} %pad_maximum_fusion.23), channel_id=1, source_target_pairs={{0,8},{2,6},{4,12},{6,2},{8,0},{10,14},{12,4},{14,10},{16,24},{18,... | collective-permute-start | bytes 491528 | tf_op jit(solution)/shard_map/while/body/ppermute | solution.py:409
  54.6 2.3 %collective-permute-start.11 = (f32[320,128]{1,0:T(8,128)S(1)}, f32[320,128]{1,0:T(8,128)S(1)}, u32[]{:S(2)}, u32[]{:S(2)}) collective-permute-start(f32[320,128]{1,0:T(8,128)S(1)} %pad_maximum_fusion.27), channel_id=1, source_target_pairs={{0,8},{2,6},{4,12},{6,2},{8,0},{10,14},{12,4},{14,10},{16,24},{18,... | collective-permute-start | bytes 491528 | tf_op jit(solution)/shard_map/while/body/ppermute | solution.py:409
  57.3 2.9 %collective-permute-done.11 = f32[320,128]{1,0:T(8,128)S(1)} collective-permute-done((f32[320,128]{1,0:T(8,128)S(1)}, f32[320,128]{1,0:T(8,128)S(1)}, u32[]{:S(2)}, u32[]{:S(2)}) %collective-permute-start.11) | collective-permute-done | bytes 163872 | tf_op jit(solution)/shard_map/while/body/ppermute | solution.py:409
  64.5 19.6 %first_factor.1 = (f32[512,512]{1,0:T(8,128)S(1)}, f32[512,512]{1,0:T(8,128)S(1)}) custom-call(f32[1280,128]{1,0:T(8,128)S(1)} %get-tuple-element.213.g_ref), custom_call_target="tpu_custom_call" | custom-call | flops 1 | bytes 1 | tf_op jit(solution)/shard_map/first_factor/pallas_call | solution.py:257
  86.2 3.6 %collective-permute-start.25 = (f32[1024,512]{1,0:T(8,128)}, f32[1024,512]{1,0:T(8,128)}, u32[]{:S(2)}, u32[]{:S(2)}) collective-permute-start(f32[1024,512]{1,0:T(8,128)} %get-tuple-element.222), channel_id=1, source_target_pairs={{0,1},{2,3},{4,5},{6,7},{8,9},{10,11},{12,13},{14,15},{16,17},{18,... | collective-permute-start | bytes 6291464 | tf_op jit(solution)/shard_map/ppermute | solution.py:482
  91.1 7.2 %cross_gram.2.refs_1_ = f32[512,512]{1,0:T(8,128)} custom-call(s32[1]{0:T(128)} %bitcast.side_ref, f32[4096,512]{1,0:T(8,128)} %own_hbm.1, f32[512,512]{1,0:T(8,128)} %collective-permute-done.21.refs_0_, f32[1024,512]{1,0:T(8,128)} %copy-done.4, f32[512,512]{1,0:T(8,128)} %copy-done, f32[1280,128]{1,0:T(8,128)} %get-tuple-element.215.refs_3_.g_ref), custom_call_target="tpu_custom_call" | custom-call | flops 1 | bytes 1 | tf_op jit(solution)/shard_map/cross_gram/pallas_call | solution.py:148
  99.8 3.2 %cross_gram.3 = f32[512,512]{1,0:T(8,128)S(1)} custom-call(s32[1]{0:T(128)} %bitcast.side_ref, f32[4096,512]{1,0:T(8,128)} %own_hbm.1, f32[512,512]{1,0:T(8,128)} %collective-permute-done.24.refs_0_.refs_2_, f32[512,512]{1,0:T(8,128)} %cross_gram.2.refs_1_), custom_call_target="tpu_custom_call" | custom-call | flops 1 | bytes 1 | tf_op jit(solution)/shard_map/cross_gram/pallas_call | solution.py:148
  103.0 44.4 %while.27 = (s32[]{:T(128)}, f32[512,512]{1,0:T(8,128)S(1)}, s32[]{:T(128)}, pred[]{:T(512)}, pred[]{:T(512)}, /*index=5*/pred[]{:T(512)}, s32[]{:T(128)}) while((s32[]{:T(128)}, f32[512,512]{1,0:T(8,128)S(1)}, s32[]{:T(128)}, pred[]{:T(512)}, pred[]{:T(512)}, /*index=5*/pred[]{:T(512)}, s32[]{:T(128)}) %tuple.94), condition=%wide.region_3.4_spmd, body=%wide.region_2.3_spmd.sunk | while | flops 1867778 | bytes 22938004 | solution.py:499
  105.3 2.1 %collective-permute-start.14 = (f32[128,512]{1,0:T(8,128)S(1)}, f32[128,512]{1,0:T(8,128)S(1)}, u32[]{:S(2)}, u32[]{:S(2)}) collective-permute-start(f32[128,512]{1,0:T(8,128)S(1)} %slice_select_fusion.19), channel_id=1, source_target_pairs={{0,8},{2,6},{4,12},{6,2},{8,0},{10,14},{12,4},{14,10},{16,24},{18,... | collective-permute-start | bytes 786440 | tf_op jit(solution)/shard_map/while/body/ppermute | solution.py:409
  107.4 4.4 %collective-permute-done.14 = f32[128,512]{1,0:T(8,128)S(1)} collective-permute-done((f32[128,512]{1,0:T(8,128)S(1)}, f32[128,512]{1,0:T(8,128)S(1)}, u32[]{:S(2)}, u32[]{:S(2)}) %collective-permute-start.14) | collective-permute-done | bytes 262176 | tf_op jit(solution)/shard_map/while/body/ppermute | solution.py:409
  111.8 3.1 %collective-permute-start.15 = (f32[64,512]{1,0:T(8,128)S(1)}, f32[64,512]{1,0:T(8,128)S(1)}, u32[]{:S(2)}, u32[]{:S(2)}) collective-permute-start(f32[64,512]{1,0:T(8,128)S(1)} %slice_select_fusion.20), channel_id=1, source_target_pairs={{0,16},{2,10},{4,20},{6,14},{8,24},{10,2},{12,28},{14,6},{16,0},{1... | collective-permute-start | bytes 393224 | tf_op jit(solution)/shard_map/while/body/ppermute | solution.py:409
  114.9 3.0 %collective-permute-done.15 = f32[64,512]{1,0:T(8,128)S(1)} collective-permute-done((f32[64,512]{1,0:T(8,128)S(1)}, f32[64,512]{1,0:T(8,128)S(1)}, u32[]{:S(2)}, u32[]{:S(2)}) %collective-permute-start.15) | collective-permute-done | bytes 131104 | tf_op jit(solution)/shard_map/while/body/ppermute | solution.py:409
  117.9 4.9 %collective-permute-start.16 = (f32[64,512]{1,0:T(8,128)S(1)}, f32[64,512]{1,0:T(8,128)S(1)}, u32[]{:S(2)}, u32[]{:S(2)}) collective-permute-start(f32[64,512]{1,0:T(8,128)S(1)} %select_add_fusion.20), channel_id=1, source_target_pairs={{0,5},{2,19},{4,1},{6,23},{8,13},{10,27},{12,9},{14,31},{16,21},{1... | collective-permute-start | bytes 393224 | tf_op jit(solution)/shard_map/while/body/ppermute | solution.py:415
  122.8 2.5 %collective-permute-done.16 = f32[64,512]{1,0:T(8,128)S(1)} collective-permute-done((f32[64,512]{1,0:T(8,128)S(1)}, f32[64,512]{1,0:T(8,128)S(1)}, u32[]{:S(2)}, u32[]{:S(2)}) %collective-permute-start.16) | collective-permute-done | bytes 131104 | tf_op jit(solution)/shard_map/while/body/ppermute | solution.py:415
  125.9 4.4 %collective-permute-done.17 = f32[64,512]{1,0:T(8,128)S(1)} collective-permute-done((f32[64,512]{1,0:T(8,128)S(1)}, f32[64,512]{1,0:T(8,128)S(1)}, u32[]{:S(2)}, u32[]{:S(2)}) %collective-permute-start.17) | collective-permute-done | bytes 131104 | tf_op jit(solution)/shard_map/while/body/ppermute | solution.py:409
  131.7 6.0 %collective-permute-done.18 = f32[64,512]{1,0:T(8,128)S(1)} collective-permute-done((f32[64,512]{1,0:T(8,128)S(1)}, f32[64,512]{1,0:T(8,128)S(1)}, u32[]{:S(2)}, u32[]{:S(2)}) %collective-permute-start.18) | collective-permute-done | bytes 131104 | tf_op jit(solution)/shard_map/while/body/ppermute | solution.py:409
  137.9 6.4 %collective-permute-done.19 = f32[128,512]{1,0:T(8,128)S(1)} collective-permute-done((f32[128,512]{1,0:T(8,128)S(1)}, f32[128,512]{1,0:T(8,128)S(1)}, u32[]{:S(2)}, u32[]{:S(2)}) %collective-permute-start.19) | collective-permute-done | bytes 262176 | tf_op jit(solution)/shard_map/while/body/ppermute | solution.py:409
  145.1 2.1 %collective-permute-done.20 = f32[256,512]{1,0:T(8,128)S(1)} collective-permute-done((f32[256,512]{1,0:T(8,128)}, f32[256,512]{1,0:T(8,128)S(1)}, u32[]{:S(2)}, u32[]{:S(2)}) %collective-permute-start.20) | collective-permute-done | bytes 524320 | tf_op jit(solution)/shard_map/while/body/ppermute | solution.py:409
  147.4 38.1 %finish.1 = (f32[1024,512]{1,0:T(8,128)}, bf16[1536,512]{1,0:T(8,128)(2,1)}, f32[1024,512]{1,0:T(8,128)}, f32[4096,512]{1,0:T(8,128)}) custom-call(s32[1]{0:T(128)} %bitcast.side_ref, f32[512,512]{1,0:T(8,128)S(1)} %get-tuple-element.219.cross_ref, f32[1280,128]{1,0:T(8,128)} %get-tuple-element.215.refs_3_.g_ref, f32[512,512]{1,0:T(8,128)} %copy-done.3, ...), custom_call_target="tpu_custom_call" | custom-call | flops 1 | bytes 1 | tf_op jit(solution)/shard_map/finish/pallas_call | solution.py:349
  185.5 4.1 %collective-permute-done.23.chunk_ref = f32[1024,512]{1,0:T(8,128)S(1)} collective-permute-done((f32[1024,512]{1,0:T(8,128)}, f32[1024,512]{1,0:T(8,128)S(1)}, u32[]{:S(2)}, u32[]{:S(2)}) %collective-permute-start.23) | collective-permute-done | bytes 2097184 | tf_op jit(solution)/shard_map/ppermute | solution.py:482
  192.6 2.6 %tail.1 = f32[4096,512]{1,0:T(8,128)} custom-call(f32[1024,512]{1,0:T(8,128)S(1)} %collective-permute-done.23.chunk_ref, bf16[1536,512]{1,0:T(8,128)(2,1)S(1)} %copy-done.2, f32[1024,512]{1,0:T(8,128)S(1)} %copy-done.1, f32[4096,512]{1,0:T(8,128)} %get-tuple-element.225.before_hbm), custom_call_target="tpu_custom_call", output_to_operand_aliasing={{}: (3, {})} | custom-call | flops 1 | bytes 1 | tf_op jit(solution)/shard_map/tail/pallas_call | solution.py:394
  (79 shorter events, 31.8 us)
Async XLA Ops:
  2.9 86.8 %collective-permute-start.21 = (f32[512,512]{1,0:T(8,128)}, f32[512,512]{1,0:T(8,128)}, u32[]{:S(2)}, u32[]{:S(2)}) collective-permute-start(f32[512,512]{1,0:T(8,128)} %constant_dynamic-slice_fusion), channel_id=1, source_target_pairs={{0,1},{1,0},{2,3},{3,2},{4,5},{5,4},{6,7},{7,6},{8,9},{9,8},{10,11... | collective-permute-start | bytes 3145736 | tf_op jit(solution)/shard_map/ppermute | solution.py:479
  19.2 70.6 %collective-permute-start.22 = (f32[1024,512]{1,0:T(8,128)}, f32[1024,512]{1,0:T(8,128)S(1)}, u32[]{:S(2)}, u32[]{:S(2)}) collective-permute-start(f32[1024,512]{1,0:T(8,128)} %get-tuple-element.211), channel_id=1, source_target_pairs={{0,1},{1,0},{2,3},{3,2},{4,5},{5,4},{6,7},{7,6},{8,9},{9,8},{10,11... | collective-permute-start | bytes 6291464 | tf_op jit(solution)/shard_map/ppermute | solution.py:479
  20.1 1.7 collective-permute-start
  21.8 5.4 %collective-permute-start.1 = (f32[320,128]{1,0:T(8,128)S(1)}, f32[320,128]{1,0:T(8,128)S(1)}, u32[]{:S(2)}, u32[]{:S(2)}) collective-permute-start(f32[320,128]{1,0:T(8,128)S(1)} %slice_select_fusion.15), channel_id=1, source_target_pairs={{0,8},{2,6},{4,12},{6,2},{8,0},{10,14},{12,4},{14,10},{16,24},{18,... | collective-permute-start | bytes 491528 | tf_op jit(solution)/shard_map/while/body/ppermute | solution.py:409
  27.3 5.4 %collective-permute-start.2 = (f32[160,128]{1,0:T(8,128)S(1)}, f32[160,128]{1,0:T(8,128)S(1)}, u32[]{:S(2)}, u32[]{:S(2)}) collective-permute-start(f32[160,128]{1,0:T(8,128)S(1)} %slice_select_fusion.16), channel_id=1, source_target_pairs={{0,16},{2,10},{4,20},{6,14},{8,24},{10,2},{12,28},{14,6},{16,0},{1... | collective-permute-start | bytes 245768 | tf_op jit(solution)/shard_map/while/body/ppermute | solution.py:409
  32.8 4.1 %collective-permute-start.3 = (f32[80,128]{1,0:T(8,128)S(1)}, f32[80,128]{1,0:T(8,128)S(1)}, u32[]{:S(2)}, u32[]{:S(2)}) collective-permute-start(f32[80,128]{1,0:T(8,128)S(1)} %slice_select_fusion.17), channel_id=1, source_target_pairs={{0,4},{2,18},{4,0},{6,22},{8,12},{10,26},{12,8},{14,30},{16,20},{1... | collective-permute-start | bytes 122888 | tf_op jit(solution)/shard_map/while/body/ppermute | solution.py:409
  36.8 5.1 %collective-permute-start.4 = (f32[80,128]{1,0:T(8,128)S(1)}, f32[80,128]{1,0:T(8,128)S(1)}, u32[]{:S(2)}, u32[]{:S(2)}) collective-permute-start(f32[80,128]{1,0:T(8,128)S(1)} %select_add_fusion.17), channel_id=1, source_target_pairs={{0,5},{1,4},{2,19},{3,18},{4,1},{5,0},{6,23},{7,22},{8,13},{9,12},... | collective-permute-start | bytes 122888 | tf_op jit(solution)/shard_map/while/body/ppermute | solution.py:415
  41.9 4.1 %collective-permute-start.5 = (f32[80,128]{1,0:T(8,128)S(1)}, f32[80,128]{1,0:T(8,128)S(1)}, u32[]{:S(2)}, u32[]{:S(2)}) collective-permute-start(f32[80,128]{1,0:T(8,128)S(1)} %get-tuple-element.407), channel_id=1, source_target_pairs={{0,4},{2,18},{4,0},{6,22},{8,12},{10,26},{12,8},{14,30},{16,20},{1... | collective-permute-start | bytes 122888 | tf_op jit(solution)/shard_map/while/body/ppermute | solution.py:409
  43.8 5.3 %collective-permute-start.9 = (f32[80,128]{1,0:T(8,128)S(1)}, f32[80,128]{1,0:T(8,128)S(1)}, u32[]{:S(2)}, u32[]{:S(2)}) collective-permute-start(f32[80,128]{1,0:T(8,128)S(1)} %get-tuple-element.416), channel_id=1, source_target_pairs={{0,4},{2,18},{4,0},{6,22},{8,12},{10,26},{12,8},{14,30},{16,20},{1... | collective-permute-start | bytes 122888 | tf_op jit(solution)/shard_map/while/body/ppermute | solution.py:409
  46.0 5.5 %collective-permute-start.6 = (f32[160,128]{1,0:T(8,128)S(1)}, f32[160,128]{1,0:T(8,128)S(1)}, u32[]{:S(2)}, u32[]{:S(2)}) collective-permute-start(f32[160,128]{1,0:T(8,128)S(1)} %pad_maximum_fusion.22), channel_id=1, source_target_pairs={{0,16},{2,10},{4,20},{6,14},{8,24},{10,2},{12,28},{14,6},{16,0},{1... | collective-permute-start | bytes 245768 | tf_op jit(solution)/shard_map/while/body/ppermute | solution.py:409
  49.1 5.4 %collective-permute-start.10 = (f32[160,128]{1,0:T(8,128)S(1)}, f32[160,128]{1,0:T(8,128)S(1)}, u32[]{:S(2)}, u32[]{:S(2)}) collective-permute-start(f32[160,128]{1,0:T(8,128)S(1)} %pad_maximum_fusion.26), channel_id=1, source_target_pairs={{0,16},{2,10},{4,20},{6,14},{8,24},{10,2},{12,28},{14,6},{16,0},{1... | collective-permute-start | bytes 245768 | tf_op jit(solution)/shard_map/while/body/ppermute | solution.py:409
  51.5 5.6 %collective-permute-start.7 = (f32[320,128]{1,0:T(8,128)S(1)}, f32[320,128]{1,0:T(8,128)S(1)}, u32[]{:S(2)}, u32[]{:S(2)}) collective-permute-start(f32[320,128]{1,0:T(8,128)S(1)} %pad_maximum_fusion.23), channel_id=1, source_target_pairs={{0,8},{2,6},{4,12},{6,2},{8,0},{10,14},{12,4},{14,10},{16,24},{18,... | collective-permute-start | bytes 491528 | tf_op jit(solution)/shard_map/while/body/ppermute | solution.py:409
  54.6 5.6 %collective-permute-start.11 = (f32[320,128]{1,0:T(8,128)S(1)}, f32[320,128]{1,0:T(8,128)S(1)}, u32[]{:S(2)}, u32[]{:S(2)}) collective-permute-start(f32[320,128]{1,0:T(8,128)S(1)} %pad_maximum_fusion.27), channel_id=1, source_target_pairs={{0,8},{2,6},{4,12},{6,2},{8,0},{10,14},{12,4},{14,10},{16,24},{18,... | collective-permute-start | bytes 491528 | tf_op jit(solution)/shard_map/while/body/ppermute | solution.py:409
  57.2 3.1 %collective-permute-start.8 = (f32[640,128]{1,0:T(8,128)S(1)}, f32[640,128]{1,0:T(8,128)S(1)}, u32[]{:S(2)}, u32[]{:S(2)}) collective-permute-start(f32[640,128]{1,0:T(8,128)S(1)} %pad_maximum_fusion.24), channel_id=1, source_target_pairs={{0,2},{2,0},{4,6},{6,4},{8,10},{10,8},{12,14},{14,12},{16,18},{18,... | collective-permute-start | bytes 983048 | tf_op jit(solution)/shard_map/while/body/ppermute | solution.py:409
  60.2 1.7 collective-permute-start.12
  62.9 36.9 %collective-permute-start.24 = (f32[512,512]{1,0:T(8,128)}, f32[512,512]{1,0:T(8,128)}, u32[]{:S(2)}, u32[]{:S(2)}) collective-permute-start(f32[512,512]{1,0:T(8,128)} %get-tuple-element.218), channel_id=1, source_target_pairs={{0,1},{1,0},{2,3},{3,2},{4,5},{5,4},{6,7},{7,6},{8,9},{9,8},{10,11... | collective-permute-start | bytes 3145736 | tf_op jit(solution)/shard_map/ppermute | solution.py:479
  84.2 1.0 copy-start
  85.2 1.0 copy-start.3
  86.2 61.3 %collective-permute-start.25 = (f32[1024,512]{1,0:T(8,128)}, f32[1024,512]{1,0:T(8,128)}, u32[]{:S(2)}, u32[]{:S(2)}) collective-permute-start(f32[1024,512]{1,0:T(8,128)} %get-tuple-element.222), channel_id=1, source_target_pairs={{0,1},{2,3},{4,5},{6,7},{8,9},{10,11},{12,13},{14,15},{16,17},{18,... | collective-permute-start | bytes 6291464 | tf_op jit(solution)/shard_map/ppermute | solution.py:482
  89.8 1.4 copy-start.4
  98.4 91.3 %collective-permute-start.23 = (f32[1024,512]{1,0:T(8,128)}, f32[1024,512]{1,0:T(8,128)S(1)}, u32[]{:S(2)}, u32[]{:S(2)}) collective-permute-start(f32[1024,512]{1,0:T(8,128)} %get-tuple-element.216), channel_id=1, source_target_pairs={{0,1},{2,3},{4,5},{6,7},{8,9},{10,11},{12,13},{14,15},{16,17},{18,... | collective-permute-start | bytes 6291464 | tf_op jit(solution)/shard_map/ppermute | solution.py:482
  103.1 2.0 %collective-permute-start.13 = (f32[256,512]{1,0:T(8,128)S(1)}, f32[256,512]{1,0:T(8,128)S(1)}, u32[]{:S(2)}, u32[]{:S(2)}) collective-permute-start(f32[256,512]{1,0:T(8,128)S(1)} %slice_select_fusion.18), channel_id=1, source_target_pairs={{0,2},{2,0},{4,6},{6,4},{8,10},{10,8},{12,14},{14,12},{16,18},{18,... | collective-permute-start | bytes 1572872 | tf_op jit(solution)/shard_map/while/body/ppermute | solution.py:409
  105.3 6.5 %collective-permute-start.14 = (f32[128,512]{1,0:T(8,128)S(1)}, f32[128,512]{1,0:T(8,128)S(1)}, u32[]{:S(2)}, u32[]{:S(2)}) collective-permute-start(f32[128,512]{1,0:T(8,128)S(1)} %slice_select_fusion.19), channel_id=1, source_target_pairs={{0,8},{2,6},{4,12},{6,2},{8,0},{10,14},{12,4},{14,10},{16,24},{18,... | collective-permute-start | bytes 786440 | tf_op jit(solution)/shard_map/while/body/ppermute | solution.py:409
  111.8 6.0 %collective-permute-start.15 = (f32[64,512]{1,0:T(8,128)S(1)}, f32[64,512]{1,0:T(8,128)S(1)}, u32[]{:S(2)}, u32[]{:S(2)}) collective-permute-start(f32[64,512]{1,0:T(8,128)S(1)} %slice_select_fusion.20), channel_id=1, source_target_pairs={{0,16},{2,10},{4,20},{6,14},{8,24},{10,2},{12,28},{14,6},{16,0},{1... | collective-permute-start | bytes 393224 | tf_op jit(solution)/shard_map/while/body/ppermute | solution.py:409
  117.9 7.4 %collective-permute-start.16 = (f32[64,512]{1,0:T(8,128)S(1)}, f32[64,512]{1,0:T(8,128)S(1)}, u32[]{:S(2)}, u32[]{:S(2)}) collective-permute-start(f32[64,512]{1,0:T(8,128)S(1)} %select_add_fusion.20), channel_id=1, source_target_pairs={{0,5},{2,19},{4,1},{6,23},{8,13},{10,27},{12,9},{14,31},{16,21},{1... | collective-permute-start | bytes 393224 | tf_op jit(solution)/shard_map/while/body/ppermute | solution.py:415
  125.3 5.0 %collective-permute-start.17 = (f32[64,512]{1,0:T(8,128)S(1)}, f32[64,512]{1,0:T(8,128)S(1)}, u32[]{:S(2)}, u32[]{:S(2)}) collective-permute-start(f32[64,512]{1,0:T(8,128)S(1)} %add.115), channel_id=1, source_target_pairs={{0,4},{2,18},{4,0},{6,22},{8,12},{10,26},{12,8},{14,30},{16,20},{1... | collective-permute-start | bytes 393224 | tf_op jit(solution)/shard_map/while/body/ppermute | solution.py:409
  130.4 7.3 %collective-permute-start.18 = (f32[64,512]{1,0:T(8,128)S(1)}, f32[64,512]{1,0:T(8,128)S(1)}, u32[]{:S(2)}, u32[]{:S(2)}) collective-permute-start(f32[64,512]{1,0:T(8,128)S(1)} %add.116), channel_id=1, source_target_pairs={{0,16},{2,10},{4,20},{6,14},{8,24},{10,2},{12,28},{14,6},{16,0},{1... | collective-permute-start | bytes 393224 | tf_op jit(solution)/shard_map/while/body/ppermute | solution.py:409
  137.8 6.4 %collective-permute-start.19 = (f32[128,512]{1,0:T(8,128)S(1)}, f32[128,512]{1,0:T(8,128)S(1)}, u32[]{:S(2)}, u32[]{:S(2)}) collective-permute-start(f32[128,512]{1,0:T(8,128)S(1)} %pad_maximum_fusion.30), channel_id=1, source_target_pairs={{0,8},{2,6},{4,12},{6,2},{8,0},{10,14},{12,4},{14,10},{16,24},{18,... | collective-permute-start | bytes 786440 | tf_op jit(solution)/shard_map/while/body/ppermute | solution.py:409
  145.1 2.1 %collective-permute-start.20 = (f32[256,512]{1,0:T(8,128)}, f32[256,512]{1,0:T(8,128)S(1)}, u32[]{:S(2)}, u32[]{:S(2)}) collective-permute-start(f32[256,512]{1,0:T(8,128)} %pad_maximum_fusion.31), channel_id=1, source_target_pairs={{0,2},{2,0},{4,6},{6,4},{8,10},{10,8},{12,14},{14,12},{16,18},{18,... | collective-permute-start | bytes 1572872 | tf_op jit(solution)/shard_map/while/body/ppermute | solution.py:409
  189.6 1.6 copy-start.1
  191.2 1.4 copy-start.2

commit v4 on v3

--- a/solution.py
+++ b/solution.py
@@ -41,6 +41,41 @@
     ah, al = split(a)
     bh, bl = split(b)
     return dot(ah, bh, contract) + (dot(ah, bl, contract) + dot(al, bh, contract))
+
+
+def pick_kernel(starts, side_ref, s_hbm, out_hbm, buffer, in_sems, out_sems):
+    count, rows = buffer.shape[:2]
+    start = pl.multiple_of(jnp.where(side_ref[0] == 0, starts[0], starts[1]), TILE)
+    ins, outs = [], []
+    for k in range(count):
+        here = pl.ds(k * rows, rows)
+        ins.append(pltpu.make_async_copy(s_hbm.at[pl.ds(start + k * rows, rows)], buffer.at[k], in_sems.at[k]))
+        outs.append(pltpu.make_async_copy(buffer.at[k], out_hbm.at[here], out_sems.at[k]))
+    for copy in ins:
+        copy.start()
+    for before, after in zip(ins, outs):
+        before.wait()
+        after.start()
+    for copy in outs:
+        copy.wait()
+
+
+def pick(side, s, starts, rows):
+    hbm = pl.BlockSpec(memory_space=pltpu.HBM)
+    return pl.pallas_call(
+        functools.partial(pick_kernel, starts),
+        in_specs=[pl.BlockSpec(memory_space=pltpu.SMEM), hbm],
+        out_specs=hbm,
+        out_shape=jax.ShapeDtypeStruct((rows, s.shape[1]), F32),
+        scratch_shapes=[
+            pltpu.VMEM((4, rows // 4, s.shape[1]), F32),
+            pltpu.SemaphoreType.DMA((4,)),
+            pltpu.SemaphoreType.DMA((4,)),
+        ],
+        compiler_params=params(60),
+        cost_estimate=COST,
+        name="pick",
+    )(side, s)
 
 
 def block_pairs(blocks):
@@ -375,6 +410,23 @@
     )(side, cross, packed, r00, x0, own, *chunks)
 
 
+def stage_kernel(factor_ref, part_ref, factor_out, part_out):
+    factor_out[...] = factor_ref[...]
+    part_out[...] = part_ref[...]
+
+
+def stage(factor, part):
+    return pl.pallas_call(
+        stage_kernel,
+        in_specs=whole(2),
+        out_specs=whole(2),
+        out_shape=[jax.ShapeDtypeStruct(factor.shape, BF16), jax.ShapeDtypeStruct(part.shape, F32)],
+        compiler_params=params(12),
+        cost_estimate=COST,
+        name="stage",
+    )(factor, part)
+
+
 def tail_kernel(start, row, chunk_ref, factor_ref, part_ref, before_hbm, basis_hbm, out, sems):
     copies = []
     for k in range(out.shape[0]):
@@ -485,7 +537,7 @@
         return lax.optimization_barrier((x, after))[0]
 
     once = 1 + jnp.minimum(side, 0)
-    arrived = [swap(lax.dynamic_slice_in_dim(snapshots, side * half * TILE, parts[0] * TILE, 0))]
+    arrived = [swap(pick(side_operand, snapshots, (0, half * TILE), parts[0] * TILE))]
     own, *sends = own_gram(side_operand, snapshots, scale, spans)
     arrived.append(swap(sends[0]))
     first, second = lax.fori_loop(0, once, reduce_own, (own, own))
@@ -498,6 +550,7 @@
     cross = cross_gram(side_operand, snapshots, arrived[2:3], cross, [], early * TILE, scale)
     cross = lax.fori_loop(0, once, reduce_cross, cross)
     factor, share, part, basis = finish(side_operand, cross, second, r00, x00, snapshots, arrived[:4])
+    share, part = stage(share, part)
     begin = half + rests[0]
     basis = tail(arrived[4], share, part, 0, begin * TILE, basis)
     return (basis, factor)

time: 196 us -> 193 us (0.985)
  waiting for transfers between devices: 54.6 us -> 51.4 us
  local copies, waits for them, and re-layouts: 9.49 us -> 7.18 us
  Pallas kernels: 84.1 us -> 86.3 us
    ppermute x2, waiting for transfers between devices: 4.08 us -> 0.86 us  [one_way(): return lax.ppermute(x, 'snap', [(0, 1)])]
    dynamic_slice x1 -> x0, local copies, waits for them, and re-layouts: 2.29 us -> none  [on_device(): lax.dynamic_slice_in_dim(snapshots, side * half * TILE, parts[0] * TILE, 0)]
    pallas_call x0 -> x2, Pallas kernels: none -> 2.25 us  [the longest x1 2.02 us: pick(): pl.pallas_call(functools.partial(pick_kernel, starts), in_specs=[pl.Block...]
  transfers between devices with their start and end apart: 26 -> 26, of which waited for: 20 -> 20; matrix products, arithmetic and copies ran while one was open for 2% -> 2% of each run, Pallas kernels for 42% -> 43%
where the time goes in v4:
time: 193 us; the launch traced here: 192 us
  Pallas kernels  86.3 us (45%)
  waiting for transfers between devices  51.4 us (27%)
  starting transfers between devices  43.2 us (22%)
  local copies, waits for them, and re-layouts  7.18 us (4%)
  other arithmetic  2.89 us (1%)
    ppermute x19, waiting for transfers between devices, flip(): lax.ppermute(x, 'dof', [(i, i ^ order[i % 2][step]) for i in range(count)])  46 us
    pallas_call x1, Pallas kernels, finish(): pl.pallas_call(functools.partial(finish_kernel, counts), out_shape=[jax.S...  38.1 us
    ppermute x19, starting transfers between devices, flip(): lax.ppermute(x, 'dof', [(i, i ^ order[i % 2][step]) for i in range(count)])  25.6 us
    pallas_call x1, Pallas kernels, first_factor(): pl.pallas_call(first_factor_kernel, out_shape=[square, square], in_specs=...  19.6 us
    pallas_call x1, Pallas kernels, own_gram(): pl.pallas_call(functools.partial(own_gram_kernel, scale, spans), grid_spe...  13.3 us
    pallas_call x2, Pallas kernels, cross_gram(): pl.pallas_call(functools.partial(cross_gram_kernel, scale, before is not...  10.5 us
    ppermute x2, starting transfers between devices, flip_side(): return lax.ppermute(x, ('dof', 'snap'), pairs)  7.89 us
    unnamed x11, local copies, waits for them, and re-layouts  7.18 us
  transfers between devices with their start and end apart: 26, of which 20 were waited for; matrix products, arithmetic and copies ran while one was open for 2% of the time, Pallas kernels for 43%

profile of v4, /device:TPU:0, one launch (start us, length us, event | category | flops | bytes accessed | tf_op | source)
XLA Modules:
  0.0 192.2 jit_solution(10568167389640717798)
XLA Ops:
  0.6 2.0 %pick.1 = f32[512,512]{1,0:T(8,128)} custom-call(s32[1]{0:T(128)} %bitcast.side_ref, f32[4096,512]{1,0:T(8,128)} %own_hbm.1), custom_call_target="tpu_custom_call" | custom-call | flops 1 | bytes 1 | tf_op jit(solution)/shard_map/pick/pallas_call | solution.py:65
  2.7 3.0 %collective-permute-start.21 = (f32[512,512]{1,0:T(8,128)}, f32[512,512]{1,0:T(8,128)}, u32[]{:S(2)}, u32[]{:S(2)}) collective-permute-start(f32[512,512]{1,0:T(8,128)} %pick.1), channel_id=1, source_target_pairs={{0,1},{1,0},{2,3},{3,2},{4,5},{5,4},{6,7},{7,6},{8,9},{9,8},{10,11... | collective-permute-start | bytes 3145736 | tf_op jit(solution)/shard_map/ppermute | solution.py:531
  5.7 13.3 %own_gram.1 = (f32[1280,128]{1,0:T(8,128)S(1)}, f32[1024,512]{1,0:T(8,128)}, f32[512,512]{1,0:T(8,128)}, f32[1024,512]{1,0:T(8,128)}, f32[1024,512]{1,0:T(8,128)}) custom-call(s32[1]{0:T(128)} %bitcast.side_ref, f32[4096,512]{1,0:T(8,128)} %own_hbm.1), custom_call_target="tpu_custom_call" | custom-call | flops 1 | bytes 1 | tf_op jit(solution)/shard_map/own_gram/pallas_call | solution.py:125
  19.8 42.8 %while.26 = (s32[]{:T(128)}, f32[1280,128]{1,0:T(8,128)S(1)}, f32[1280,128]{1,0:T(8,128)}, s32[]{:T(128)}, pred[]{:T(512)}, /*index=5*/pred[]{:T(512)}, pred[]{:...) while((s32[]{:T(128)}, f32[1280,128]{1,0:T(8,128)S(1)}, ...), condition=%wide.region_1.2_spmd, body=%wide.region_0.1_spmd.sunk | while | flops 1996802 | bytes 21832332 | solution.py:543
  21.7 2.0 %collective-permute-start.1 = (f32[320,128]{1,0:T(8,128)S(1)}, f32[320,128]{1,0:T(8,128)S(1)}, u32[]{:S(2)}, u32[]{:S(2)}) collective-permute-start(f32[320,128]{1,0:T(8,128)S(1)} %slice_select_fusion.15), channel_id=1, source_target_pairs={{0,8},{2,6},{4,12},{6,2},{8,0},{10,14},{12,4},{14,10},{16,24},{18,... | collective-permute-start | bytes 491528 | tf_op jit(solution)/shard_map/while/body/ppermute | solution.py:461
  23.7 3.4 %collective-permute-done.1 = f32[320,128]{1,0:T(8,128)S(1)} collective-permute-done((f32[320,128]{1,0:T(8,128)S(1)}, f32[320,128]{1,0:T(8,128)S(1)}, u32[]{:S(2)}, u32[]{:S(2)}) %collective-permute-start.1) | collective-permute-done | bytes 163872 | tf_op jit(solution)/shard_map/while/body/ppermute | solution.py:461
  27.1 3.0 %collective-permute-start.2 = (f32[160,128]{1,0:T(8,128)S(1)}, f32[160,128]{1,0:T(8,128)S(1)}, u32[]{:S(2)}, u32[]{:S(2)}) collective-permute-start(f32[160,128]{1,0:T(8,128)S(1)} %slice_select_fusion.16), channel_id=1, source_target_pairs={{0,16},{2,10},{4,20},{6,14},{8,24},{10,2},{12,28},{14,6},{16,0},{1... | collective-permute-start | bytes 245768 | tf_op jit(solution)/shard_map/while/body/ppermute | solution.py:461
  30.1 2.4 %collective-permute-done.2 = f32[160,128]{1,0:T(8,128)S(1)} collective-permute-done((f32[160,128]{1,0:T(8,128)S(1)}, f32[160,128]{1,0:T(8,128)S(1)}, u32[]{:S(2)}, u32[]{:S(2)}) %collective-permute-start.2) | collective-permute-done | bytes 81952 | tf_op jit(solution)/shard_map/while/body/ppermute | solution.py:461
  34.5 2.2 %collective-permute-done.3 = f32[80,128]{1,0:T(8,128)S(1)} collective-permute-done((f32[80,128]{1,0:T(8,128)S(1)}, f32[80,128]{1,0:T(8,128)S(1)}, u32[]{:S(2)}, u32[]{:S(2)}) %collective-permute-start.3) | collective-permute-done | bytes 40992 | tf_op jit(solution)/shard_map/while/body/ppermute | solution.py:461
  36.7 3.0 %collective-permute-start.4 = (f32[80,128]{1,0:T(8,128)S(1)}, f32[80,128]{1,0:T(8,128)S(1)}, u32[]{:S(2)}, u32[]{:S(2)}) collective-permute-start(f32[80,128]{1,0:T(8,128)S(1)} %select_add_fusion.17), channel_id=1, source_target_pairs={{0,5},{1,4},{2,19},{3,18},{4,1},{5,0},{6,23},{7,22},{8,13},{9,12},... | collective-permute-start | bytes 122888 | tf_op jit(solution)/shard_map/while/body/ppermute | solution.py:467
  39.6 2.1 %collective-permute-done.4 = f32[80,128]{1,0:T(8,128)S(1)} collective-permute-done((f32[80,128]{1,0:T(8,128)S(1)}, f32[80,128]{1,0:T(8,128)S(1)}, u32[]{:S(2)}, u32[]{:S(2)}) %collective-permute-start.4) | collective-permute-done | bytes 40992 | tf_op jit(solution)/shard_map/while/body/ppermute | solution.py:467
  45.8 3.1 %collective-permute-start.6 = (f32[160,128]{1,0:T(8,128)S(1)}, f32[160,128]{1,0:T(8,128)S(1)}, u32[]{:S(2)}, u32[]{:S(2)}) collective-permute-start(f32[160,128]{1,0:T(8,128)S(1)} %pad_maximum_fusion.22), channel_id=1, source_target_pairs={{0,16},{2,10},{4,20},{6,14},{8,24},{10,2},{12,28},{14,6},{16,0},{1... | collective-permute-start | bytes 245768 | tf_op jit(solution)/shard_map/while/body/ppermute | solution.py:461
  51.4 2.3 %collective-permute-start.7 = (f32[320,128]{1,0:T(8,128)S(1)}, f32[320,128]{1,0:T(8,128)S(1)}, u32[]{:S(2)}, u32[]{:S(2)}) collective-permute-start(f32[320,128]{1,0:T(8,128)S(1)} %pad_maximum_fusion.23), channel_id=1, source_target_pairs={{0,8},{2,6},{4,12},{6,2},{8,0},{10,14},{12,4},{14,10},{16,24},{18,... | collective-permute-start | bytes 491528 | tf_op jit(solution)/shard_map/while/body/ppermute | solution.py:461
  54.4 2.3 %collective-permute-start.11 = (f32[320,128]{1,0:T(8,128)S(1)}, f32[320,128]{1,0:T(8,128)S(1)}, u32[]{:S(2)}, u32[]{:S(2)}) collective-permute-start(f32[320,128]{1,0:T(8,128)S(1)} %pad_maximum_fusion.27), channel_id=1, source_target_pairs={{0,8},{2,6},{4,12},{6,2},{8,0},{10,14},{12,4},{14,10},{16,24},{18,... | collective-permute-start | bytes 491528 | tf_op jit(solution)/shard_map/while/body/ppermute | solution.py:461
  57.1 2.9 %collective-permute-done.11 = f32[320,128]{1,0:T(8,128)S(1)} collective-permute-done((f32[320,128]{1,0:T(8,128)S(1)}, f32[320,128]{1,0:T(8,128)S(1)}, u32[]{:S(2)}, u32[]{:S(2)}) %collective-permute-start.11) | collective-permute-done | bytes 163872 | tf_op jit(solution)/shard_map/while/body/ppermute | solution.py:461
  64.3 19.6 %first_factor.1 = (f32[512,512]{1,0:T(8,128)S(1)}, f32[512,512]{1,0:T(8,128)S(1)}) custom-call(f32[1280,128]{1,0:T(8,128)S(1)} %get-tuple-element.215.g_ref), custom_call_target="tpu_custom_call" | custom-call | flops 1 | bytes 1 | tf_op jit(solution)/shard_map/first_factor/pallas_call | solution.py:292
  86.0 3.6 %collective-permute-start.25 = (f32[1024,512]{1,0:T(8,128)}, f32[1024,512]{1,0:T(8,128)}, u32[]{:S(2)}, u32[]{:S(2)}) collective-permute-start(f32[1024,512]{1,0:T(8,128)} %get-tuple-element.224), channel_id=1, source_target_pairs={{0,1},{2,3},{4,5},{6,7},{8,9},{10,11},{12,13},{14,15},{16,17},{18,... | collective-permute-start | bytes 6291464 | tf_op jit(solution)/shard_map/ppermute | solution.py:534
  91.0 7.2 %cross_gram.2.refs_1_ = f32[512,512]{1,0:T(8,128)} custom-call(s32[1]{0:T(128)} %bitcast.side_ref, f32[4096,512]{1,0:T(8,128)} %own_hbm.1, f32[512,512]{1,0:T(8,128)} %collective-permute-done.21.refs_0_, f32[1024,512]{1,0:T(8,128)} %copy-done.4, f32[512,512]{1,0:T(8,128)} %copy-done, f32[1280,128]{1,0:T(8,128)} %get-tuple-element.217.refs_3_.g_ref), custom_call_target="tpu_custom_call" | custom-call | flops 1 | bytes 1 | tf_op jit(solution)/shard_map/cross_gram/pallas_call | solution.py:183
  99.6 3.2 %cross_gram.3 = f32[512,512]{1,0:T(8,128)S(1)} custom-call(s32[1]{0:T(128)} %bitcast.side_ref, f32[4096,512]{1,0:T(8,128)} %own_hbm.1, f32[512,512]{1,0:T(8,128)} %collective-permute-done.24.refs_0_.refs_2_, f32[512,512]{1,0:T(8,128)} %cross_gram.2.refs_1_), custom_call_target="tpu_custom_call" | custom-call | flops 1 | bytes 1 | tf_op jit(solution)/shard_map/cross_gram/pallas_call | solution.py:183
  102.9 44.4 %while.27 = (s32[]{:T(128)}, f32[512,512]{1,0:T(8,128)S(1)}, s32[]{:T(128)}, pred[]{:T(512)}, pred[]{:T(512)}, /*index=5*/pred[]{:T(512)}, s32[]{:T(128)}) while((s32[]{:T(128)}, f32[512,512]{1,0:T(8,128)S(1)}, s32[]{:T(128)}, pred[]{:T(512)}, pred[]{:T(512)}, /*index=5*/pred[]{:T(512)}, s32[]{:T(128)}) %tuple.94), condition=%wide.region_3.4_spmd, body=%wide.region_2.3_spmd.sunk | while | flops 1867778 | bytes 22938004 | solution.py:551
  105.1 2.1 %collective-permute-start.14 = (f32[128,512]{1,0:T(8,128)S(1)}, f32[128,512]{1,0:T(8,128)S(1)}, u32[]{:S(2)}, u32[]{:S(2)}) collective-permute-start(f32[128,512]{1,0:T(8,128)S(1)} %slice_select_fusion.19), channel_id=1, source_target_pairs={{0,8},{2,6},{4,12},{6,2},{8,0},{10,14},{12,4},{14,10},{16,24},{18,... | collective-permute-start | bytes 786440 | tf_op jit(solution)/shard_map/while/body/ppermute | solution.py:461
  107.2 4.4 %collective-permute-done.14 = f32[128,512]{1,0:T(8,128)S(1)} collective-permute-done((f32[128,512]{1,0:T(8,128)S(1)}, f32[128,512]{1,0:T(8,128)S(1)}, u32[]{:S(2)}, u32[]{:S(2)}) %collective-permute-start.14) | collective-permute-done | bytes 262176 | tf_op jit(solution)/shard_map/while/body/ppermute | solution.py:461
  111.7 3.0 %collective-permute-start.15 = (f32[64,512]{1,0:T(8,128)S(1)}, f32[64,512]{1,0:T(8,128)S(1)}, u32[]{:S(2)}, u32[]{:S(2)}) collective-permute-start(f32[64,512]{1,0:T(8,128)S(1)} %slice_select_fusion.20), channel_id=1, source_target_pairs={{0,16},{2,10},{4,20},{6,14},{8,24},{10,2},{12,28},{14,6},{16,0},{1... | collective-permute-start | bytes 393224 | tf_op jit(solution)/shard_map/while/body/ppermute | solution.py:461
  114.7 3.0 %collective-permute-done.15 = f32[64,512]{1,0:T(8,128)S(1)} collective-permute-done((f32[64,512]{1,0:T(8,128)S(1)}, f32[64,512]{1,0:T(8,128)S(1)}, u32[]{:S(2)}, u32[]{:S(2)}) %collective-permute-start.15) | collective-permute-done | bytes 131104 | tf_op jit(solution)/shard_map/while/body/ppermute | solution.py:461
  117.7 4.9 %collective-permute-start.16 = (f32[64,512]{1,0:T(8,128)S(1)}, f32[64,512]{1,0:T(8,128)S(1)}, u32[]{:S(2)}, u32[]{:S(2)}) collective-permute-start(f32[64,512]{1,0:T(8,128)S(1)} %select_add_fusion.20), channel_id=1, source_target_pairs={{0,5},{2,19},{4,1},{6,23},{8,13},{10,27},{12,9},{14,31},{16,21},{1... | collective-permute-start | bytes 393224 | tf_op jit(solution)/shard_map/while/body/ppermute | solution.py:467
  122.6 2.5 %collective-permute-done.16 = f32[64,512]{1,0:T(8,128)S(1)} collective-permute-done((f32[64,512]{1,0:T(8,128)S(1)}, f32[64,512]{1,0:T(8,128)S(1)}, u32[]{:S(2)}, u32[]{:S(2)}) %collective-permute-start.16) | collective-permute-done | bytes 131104 | tf_op jit(solution)/shard_map/while/body/ppermute | solution.py:467
  125.7 4.4 %collective-permute-done.17 = f32[64,512]{1,0:T(8,128)S(1)} collective-permute-done((f32[64,512]{1,0:T(8,128)S(1)}, f32[64,512]{1,0:T(8,128)S(1)}, u32[]{:S(2)}, u32[]{:S(2)}) %collective-permute-start.17) | collective-permute-done | bytes 131104 | tf_op jit(solution)/shard_map/while/body/ppermute | solution.py:461
  131.5 6.0 %collective-permute-done.18 = f32[64,512]{1,0:T(8,128)S(1)} collective-permute-done((f32[64,512]{1,0:T(8,128)S(1)}, f32[64,512]{1,0:T(8,128)S(1)}, u32[]{:S(2)}, u32[]{:S(2)}) %collective-permute-start.18) | collective-permute-done | bytes 131104 | tf_op jit(solution)/shard_map/while/body/ppermute | solution.py:461
  137.6 6.4 %collective-permute-done.19 = f32[128,512]{1,0:T(8,128)S(1)} collective-permute-done((f32[128,512]{1,0:T(8,128)S(1)}, f32[128,512]{1,0:T(8,128)S(1)}, u32[]{:S(2)}, u32[]{:S(2)}) %collective-permute-start.19) | collective-permute-done | bytes 262176 | tf_op jit(solution)/shard_map/while/body/ppermute | solution.py:461
  144.9 2.1 %collective-permute-done.20 = f32[256,512]{1,0:T(8,128)S(1)} collective-permute-done((f32[256,512]{1,0:T(8,128)}, f32[256,512]{1,0:T(8,128)S(1)}, u32[]{:S(2)}, u32[]{:S(2)}) %collective-permute-start.20) | collective-permute-done | bytes 524320 | tf_op jit(solution)/shard_map/while/body/ppermute | solution.py:461
  147.2 38.1 %finish.1 = (f32[1024,512]{1,0:T(8,128)}, bf16[1536,512]{1,0:T(8,128)(2,1)}, f32[1024,512]{1,0:T(8,128)}, f32[4096,512]{1,0:T(8,128)}) custom-call(s32[1]{0:T(128)} %bitcast.side_ref, f32[512,512]{1,0:T(8,128)S(1)} %get-tuple-element.221.cross_ref, f32[1280,128]{1,0:T(8,128)} %get-tuple-element.217.refs_3_.g_ref, f32[512,512]{1,0:T(8,128)} %copy-done.3, ...), custom_call_target="tpu_custom_call" | custom-call | flops 1 | bytes 1 | tf_op jit(solution)/shard_map/finish/pallas_call | solution.py:384
  189.4 2.6 %tail.1 = f32[4096,512]{1,0:T(8,128)} custom-call(f32[1024,512]{1,0:T(8,128)S(1)} %collective-permute-done.23.chunk_ref, bf16[1536,512]{1,0:T(8,128)(2,1)S(1)} %get-tuple-element.227.factor_ref, f32[1024,512]{1,0:T(8,128)S(1)} %get-tuple-element.228.part_ref, f32[4096,512]{1,0:T(8,128)} %get-tuple-element.229.before_hbm), custom_call_target="tpu_custom_call", output_to_operand_aliasing={{}: (3, {})} | custom-call | flops 1 | bytes 1 | tf_op jit(solution)/shard_map/tail/pallas_call | solution.py:446
  (80 shorter events, 30.8 us)
Async XLA Ops:
  2.7 86.9 %collective-permute-start.21 = (f32[512,512]{1,0:T(8,128)}, f32[512,512]{1,0:T(8,128)}, u32[]{:S(2)}, u32[]{:S(2)}) collective-permute-start(f32[512,512]{1,0:T(8,128)} %pick.1), channel_id=1, source_target_pairs={{0,1},{1,0},{2,3},{3,2},{4,5},{5,4},{6,7},{7,6},{8,9},{9,8},{10,11... | collective-permute-start | bytes 3145736 | tf_op jit(solution)/shard_map/ppermute | solution.py:531
  19.0 70.6 %collective-permute-start.22 = (f32[1024,512]{1,0:T(8,128)}, f32[1024,512]{1,0:T(8,128)S(1)}, u32[]{:S(2)}, u32[]{:S(2)}) collective-permute-start(f32[1024,512]{1,0:T(8,128)} %get-tuple-element.213), channel_id=1, source_target_pairs={{0,1},{1,0},{2,3},{3,2},{4,5},{5,4},{6,7},{7,6},{8,9},{9,8},{10,11... | collective-permute-start | bytes 6291464 | tf_op jit(solution)/shard_map/ppermute | solution.py:531
  19.9 1.7 collective-permute-start
  21.7 5.4 %collective-permute-start.1 = (f32[320,128]{1,0:T(8,128)S(1)}, f32[320,128]{1,0:T(8,128)S(1)}, u32[]{:S(2)}, u32[]{:S(2)}) collective-permute-start(f32[320,128]{1,0:T(8,128)S(1)} %slice_select_fusion.15), channel_id=1, source_target_pairs={{0,8},{2,6},{4,12},{6,2},{8,0},{10,14},{12,4},{14,10},{16,24},{18,... | collective-permute-start | bytes 491528 | tf_op jit(solution)/shard_map/while/body/ppermute | solution.py:461
  27.1 5.4 %collective-permute-start.2 = (f32[160,128]{1,0:T(8,128)S(1)}, f32[160,128]{1,0:T(8,128)S(1)}, u32[]{:S(2)}, u32[]{:S(2)}) collective-permute-start(f32[160,128]{1,0:T(8,128)S(1)} %slice_select_fusion.16), channel_id=1, source_target_pairs={{0,16},{2,10},{4,20},{6,14},{8,24},{10,2},{12,28},{14,6},{16,0},{1... | collective-permute-start | bytes 245768 | tf_op jit(solution)/shard_map/while/body/ppermute | solution.py:461
  32.6 4.1 %collective-permute-start.3 = (f32[80,128]{1,0:T(8,128)S(1)}, f32[80,128]{1,0:T(8,128)S(1)}, u32[]{:S(2)}, u32[]{:S(2)}) collective-permute-start(f32[80,128]{1,0:T(8,128)S(1)} %slice_select_fusion.17), channel_id=1, source_target_pairs={{0,4},{2,18},{4,0},{6,22},{8,12},{10,26},{12,8},{14,30},{16,20},{1... | collective-permute-start | bytes 122888 | tf_op jit(solution)/shard_map/while/body/ppermute | solution.py:461
  36.7 5.1 %collective-permute-start.4 = (f32[80,128]{1,0:T(8,128)S(1)}, f32[80,128]{1,0:T(8,128)S(1)}, u32[]{:S(2)}, u32[]{:S(2)}) collective-permute-start(f32[80,128]{1,0:T(8,128)S(1)} %select_add_fusion.17), channel_id=1, source_target_pairs={{0,5},{1,4},{2,19},{3,18},{4,1},{5,0},{6,23},{7,22},{8,13},{9,12},... | collective-permute-start | bytes 122888 | tf_op jit(solution)/shard_map/while/body/ppermute | solution.py:467
  41.7 4.1 %collective-permute-start.5 = (f32[80,128]{1,0:T(8,128)S(1)}, f32[80,128]{1,0:T(8,128)S(1)}, u32[]{:S(2)}, u32[]{:S(2)}) collective-permute-start(f32[80,128]{1,0:T(8,128)S(1)} %get-tuple-element.411), channel_id=1, source_target_pairs={{0,4},{2,18},{4,0},{6,22},{8,12},{10,26},{12,8},{14,30},{16,20},{1... | collective-permute-start | bytes 122888 | tf_op jit(solution)/shard_map/while/body/ppermute | solution.py:461
  43.6 5.3 %collective-permute-start.9 = (f32[80,128]{1,0:T(8,128)S(1)}, f32[80,128]{1,0:T(8,128)S(1)}, u32[]{:S(2)}, u32[]{:S(2)}) collective-permute-start(f32[80,128]{1,0:T(8,128)S(1)} %get-tuple-element.420), channel_id=1, source_target_pairs={{0,4},{2,18},{4,0},{6,22},{8,12},{10,26},{12,8},{14,30},{16,20},{1... | collective-permute-start | bytes 122888 | tf_op jit(solution)/shard_map/while/body/ppermute | solution.py:461
  45.8 5.5 %collective-permute-start.6 = (f32[160,128]{1,0:T(8,128)S(1)}, f32[160,128]{1,0:T(8,128)S(1)}, u32[]{:S(2)}, u32[]{:S(2)}) collective-permute-start(f32[160,128]{1,0:T(8,128)S(1)} %pad_maximum_fusion.22), channel_id=1, source_target_pairs={{0,16},{2,10},{4,20},{6,14},{8,24},{10,2},{12,28},{14,6},{16,0},{1... | collective-permute-start | bytes 245768 | tf_op jit(solution)/shard_map/while/body/ppermute | solution.py:461
  48.9 5.4 %collective-permute-start.10 = (f32[160,128]{1,0:T(8,128)S(1)}, f32[160,128]{1,0:T(8,128)S(1)}, u32[]{:S(2)}, u32[]{:S(2)}) collective-permute-start(f32[160,128]{1,0:T(8,128)S(1)} %pad_maximum_fusion.26), channel_id=1, source_target_pairs={{0,16},{2,10},{4,20},{6,14},{8,24},{10,2},{12,28},{14,6},{16,0},{1... | collective-permute-start | bytes 245768 | tf_op jit(solution)/shard_map/while/body/ppermute | solution.py:461
  51.4 5.6 %collective-permute-start.7 = (f32[320,128]{1,0:T(8,128)S(1)}, f32[320,128]{1,0:T(8,128)S(1)}, u32[]{:S(2)}, u32[]{:S(2)}) collective-permute-start(f32[320,128]{1,0:T(8,128)S(1)} %pad_maximum_fusion.23), channel_id=1, source_target_pairs={{0,8},{2,6},{4,12},{6,2},{8,0},{10,14},{12,4},{14,10},{16,24},{18,... | collective-permute-start | bytes 491528 | tf_op jit(solution)/shard_map/while/body/ppermute | solution.py:461
  54.4 5.6 %collective-permute-start.11 = (f32[320,128]{1,0:T(8,128)S(1)}, f32[320,128]{1,0:T(8,128)S(1)}, u32[]{:S(2)}, u32[]{:S(2)}) collective-permute-start(f32[320,128]{1,0:T(8,128)S(1)} %pad_maximum_fusion.27), channel_id=1, source_target_pairs={{0,8},{2,6},{4,12},{6,2},{8,0},{10,14},{12,4},{14,10},{16,24},{18,... | collective-permute-start | bytes 491528 | tf_op jit(solution)/shard_map/while/body/ppermute | solution.py:461
  57.0 3.1 %collective-permute-start.8 = (f32[640,128]{1,0:T(8,128)S(1)}, f32[640,128]{1,0:T(8,128)S(1)}, u32[]{:S(2)}, u32[]{:S(2)}) collective-permute-start(f32[640,128]{1,0:T(8,128)S(1)} %pad_maximum_fusion.24), channel_id=1, source_target_pairs={{0,2},{2,0},{4,6},{6,4},{8,10},{10,8},{12,14},{14,12},{16,18},{18,... | collective-permute-start | bytes 983048 | tf_op jit(solution)/shard_map/while/body/ppermute | solution.py:461
  60.1 1.7 collective-permute-start.12
  62.7 36.9 %collective-permute-start.24 = (f32[512,512]{1,0:T(8,128)}, f32[512,512]{1,0:T(8,128)}, u32[]{:S(2)}, u32[]{:S(2)}) collective-permute-start(f32[512,512]{1,0:T(8,128)} %get-tuple-element.220), channel_id=1, source_target_pairs={{0,1},{1,0},{2,3},{3,2},{4,5},{5,4},{6,7},{7,6},{8,9},{9,8},{10,11... | collective-permute-start | bytes 3145736 | tf_op jit(solution)/shard_map/ppermute | solution.py:531
  84.0 1.0 copy-start
  85.0 1.0 copy-start.3
  86.0 61.3 %collective-permute-start.25 = (f32[1024,512]{1,0:T(8,128)}, f32[1024,512]{1,0:T(8,128)}, u32[]{:S(2)}, u32[]{:S(2)}) collective-permute-start(f32[1024,512]{1,0:T(8,128)} %get-tuple-element.224), channel_id=1, source_target_pairs={{0,1},{2,3},{4,5},{6,7},{8,9},{10,11},{12,13},{14,15},{16,17},{18,... | collective-permute-start | bytes 6291464 | tf_op jit(solution)/shard_map/ppermute | solution.py:534
  89.6 1.4 copy-start.4
  98.2 91.2 %collective-permute-start.23 = (f32[1024,512]{1,0:T(8,128)}, f32[1024,512]{1,0:T(8,128)S(1)}, u32[]{:S(2)}, u32[]{:S(2)}) collective-permute-start(f32[1024,512]{1,0:T(8,128)} %get-tuple-element.218), channel_id=1, source_target_pairs={{0,1},{2,3},{4,5},{6,7},{8,9},{10,11},{12,13},{14,15},{16,17},{18,... | collective-permute-start | bytes 6291464 | tf_op jit(solution)/shard_map/ppermute | solution.py:534
  103.0 2.0 %collective-permute-start.13 = (f32[256,512]{1,0:T(8,128)S(1)}, f32[256,512]{1,0:T(8,128)S(1)}, u32[]{:S(2)}, u32[]{:S(2)}) collective-permute-start(f32[256,512]{1,0:T(8,128)S(1)} %slice_select_fusion.18), channel_id=1, source_target_pairs={{0,2},{2,0},{4,6},{6,4},{8,10},{10,8},{12,14},{14,12},{16,18},{18,... | collective-permute-start | bytes 1572872 | tf_op jit(solution)/shard_map/while/body/ppermute | solution.py:461
  105.1 6.4 %collective-permute-start.14 = (f32[128,512]{1,0:T(8,128)S(1)}, f32[128,512]{1,0:T(8,128)S(1)}, u32[]{:S(2)}, u32[]{:S(2)}) collective-permute-start(f32[128,512]{1,0:T(8,128)S(1)} %slice_select_fusion.19), channel_id=1, source_target_pairs={{0,8},{2,6},{4,12},{6,2},{8,0},{10,14},{12,4},{14,10},{16,24},{18,... | collective-permute-start | bytes 786440 | tf_op jit(solution)/shard_map/while/body/ppermute | solution.py:461
  111.7 6.0 %collective-permute-start.15 = (f32[64,512]{1,0:T(8,128)S(1)}, f32[64,512]{1,0:T(8,128)S(1)}, u32[]{:S(2)}, u32[]{:S(2)}) collective-permute-start(f32[64,512]{1,0:T(8,128)S(1)} %slice_select_fusion.20), channel_id=1, source_target_pairs={{0,16},{2,10},{4,20},{6,14},{8,24},{10,2},{12,28},{14,6},{16,0},{1... | collective-permute-start | bytes 393224 | tf_op jit(solution)/shard_map/while/body/ppermute | solution.py:461
  117.7 7.4 %collective-permute-start.16 = (f32[64,512]{1,0:T(8,128)S(1)}, f32[64,512]{1,0:T(8,128)S(1)}, u32[]{:S(2)}, u32[]{:S(2)}) collective-permute-start(f32[64,512]{1,0:T(8,128)S(1)} %select_add_fusion.20), channel_id=1, source_target_pairs={{0,5},{2,19},{4,1},{6,23},{8,13},{10,27},{12,9},{14,31},{16,21},{1... | collective-permute-start | bytes 393224 | tf_op jit(solution)/shard_map/while/body/ppermute | solution.py:467
  125.1 5.0 %collective-permute-start.17 = (f32[64,512]{1,0:T(8,128)S(1)}, f32[64,512]{1,0:T(8,128)S(1)}, u32[]{:S(2)}, u32[]{:S(2)}) collective-permute-start(f32[64,512]{1,0:T(8,128)S(1)} %add.111), channel_id=1, source_target_pairs={{0,4},{2,18},{4,0},{6,22},{8,12},{10,26},{12,8},{14,30},{16,20},{1... | collective-permute-start | bytes 393224 | tf_op jit(solution)/shard_map/while/body/ppermute | solution.py:461
  130.2 7.3 %collective-permute-start.18 = (f32[64,512]{1,0:T(8,128)S(1)}, f32[64,512]{1,0:T(8,128)S(1)}, u32[]{:S(2)}, u32[]{:S(2)}) collective-permute-start(f32[64,512]{1,0:T(8,128)S(1)} %add.112), channel_id=1, source_target_pairs={{0,16},{2,10},{4,20},{6,14},{8,24},{10,2},{12,28},{14,6},{16,0},{1... | collective-permute-start | bytes 393224 | tf_op jit(solution)/shard_map/while/body/ppermute | solution.py:461
  137.6 6.4 %collective-permute-start.19 = (f32[128,512]{1,0:T(8,128)S(1)}, f32[128,512]{1,0:T(8,128)S(1)}, u32[]{:S(2)}, u32[]{:S(2)}) collective-permute-start(f32[128,512]{1,0:T(8,128)S(1)} %pad_maximum_fusion.30), channel_id=1, source_target_pairs={{0,8},{2,6},{4,12},{6,2},{8,0},{10,14},{12,4},{14,10},{16,24},{18,... | collective-permute-start | bytes 786440 | tf_op jit(solution)/shard_map/while/body/ppermute | solution.py:461
  144.9 2.1 %collective-permute-start.20 = (f32[256,512]{1,0:T(8,128)}, f32[256,512]{1,0:T(8,128)S(1)}, u32[]{:S(2)}, u32[]{:S(2)}) collective-permute-start(f32[256,512]{1,0:T(8,128)} %pad_maximum_fusion.31), channel_id=1, source_target_pairs={{0,2},{2,0},{4,6},{6,4},{8,10},{10,8},{12,14},{14,12},{16,18},{18,... | collective-permute-start | bytes 1572872 | tf_op jit(solution)/shard_map/while/body/ppermute | solution.py:461
  185.3 1.6 copy-start.1
  186.9 1.4 copy-start.2

commit v5 on v4

--- a/solution.py
+++ b/solution.py
@@ -83,14 +83,14 @@
 
 
 def own_gram_kernel(scale, spans, side_ref, s_ref, g_ref, *refs):
-    copies, (high_acc, mixed_acc) = refs[:-2], refs[-2:]
+    copies, (high_acc, low_acc) = refs[:-2], refs[-2:]
     step = pl.program_id(0)
-    half = high_acc.shape[0] // 2
+    order = low_acc.shape[0]
 
     @pl.when(step == 0)
     def _():
         high_acc[...] = jnp.zeros_like(high_acc)
-        mixed_acc[...] = jnp.zeros_like(mixed_acc)
+        low_acc[...] = jnp.zeros_like(low_acc)
 
     block = s_ref[...]
     for copy, (start, shift, count) in zip(copies, spans):
@@ -101,17 +101,15 @@
             copy[...] = block
 
     high, low = split(block)
-    both = jnp.concatenate([high, low])
-    high_acc[:half] += dot(both[:, :half], both, (0, 0))
-    high_acc[half:, half:] += dot(both[:, half:], both[:, half:], (0, 0))
-    mixed_acc[...] += dot(high, low, (0, 0))
+    high_acc[...] += dot(high, jnp.concatenate([high, low], axis=1), (0, 0))
+    low_acc[...] += dot(low, low, (0, 0))
 
     @pl.when(step == pl.num_programs(0) - 1)
     def _():
-        for k, (i, j) in enumerate(block_pairs(high_acc.shape[0] // BLOCK)):
+        for k, (i, j) in enumerate(block_pairs(order // BLOCK)):
             rows, columns = pl.ds(i * BLOCK, BLOCK), pl.ds(j * BLOCK, BLOCK)
-            mixed = mixed_acc[rows, columns] + mixed_acc[columns, rows].T
-            g_ref[pl.ds(k * BLOCK, BLOCK), :] = (high_acc[rows, columns] + mixed) * scale
+            mixed = high_acc[rows, pl.ds(order + j * BLOCK, BLOCK)] + high_acc[columns, pl.ds(order + i * BLOCK, BLOCK)].T
+            g_ref[pl.ds(k * BLOCK, BLOCK), :] = (high_acc[rows, columns] + (mixed + low_acc[rows, columns])) * scale
 
 
 def own_gram(side, s, scale, spans):
@@ -129,7 +127,7 @@
             grid=(rows // TILE,),
             in_specs=[pl.BlockSpec((TILE, width), lambda i, side: (i, 0))],
             out_specs=[pl.BlockSpec(packed, lambda i, side: (0, 0))] + [copy_spec(*span) for span in spans],
-            scratch_shapes=[pltpu.VMEM(square, F32), pltpu.VMEM(square, F32)],
+            scratch_shapes=[pltpu.VMEM((width, 2 * width), F32), pltpu.VMEM(square, F32)],
         ),
         out_shape=[jax.ShapeDtypeStruct(packed, F32)]
         + [jax.ShapeDtypeStruct((count * TILE, width), F32) for _, _, count in spans],
@@ -140,13 +138,13 @@
 
 
 def cross_gram_kernel(scale, resume, counts, side_ref, own_ref, *refs):
-    chunks, before_ref, g_ref = refs[: len(counts)], refs[len(counts)], refs[-1]
+    chunks, before_ref, g_ref, acc = refs[: len(counts)], refs[len(counts)], refs[-2], refs[-1]
     step = pl.program_id(0)
     first = side_ref[0] == 0
 
     @pl.when(step == 0)
     def _():
-        g_ref[...] = before_ref[...] if resume else jnp.zeros_like(g_ref)
+        acc[...] = jnp.zeros_like(acc)
 
     begin = 0
     for chunk, count in zip(chunks, counts):
@@ -158,11 +156,16 @@
             right = jnp.where(first, other, own)
             lh, ll = split(left)
             rh, rl = split(right * scale)
-            left = jnp.concatenate([lh, ll, lh, ll])
-            right = jnp.concatenate([rh, rl, rl, rh])
-            g_ref[...] += dot(left, right, (0, 0))
+            right = jnp.concatenate([rh, rl], axis=1)
+            acc[...] += dot(jnp.concatenate([lh, ll]), jnp.concatenate([right, right]), (0, 0))
 
         begin += count
+
+    @pl.when(step == pl.num_programs(0) - 1)
+    def _():
+        width = g_ref.shape[0]
+        total = acc[:, :width] + acc[:, width:]
+        g_ref[...] = before_ref[...] + total if resume else total
 
 
 def cross_gram(side, own, chunks, before, after, offset, scale):
@@ -187,6 +190,7 @@
             grid=(sum(counts),),
             in_specs=in_specs,
             out_specs=pl.BlockSpec(square, lambda i, side: (0, 0)),
+            scratch_shapes=[pltpu.VMEM((width, 2 * width), F32)],
         ),
         out_shape=jax.ShapeDtypeStruct(square, F32),
         compiler_params=params(60),
@@ -282,23 +286,48 @@
         a_ref[pl.ds(i * BLOCK, BLOCK), pl.ds(j * BLOCK, BLOCK)] = packed_ref[pl.ds(k * BLOCK, BLOCK), :]
 
 
-def first_factor_kernel(g_ref, r_ref, x_ref, a_ref, e_ref):
+def first_factor_kernel(start, g_ref, s_hbm, r_ref, x_ref, *refs):
+    sends, (a_ref, e_ref, buffer, in_sem, out_sems) = refs[:-5], refs[-5:]
+    load = pltpu.make_async_copy(s_hbm.at[pl.ds(start, buffer.shape[0])], buffer, in_sem)
+    load.start()
+    stores, begin = [], 0
+    for k, send in enumerate(sends):
+        here = pl.ds(begin, send.shape[0])
+        stores.append(pltpu.make_async_copy(buffer.at[here], send, out_sems.at[k]))
+        begin += send.shape[0]
+
+    def beside(b, blocks):
+        @pl.when(b == blocks - 2)
+        def _():
+            load.wait()
+            for store in stores:
+                store.start()
+
     unpack(g_ref, a_ref)
-    factor_whole(a_ref, r_ref, x_ref, e_ref)
-
-
-def first_factor(packed, order):
+    factor_whole(a_ref, r_ref, x_ref, e_ref, beside)
+    for store in stores:
+        store.wait()
+
+
+def first_factor(packed, order, own, start, sizes):
     square = jax.ShapeDtypeStruct((order, order), F32)
+    hbm = pl.BlockSpec(memory_space=pltpu.HBM)
     return pl.pallas_call(
-        first_factor_kernel,
-        out_shape=[square, square],
-        in_specs=whole(1),
-        out_specs=whole(2),
-        scratch_shapes=[pltpu.VMEM((order, order), F32), pltpu.VMEM((BLOCK, BLOCK), F32)],
-        compiler_params=params(40),
+        functools.partial(first_factor_kernel, start),
+        out_shape=[square, square] + [jax.ShapeDtypeStruct((size, order), F32) for size in sizes],
+        in_specs=whole(1) + [hbm],
+        out_specs=whole(2) + [hbm] * len(sizes),
+        scratch_shapes=[
+            pltpu.VMEM((order, order), F32),
+            pltpu.VMEM((BLOCK, BLOCK), F32),
+            pltpu.VMEM((sum(sizes), order), F32),
+            pltpu.SemaphoreType.DMA,
+            pltpu.SemaphoreType.DMA((len(sizes),)),
+        ],
+        compiler_params=params(60),
         cost_estimate=COST,
         name="first_factor",
-    )(packed)
+    )(packed, own)
 
 
 def thrice(x):
@@ -320,8 +349,9 @@
 
 def finish_kernel(counts, side_ref, cross_ref, g_ref, r00_ref, x0_ref, own_hbm, *refs):
     chunks, refs = refs[: len(counts)], refs[len(counts) :]
-    f_ref, factor_ref, part_ref, basis_hbm = refs[:4]
-    own, other, u_ref, left_ref, right_ref, a_ref, r_ref, x_ref, e_ref, load_sems, store_sems = refs[4:]
+    f_hbm, share_hbm, part_hbm, basis_hbm = refs[:4]
+    own, other, f_ref, share, u_ref, left_ref, right_ref, a_ref, r_ref, x_ref, e_ref = refs[4:15]
+    load_sems, store_sems, out_sems = refs[15:]
     order = a_ref.shape[0]
     half = order // 2
     rows, known = own.shape[0], sum(counts)
@@ -333,6 +363,11 @@
         begin += count
     for load in loads:
         load.start()
+    outs = [
+        pltpu.make_async_copy(f_ref.at[pl.ds(0, order)], f_hbm.at[pl.ds(0, order)], out_sems.at[0]),
+        pltpu.make_async_copy(f_ref.at[pl.ds(order, order)], f_hbm.at[pl.ds(order, order)], out_sems.at[1]),
+        pltpu.make_async_copy(share, share_hbm, out_sems.at[2]),
+    ]
     x0 = x0_ref[...]
     r01 = dot(x0, cross_ref[...], (1, 0), HIGHEST)
     u = dot3(x0, r01, (0, 0))
@@ -340,6 +375,7 @@
     unpack(g_ref, a_ref)
     a_ref[...] -= dot(r01, r01, (0, 0), HIGHEST)
     f_ref[:order] = jnp.where(first, r00_ref[...], r01)
+    outs[0].start()
     for load in loads:
         load.wait()
 
@@ -351,7 +387,11 @@
             own[here] -= dot(thrice(other[here]), u_ref[...], (1, 0))
 
     factor_whole(a_ref, r_ref, x_ref, e_ref, project)
+    f_ref[order:] = jnp.where(first, 0.0, r_ref[...])
+    outs[1].start()
     x1 = x_ref[...]
+    share[...] = stacked(jnp.where(first, 0.0, -dot3(u, x1, (1, 1))))
+    outs[2].start()
     w = jnp.where(first, x0, x1).T
     left_ref[...] = stacked(w[:half, :half])
     right_ref[...] = stacked(w[:, half:])
@@ -366,13 +406,19 @@
         store(k).start()
         return carry
 
+    parts = []
+    for k in range(known, rows, TILE):
+        here = pl.ds(k, TILE)
+        own[here] = times_upper(own[here], left_ref[...], right_ref[...])
+        parts.append(pltpu.make_async_copy(own.at[here], part_hbm.at[pl.ds(k - known, TILE)], store_sems.at[k // TILE]))
+        parts[-1].start()
     lax.fori_loop(0, known // TILE, body, 0)
-    for k in range(known, rows, TILE):
-        part_ref[k - known : k - known + TILE] = times_upper(own[k : k + TILE], left_ref[...], right_ref[...])
-    f_ref[order:] = jnp.where(first, 0.0, r_ref[...])
-    factor_ref[...] = stacked(jnp.where(first, 0.0, -dot3(u, x1, (1, 1))))
+    for part in parts:
+        part.wait()
     for k in range(known // TILE):
         store(k).wait()
+    for out in outs:
+        out.wait()
 
 
 def finish(side, cross, packed, r00, x0, own, chunks):
@@ -390,10 +436,12 @@
             jax.ShapeDtypeStruct(own.shape, F32),
         ],
         in_specs=[pl.BlockSpec(memory_space=pltpu.SMEM)] + whole(4) + [anywhere] * (1 + len(chunks)),
-        out_specs=whole(3) + [anywhere],
+        out_specs=[anywhere] * 4,
         scratch_shapes=[
             pltpu.VMEM(own.shape, F32),
             pltpu.VMEM((sum(counts), order), F32),
+            pltpu.VMEM((2 * order, order), F32),
+            pltpu.VMEM((3 * order, order), BF16),
             pltpu.VMEM((3 * order, order), BF16),
             pltpu.VMEM((3 * half, half), BF16),
             pltpu.VMEM((3 * order, half), BF16),
@@ -402,7 +450,8 @@
             pltpu.VMEM(square, F32),
             pltpu.VMEM((BLOCK, BLOCK), F32),
             pltpu.SemaphoreType.DMA((len(chunks) + 1,)),
-            pltpu.SemaphoreType.DMA((sum(counts) // TILE,)),
+            pltpu.SemaphoreType.DMA((own.shape[0] // TILE,)),
+            pltpu.SemaphoreType.DMA((3,)),
         ],
         compiler_params=params(60),
         cost_estimate=COST,
@@ -523,9 +572,9 @@
 
     half = rows // 2 // TILE
     parts = [half // 4, half // 2, half - half // 4 - half // 2]
-    rests = [half // 2, half - half // 2]
     spans = [(parts[0], half, parts[1]), (parts[0] + parts[1], half, parts[2])]
-    spans += [(half + sum(rests[:i]), 0, rests[i]) for i in range(2)]
+    middle = rows // 2
+    rests = [middle // 2, middle // 2]
 
     def swap(x):
         return lax.ppermute(x, "snap", [(0, 1), (1, 0)])
@@ -542,17 +591,16 @@
     arrived.append(swap(sends[0]))
     first, second = lax.fori_loop(0, once, reduce_own, (own, own))
     arrived.append(swap(late(sends[1], first)))
-    r00, x00 = first_factor(first, width)
-    arrived.append(one_way(late(sends[2], r00)))
+    r00, x00, *rest = first_factor(first, width, snapshots, middle, rests)
+    arrived.append(one_way(rest[0]))
     early = parts[0] + parts[1]
     cross = cross_gram(side_operand, snapshots, arrived[:2], None, [x00, second], 0, scale)
-    arrived.append(one_way(late(sends[3], cross)))
+    arrived.append(one_way(late(rest[1], cross)))
     cross = cross_gram(side_operand, snapshots, arrived[2:3], cross, [], early * TILE, scale)
     cross = lax.fori_loop(0, once, reduce_cross, cross)
     factor, share, part, basis = finish(side_operand, cross, second, r00, x00, snapshots, arrived[:4])
     share, part = stage(share, part)
-    begin = half + rests[0]
-    basis = tail(arrived[4], share, part, 0, begin * TILE, basis)
+    basis = tail(arrived[4], share, part, 0, middle + rests[0], basis)
     return (basis, factor)
 
 

time: 193 us -> 193 us (level)
  local copies, waits for them, and re-layouts: 7.18 us -> 5.19 us
    unnamed x11 -> x9, local copies, waits for them, and re-layouts: 7.18 us -> 5.19 us
  transfers between devices with their start and end apart: 26 -> 26, of which waited for: 20 -> 20; matrix products, arithmetic and copies ran while one was open for 2% -> 2% of each run, Pallas kernels for 43% -> 42%
where the time goes in v5:
time: 193 us; the launch traced here: 192 us
  Pallas kernels  85.9 us (45%)
  waiting for transfers between devices  53 us (27%)
  starting transfers between devices  44 us (23%)
  local copies, waits for them, and re-layouts  5.19 us (3%)
  other arithmetic  2.89 us (1%)
    ppermute x19, waiting for transfers between devices, flip(): lax.ppermute(x, 'dof', [(i, i ^ order[i % 2][step]) for i in range(count)])  45.8 us
    pallas_call x1, Pallas kernels, finish(): pl.pallas_call(functools.partial(finish_kernel, counts), out_shape=[jax.S...  36.5 us
    ppermute x19, starting transfers between devices, flip(): lax.ppermute(x, 'dof', [(i, i ^ order[i % 2][step]) for i in range(count)])  25.8 us
    pallas_call x1, Pallas kernels, first_factor(): pl.pallas_call(functools.partial(first_factor_kernel, start), out_shape=[...  21.1 us
    pallas_call x1, Pallas kernels, own_gram(): pl.pallas_call(functools.partial(own_gram_kernel, scale, spans), grid_spe...  12.8 us
    pallas_call x2, Pallas kernels, cross_gram(): pl.pallas_call(functools.partial(cross_gram_kernel, scale, before is not...  10.6 us
    ppermute x2, starting transfers between devices, flip_side(): return lax.ppermute(x, ('dof', 'snap'), pairs)  8.42 us
    ppermute x2, starting transfers between devices, one_way(): return lax.ppermute(x, 'snap', [(0, 1)])  5.2 us
  transfers between devices with their start and end apart: 26, of which 20 were waited for; matrix products, arithmetic and copies ran while one was open for 2% of the time, Pallas kernels for 42%

profile of v5, /device:TPU:0, one launch (start us, length us, event | category | flops | bytes accessed | tf_op | source)
XLA Modules:
  0.0 192.2 jit_solution(12932359681425615076)
XLA Ops:
  2.7 3.0 %collective-permute-start.21 = (f32[512,512]{1,0:T(8,128)}, f32[512,512]{1,0:T(8,128)}, u32[]{:S(2)}, u32[]{:S(2)}) collective-permute-start(f32[512,512]{1,0:T(8,128)} %pick.1), channel_id=1, source_target_pairs={{0,1},{1,0},{2,3},{3,2},{4,5},{5,4},{6,7},{7,6},{8,9},{9,8},{10,11... | collective-permute-start | bytes 3145736 | tf_op jit(solution)/shard_map/ppermute | solution.py:580
  5.7 12.8 %own_gram.1 = (f32[1280,128]{1,0:T(8,128)S(1)}, f32[1024,512]{1,0:T(8,128)}, f32[512,512]{1,0:T(8,128)}) custom-call(s32[1]{0:T(128)} %bitcast.side_ref, f32[4096,512]{1,0:T(8,128)} %own_hbm.1), custom_call_target="tpu_custom_call" | custom-call | flops 1 | bytes 1 | tf_op jit(solution)/shard_map/own_gram/pallas_call | solution.py:123
  19.4 42.9 %while.26 = (s32[]{:T(128)}, f32[1280,128]{1,0:T(8,128)S(1)}, f32[1280,128]{1,0:T(8,128)}, s32[]{:T(128)}, pred[]{:T(512)}, /*index=5*/pred[]{:T(512)}, pred[]{:...) while((s32[]{:T(128)}, f32[1280,128]{1,0:T(8,128)S(1)}, ...), condition=%wide.region_1.2_spmd, body=%wide.region_0.1_spmd.sunk | while | flops 1996802 | bytes 21832332 | solution.py:592
  21.2 2.1 %collective-permute-start.1 = (f32[320,128]{1,0:T(8,128)S(1)}, f32[320,128]{1,0:T(8,128)S(1)}, u32[]{:S(2)}, u32[]{:S(2)}) collective-permute-start(f32[320,128]{1,0:T(8,128)S(1)} %slice_select_fusion.15), channel_id=1, source_target_pairs={{0,8},{2,6},{4,12},{6,2},{8,0},{10,14},{12,4},{14,10},{16,24},{18,... | collective-permute-start | bytes 491528 | tf_op jit(solution)/shard_map/while/body/ppermute | solution.py:510
  23.3 3.3 %collective-permute-done.1 = f32[320,128]{1,0:T(8,128)S(1)} collective-permute-done((f32[320,128]{1,0:T(8,128)S(1)}, f32[320,128]{1,0:T(8,128)S(1)}, u32[]{:S(2)}, u32[]{:S(2)}) %collective-permute-start.1) | collective-permute-done | bytes 163872 | tf_op jit(solution)/shard_map/while/body/ppermute | solution.py:510
  26.6 3.1 %collective-permute-start.2 = (f32[160,128]{1,0:T(8,128)S(1)}, f32[160,128]{1,0:T(8,128)S(1)}, u32[]{:S(2)}, u32[]{:S(2)}) collective-permute-start(f32[160,128]{1,0:T(8,128)S(1)} %slice_select_fusion.16), channel_id=1, source_target_pairs={{0,16},{2,10},{4,20},{6,14},{8,24},{10,2},{12,28},{14,6},{16,0},{1... | collective-permute-start | bytes 245768 | tf_op jit(solution)/shard_map/while/body/ppermute | solution.py:510
  29.7 2.4 %collective-permute-done.2 = f32[160,128]{1,0:T(8,128)S(1)} collective-permute-done((f32[160,128]{1,0:T(8,128)S(1)}, f32[160,128]{1,0:T(8,128)S(1)}, u32[]{:S(2)}, u32[]{:S(2)}) %collective-permute-start.2) | collective-permute-done | bytes 81952 | tf_op jit(solution)/shard_map/while/body/ppermute | solution.py:510
  34.1 2.2 %collective-permute-done.3 = f32[80,128]{1,0:T(8,128)S(1)} collective-permute-done((f32[80,128]{1,0:T(8,128)S(1)}, f32[80,128]{1,0:T(8,128)S(1)}, u32[]{:S(2)}, u32[]{:S(2)}) %collective-permute-start.3) | collective-permute-done | bytes 40992 | tf_op jit(solution)/shard_map/while/body/ppermute | solution.py:510
  36.3 2.8 %collective-permute-start.4 = (f32[80,128]{1,0:T(8,128)S(1)}, f32[80,128]{1,0:T(8,128)S(1)}, u32[]{:S(2)}, u32[]{:S(2)}) collective-permute-start(f32[80,128]{1,0:T(8,128)S(1)} %select_add_fusion.17), channel_id=1, source_target_pairs={{0,5},{1,4},{2,19},{3,18},{4,1},{5,0},{6,23},{7,22},{8,13},{9,12},... | collective-permute-start | bytes 122888 | tf_op jit(solution)/shard_map/while/body/ppermute | solution.py:516
  39.1 2.3 %collective-permute-done.4 = f32[80,128]{1,0:T(8,128)S(1)} collective-permute-done((f32[80,128]{1,0:T(8,128)S(1)}, f32[80,128]{1,0:T(8,128)S(1)}, u32[]{:S(2)}, u32[]{:S(2)}) %collective-permute-start.4) | collective-permute-done | bytes 40992 | tf_op jit(solution)/shard_map/while/body/ppermute | solution.py:516
  45.5 3.1 %collective-permute-start.6 = (f32[160,128]{1,0:T(8,128)S(1)}, f32[160,128]{1,0:T(8,128)S(1)}, u32[]{:S(2)}, u32[]{:S(2)}) collective-permute-start(f32[160,128]{1,0:T(8,128)S(1)} %pad_maximum_fusion.22), channel_id=1, source_target_pairs={{0,16},{2,10},{4,20},{6,14},{8,24},{10,2},{12,28},{14,6},{16,0},{1... | collective-permute-start | bytes 245768 | tf_op jit(solution)/shard_map/while/body/ppermute | solution.py:510
  51.0 2.3 %collective-permute-start.7 = (f32[320,128]{1,0:T(8,128)S(1)}, f32[320,128]{1,0:T(8,128)S(1)}, u32[]{:S(2)}, u32[]{:S(2)}) collective-permute-start(f32[320,128]{1,0:T(8,128)S(1)} %pad_maximum_fusion.23), channel_id=1, source_target_pairs={{0,8},{2,6},{4,12},{6,2},{8,0},{10,14},{12,4},{14,10},{16,24},{18,... | collective-permute-start | bytes 491528 | tf_op jit(solution)/shard_map/while/body/ppermute | solution.py:510
  54.0 2.3 %collective-permute-start.11 = (f32[320,128]{1,0:T(8,128)S(1)}, f32[320,128]{1,0:T(8,128)S(1)}, u32[]{:S(2)}, u32[]{:S(2)}) collective-permute-start(f32[320,128]{1,0:T(8,128)S(1)} %pad_maximum_fusion.27), channel_id=1, source_target_pairs={{0,8},{2,6},{4,12},{6,2},{8,0},{10,14},{12,4},{14,10},{16,24},{18,... | collective-permute-start | bytes 491528 | tf_op jit(solution)/shard_map/while/body/ppermute | solution.py:510
  56.7 2.9 %collective-permute-done.11 = f32[320,128]{1,0:T(8,128)S(1)} collective-permute-done((f32[320,128]{1,0:T(8,128)S(1)}, f32[320,128]{1,0:T(8,128)S(1)}, u32[]{:S(2)}, u32[]{:S(2)}) %collective-permute-start.11) | collective-permute-done | bytes 163872 | tf_op jit(solution)/shard_map/while/body/ppermute | solution.py:510
  63.8 21.1 %first_factor.1 = (f32[512,512]{1,0:T(8,128)}, f32[512,512]{1,0:T(8,128)}, f32[1024,512]{1,0:T(8,128)}, f32[1024,512]{1,0:T(8,128)}) custom-call(f32[1280,128]{1,0:T(8,128)S(1)} %get-tuple-element.212.g_ref, f32[4096,512]{1,0:T(8,128)} %own_hbm.1), custom_call_target="tpu_custom_call" | custom-call | flops 1 | bytes 1 | tf_op jit(solution)/shard_map/first_factor/pallas_call | solution.py:315
  84.9 3.8 %collective-permute-start.25 = (f32[1024,512]{1,0:T(8,128)}, f32[1024,512]{1,0:T(8,128)}, u32[]{:S(2)}, u32[]{:S(2)}) collective-permute-start(f32[1024,512]{1,0:T(8,128)} %get-tuple-element.222), channel_id=1, source_target_pairs={{0,1},{2,3},{4,5},{6,7},{8,9},{10,11},{12,13},{14,15},{16,17},{18,... | collective-permute-start | bytes 6291464 | tf_op jit(solution)/shard_map/ppermute | solution.py:583
  90.1 7.4 %cross_gram.2.refs_1_ = f32[512,512]{1,0:T(8,128)} custom-call(s32[1]{0:T(128)} %bitcast.side_ref, f32[4096,512]{1,0:T(8,128)} %own_hbm.1, f32[512,512]{1,0:T(8,128)} %collective-permute-done.21.refs_0_, f32[1024,512]{1,0:T(8,128)} %copy-done.2, f32[512,512]{1,0:T(8,128)} %get-tuple-element.215.refs_2_.x0_ref, f32[1280,128]{1,0:T(8,128)S(1)} %copy-done.3), custom_call_target="tpu_custom_call" | custom-call | flops 1 | bytes 1 | tf_op jit(solution)/shard_map/cross_gram/pallas_call | solution.py:186
  98.9 3.2 %cross_gram.3 = f32[512,512]{1,0:T(8,128)S(1)} custom-call(s32[1]{0:T(128)} %bitcast.side_ref, f32[4096,512]{1,0:T(8,128)} %own_hbm.1, f32[512,512]{1,0:T(8,128)} %collective-permute-done.24.refs_0_.refs_2_, f32[512,512]{1,0:T(8,128)} %cross_gram.2.refs_1_), custom_call_target="tpu_custom_call" | custom-call | flops 1 | bytes 1 | tf_op jit(solution)/shard_map/cross_gram/pallas_call | solution.py:186
  102.1 45.1 %while.27 = (s32[]{:T(128)}, f32[512,512]{1,0:T(8,128)S(1)}, s32[]{:T(128)}, pred[]{:T(512)}, pred[]{:T(512)}, /*index=5*/pred[]{:T(512)}, s32[]{:T(128)}) while((s32[]{:T(128)}, f32[512,512]{1,0:T(8,128)S(1)}, s32[]{:T(128)}, pred[]{:T(512)}, pred[]{:T(512)}, /*index=5*/pred[]{:T(512)}, s32[]{:T(128)}) %tuple.92), condition=%wide.region_3.4_spmd, body=%wide.region_2.3_spmd.sunk | while | flops 1867778 | bytes 22938004 | solution.py:600
  104.4 2.1 %collective-permute-start.14 = (f32[128,512]{1,0:T(8,128)S(1)}, f32[128,512]{1,0:T(8,128)S(1)}, u32[]{:S(2)}, u32[]{:S(2)}) collective-permute-start(f32[128,512]{1,0:T(8,128)S(1)} %slice_select_fusion.19), channel_id=1, source_target_pairs={{0,8},{2,6},{4,12},{6,2},{8,0},{10,14},{12,4},{14,10},{16,24},{18,... | collective-permute-start | bytes 786440 | tf_op jit(solution)/shard_map/while/body/ppermute | solution.py:510
  106.5 4.4 %collective-permute-done.14 = f32[128,512]{1,0:T(8,128)S(1)} collective-permute-done((f32[128,512]{1,0:T(8,128)S(1)}, f32[128,512]{1,0:T(8,128)S(1)}, u32[]{:S(2)}, u32[]{:S(2)}) %collective-permute-start.14) | collective-permute-done | bytes 262176 | tf_op jit(solution)/shard_map/while/body/ppermute | solution.py:510
  110.9 3.0 %collective-permute-start.15 = (f32[64,512]{1,0:T(8,128)S(1)}, f32[64,512]{1,0:T(8,128)S(1)}, u32[]{:S(2)}, u32[]{:S(2)}) collective-permute-start(f32[64,512]{1,0:T(8,128)S(1)} %slice_select_fusion.20), channel_id=1, source_target_pairs={{0,16},{2,10},{4,20},{6,14},{8,24},{10,2},{12,28},{14,6},{16,0},{1... | collective-permute-start | bytes 393224 | tf_op jit(solution)/shard_map/while/body/ppermute | solution.py:510
  114.0 3.0 %collective-permute-done.15 = f32[64,512]{1,0:T(8,128)S(1)} collective-permute-done((f32[64,512]{1,0:T(8,128)S(1)}, f32[64,512]{1,0:T(8,128)S(1)}, u32[]{:S(2)}, u32[]{:S(2)}) %collective-permute-start.15) | collective-permute-done | bytes 131104 | tf_op jit(solution)/shard_map/while/body/ppermute | solution.py:510
  117.0 5.6 %collective-permute-start.16 = (f32[64,512]{1,0:T(8,128)S(1)}, f32[64,512]{1,0:T(8,128)S(1)}, u32[]{:S(2)}, u32[]{:S(2)}) collective-permute-start(f32[64,512]{1,0:T(8,128)S(1)} %select_add_fusion.20), channel_id=1, source_target_pairs={{0,5},{2,19},{4,1},{6,23},{8,13},{10,27},{12,9},{14,31},{16,21},{1... | collective-permute-start | bytes 393224 | tf_op jit(solution)/shard_map/while/body/ppermute | solution.py:516
  122.6 2.5 %collective-permute-done.16 = f32[64,512]{1,0:T(8,128)S(1)} collective-permute-done((f32[64,512]{1,0:T(8,128)S(1)}, f32[64,512]{1,0:T(8,128)S(1)}, u32[]{:S(2)}, u32[]{:S(2)}) %collective-permute-start.16) | collective-permute-done | bytes 131104 | tf_op jit(solution)/shard_map/while/body/ppermute | solution.py:516
  125.7 4.4 %collective-permute-done.17 = f32[64,512]{1,0:T(8,128)S(1)} collective-permute-done((f32[64,512]{1,0:T(8,128)S(1)}, f32[64,512]{1,0:T(8,128)S(1)}, u32[]{:S(2)}, u32[]{:S(2)}) %collective-permute-start.17) | collective-permute-done | bytes 131104 | tf_op jit(solution)/shard_map/while/body/ppermute | solution.py:510
  131.5 6.0 %collective-permute-done.18 = f32[64,512]{1,0:T(8,128)S(1)} collective-permute-done((f32[64,512]{1,0:T(8,128)S(1)}, f32[64,512]{1,0:T(8,128)S(1)}, u32[]{:S(2)}, u32[]{:S(2)}) %collective-permute-start.18) | collective-permute-done | bytes 131104 | tf_op jit(solution)/shard_map/while/body/ppermute | solution.py:510
  137.6 6.4 %collective-permute-done.19 = f32[128,512]{1,0:T(8,128)S(1)} collective-permute-done((f32[128,512]{1,0:T(8,128)S(1)}, f32[128,512]{1,0:T(8,128)S(1)}, u32[]{:S(2)}, u32[]{:S(2)}) %collective-permute-start.19) | collective-permute-done | bytes 262176 | tf_op jit(solution)/shard_map/while/body/ppermute | solution.py:510
  144.9 2.1 %collective-permute-done.20 = f32[256,512]{1,0:T(8,128)S(1)} collective-permute-done((f32[256,512]{1,0:T(8,128)}, f32[256,512]{1,0:T(8,128)S(1)}, u32[]{:S(2)}, u32[]{:S(2)}) %collective-permute-start.20) | collective-permute-done | bytes 524320 | tf_op jit(solution)/shard_map/while/body/ppermute | solution.py:510
  147.2 36.5 %finish.1 = (f32[1024,512]{1,0:T(8,128)}, bf16[1536,512]{1,0:T(8,128)(2,1)}, f32[1024,512]{1,0:T(8,128)}, f32[4096,512]{1,0:T(8,128)}) custom-call(s32[1]{0:T(128)} %bitcast.side_ref, f32[512,512]{1,0:T(8,128)S(1)} %get-tuple-element.220.cross_ref, f32[1280,128]{1,0:T(8,128)} %get-tuple-element.216.refs_3_.g_ref, f32[512,512]{1,0:T(8,128)} %get-tuple-element.221.r00_ref, ...), custom_call_target="tpu_custom_call" | custom-call | flops 1 | bytes 1 | tf_op jit(solution)/shard_map/finish/pallas_call | solution.py:430
  187.0 2.4 %collective-permute-done.23.chunk_ref = f32[1024,512]{1,0:T(8,128)S(1)} collective-permute-done((f32[1024,512]{1,0:T(8,128)}, f32[1024,512]{1,0:T(8,128)S(1)}, u32[]{:S(2)}, u32[]{:S(2)}) %collective-permute-start.23) | collective-permute-done | bytes 2097184 | tf_op jit(solution)/shard_map/ppermute | solution.py:583
  189.4 2.6 %tail.1 = f32[4096,512]{1,0:T(8,128)} custom-call(f32[1024,512]{1,0:T(8,128)S(1)} %collective-permute-done.23.chunk_ref, bf16[1536,512]{1,0:T(8,128)(2,1)S(1)} %get-tuple-element.225.factor_ref, f32[1024,512]{1,0:T(8,128)S(1)} %get-tuple-element.226.part_ref, f32[4096,512]{1,0:T(8,128)} %get-tuple-element.227.before_hbm), custom_call_target="tpu_custom_call", output_to_operand_aliasing={{}: (3, {})} | custom-call | flops 1 | bytes 1 | tf_op jit(solution)/shard_map/tail/pallas_call | solution.py:495
  (78 shorter events, 29.9 us)
Async XLA Ops:
  2.7 86.0 %collective-permute-start.21 = (f32[512,512]{1,0:T(8,128)}, f32[512,512]{1,0:T(8,128)}, u32[]{:S(2)}, u32[]{:S(2)}) collective-permute-start(f32[512,512]{1,0:T(8,128)} %pick.1), channel_id=1, source_target_pairs={{0,1},{1,0},{2,3},{3,2},{4,5},{5,4},{6,7},{7,6},{8,9},{9,8},{10,11... | collective-permute-start | bytes 3145736 | tf_op jit(solution)/shard_map/ppermute | solution.py:580
  18.5 70.2 %collective-permute-start.22 = (f32[1024,512]{1,0:T(8,128)}, f32[1024,512]{1,0:T(8,128)S(1)}, u32[]{:S(2)}, u32[]{:S(2)}) collective-permute-start(f32[1024,512]{1,0:T(8,128)} %get-tuple-element.214), channel_id=1, source_target_pairs={{0,1},{1,0},{2,3},{3,2},{4,5},{5,4},{6,7},{7,6},{8,9},{9,8},{10,11... | collective-permute-start | bytes 6291464 | tf_op jit(solution)/shard_map/ppermute | solution.py:580
  19.4 1.7 collective-permute-start
  21.2 5.4 %collective-permute-start.1 = (f32[320,128]{1,0:T(8,128)S(1)}, f32[320,128]{1,0:T(8,128)S(1)}, u32[]{:S(2)}, u32[]{:S(2)}) collective-permute-start(f32[320,128]{1,0:T(8,128)S(1)} %slice_select_fusion.15), channel_id=1, source_target_pairs={{0,8},{2,6},{4,12},{6,2},{8,0},{10,14},{12,4},{14,10},{16,24},{18,... | collective-permute-start | bytes 491528 | tf_op jit(solution)/shard_map/while/body/ppermute | solution.py:510
  26.6 5.5 %collective-permute-start.2 = (f32[160,128]{1,0:T(8,128)S(1)}, f32[160,128]{1,0:T(8,128)S(1)}, u32[]{:S(2)}, u32[]{:S(2)}) collective-permute-start(f32[160,128]{1,0:T(8,128)S(1)} %slice_select_fusion.16), channel_id=1, source_target_pairs={{0,16},{2,10},{4,20},{6,14},{8,24},{10,2},{12,28},{14,6},{16,0},{1... | collective-permute-start | bytes 245768 | tf_op jit(solution)/shard_map/while/body/ppermute | solution.py:510
  32.2 4.1 %collective-permute-start.3 = (f32[80,128]{1,0:T(8,128)S(1)}, f32[80,128]{1,0:T(8,128)S(1)}, u32[]{:S(2)}, u32[]{:S(2)}) collective-permute-start(f32[80,128]{1,0:T(8,128)S(1)} %slice_select_fusion.17), channel_id=1, source_target_pairs={{0,4},{2,18},{4,0},{6,22},{8,12},{10,26},{12,8},{14,30},{16,20},{1... | collective-permute-start | bytes 122888 | tf_op jit(solution)/shard_map/while/body/ppermute | solution.py:510
  36.3 5.1 %collective-permute-start.4 = (f32[80,128]{1,0:T(8,128)S(1)}, f32[80,128]{1,0:T(8,128)S(1)}, u32[]{:S(2)}, u32[]{:S(2)}) collective-permute-start(f32[80,128]{1,0:T(8,128)S(1)} %select_add_fusion.17), channel_id=1, source_target_pairs={{0,5},{1,4},{2,19},{3,18},{4,1},{5,0},{6,23},{7,22},{8,13},{9,12},... | collective-permute-start | bytes 122888 | tf_op jit(solution)/shard_map/while/body/ppermute | solution.py:516
  41.4 4.1 %collective-permute-start.5 = (f32[80,128]{1,0:T(8,128)S(1)}, f32[80,128]{1,0:T(8,128)S(1)}, u32[]{:S(2)}, u32[]{:S(2)}) collective-permute-start(f32[80,128]{1,0:T(8,128)S(1)} %get-tuple-element.409), channel_id=1, source_target_pairs={{0,4},{2,18},{4,0},{6,22},{8,12},{10,26},{12,8},{14,30},{16,20},{1... | collective-permute-start | bytes 122888 | tf_op jit(solution)/shard_map/while/body/ppermute | solution.py:510
  43.2 5.3 %collective-permute-start.9 = (f32[80,128]{1,0:T(8,128)S(1)}, f32[80,128]{1,0:T(8,128)S(1)}, u32[]{:S(2)}, u32[]{:S(2)}) collective-permute-start(f32[80,128]{1,0:T(8,128)S(1)} %get-tuple-element.418), channel_id=1, source_target_pairs={{0,4},{2,18},{4,0},{6,22},{8,12},{10,26},{12,8},{14,30},{16,20},{1... | collective-permute-start | bytes 122888 | tf_op jit(solution)/shard_map/while/body/ppermute | solution.py:510
  45.5 5.5 %collective-permute-start.6 = (f32[160,128]{1,0:T(8,128)S(1)}, f32[160,128]{1,0:T(8,128)S(1)}, u32[]{:S(2)}, u32[]{:S(2)}) collective-permute-start(f32[160,128]{1,0:T(8,128)S(1)} %pad_maximum_fusion.22), channel_id=1, source_target_pairs={{0,16},{2,10},{4,20},{6,14},{8,24},{10,2},{12,28},{14,6},{16,0},{1... | collective-permute-start | bytes 245768 | tf_op jit(solution)/shard_map/while/body/ppermute | solution.py:510
  48.6 5.4 %collective-permute-start.10 = (f32[160,128]{1,0:T(8,128)S(1)}, f32[160,128]{1,0:T(8,128)S(1)}, u32[]{:S(2)}, u32[]{:S(2)}) collective-permute-start(f32[160,128]{1,0:T(8,128)S(1)} %pad_maximum_fusion.26), channel_id=1, source_target_pairs={{0,16},{2,10},{4,20},{6,14},{8,24},{10,2},{12,28},{14,6},{16,0},{1... | collective-permute-start | bytes 245768 | tf_op jit(solution)/shard_map/while/body/ppermute | solution.py:510
  51.0 5.6 %collective-permute-start.7 = (f32[320,128]{1,0:T(8,128)S(1)}, f32[320,128]{1,0:T(8,128)S(1)}, u32[]{:S(2)}, u32[]{:S(2)}) collective-permute-start(f32[320,128]{1,0:T(8,128)S(1)} %pad_maximum_fusion.23), channel_id=1, source_target_pairs={{0,8},{2,6},{4,12},{6,2},{8,0},{10,14},{12,4},{14,10},{16,24},{18,... | collective-permute-start | bytes 491528 | tf_op jit(solution)/shard_map/while/body/ppermute | solution.py:510
  54.0 5.6 %collective-permute-start.11 = (f32[320,128]{1,0:T(8,128)S(1)}, f32[320,128]{1,0:T(8,128)S(1)}, u32[]{:S(2)}, u32[]{:S(2)}) collective-permute-start(f32[320,128]{1,0:T(8,128)S(1)} %pad_maximum_fusion.27), channel_id=1, source_target_pairs={{0,8},{2,6},{4,12},{6,2},{8,0},{10,14},{12,4},{14,10},{16,24},{18,... | collective-permute-start | bytes 491528 | tf_op jit(solution)/shard_map/while/body/ppermute | solution.py:510
  56.7 3.1 %collective-permute-start.8 = (f32[640,128]{1,0:T(8,128)S(1)}, f32[640,128]{1,0:T(8,128)S(1)}, u32[]{:S(2)}, u32[]{:S(2)}) collective-permute-start(f32[640,128]{1,0:T(8,128)S(1)} %pad_maximum_fusion.24), channel_id=1, source_target_pairs={{0,2},{2,0},{4,6},{6,4},{8,10},{10,8},{12,14},{14,12},{16,18},{18,... | collective-permute-start | bytes 983048 | tf_op jit(solution)/shard_map/while/body/ppermute | solution.py:510
  59.7 1.7 collective-permute-start.12
  62.3 27.8 %copy-start.3 = (f32[1280,128]{1,0:T(8,128)S(1)}, f32[1280,128]{1,0:T(8,128)}, u32[]{:S(2)}) copy-start(f32[1280,128]{1,0:T(8,128)} %get-tuple-element.216.refs_3_.g_ref) | copy-start | bytes 1966084
  62.3 36.6 %collective-permute-start.24 = (f32[512,512]{1,0:T(8,128)}, f32[512,512]{1,0:T(8,128)}, u32[]{:S(2)}, u32[]{:S(2)}) collective-permute-start(f32[512,512]{1,0:T(8,128)} %get-tuple-element.219), channel_id=1, source_target_pairs={{0,1},{1,0},{2,3},{3,2},{4,5},{5,4},{6,7},{7,6},{8,9},{9,8},{10,11... | collective-permute-start | bytes 3145736 | tf_op jit(solution)/shard_map/ppermute | solution.py:580
  84.9 62.3 %collective-permute-start.25 = (f32[1024,512]{1,0:T(8,128)}, f32[1024,512]{1,0:T(8,128)}, u32[]{:S(2)}, u32[]{:S(2)}) collective-permute-start(f32[1024,512]{1,0:T(8,128)} %get-tuple-element.222), channel_id=1, source_target_pairs={{0,1},{2,3},{4,5},{6,7},{8,9},{10,11},{12,13},{14,15},{16,17},{18,... | collective-permute-start | bytes 6291464 | tf_op jit(solution)/shard_map/ppermute | solution.py:583
  88.7 1.4 copy-start.2
  97.5 91.9 %collective-permute-start.23 = (f32[1024,512]{1,0:T(8,128)}, f32[1024,512]{1,0:T(8,128)S(1)}, u32[]{:S(2)}, u32[]{:S(2)}) collective-permute-start(f32[1024,512]{1,0:T(8,128)} %get-tuple-element.217), channel_id=1, source_target_pairs={{0,1},{2,3},{4,5},{6,7},{8,9},{10,11},{12,13},{14,15},{16,17},{18,... | collective-permute-start | bytes 6291464 | tf_op jit(solution)/shard_map/ppermute | solution.py:583
  102.2 2.0 %collective-permute-start.13 = (f32[256,512]{1,0:T(8,128)S(1)}, f32[256,512]{1,0:T(8,128)S(1)}, u32[]{:S(2)}, u32[]{:S(2)}) collective-permute-start(f32[256,512]{1,0:T(8,128)S(1)} %slice_select_fusion.18), channel_id=1, source_target_pairs={{0,2},{2,0},{4,6},{6,4},{8,10},{10,8},{12,14},{14,12},{16,18},{18,... | collective-permute-start | bytes 1572872 | tf_op jit(solution)/shard_map/while/body/ppermute | solution.py:510
  104.4 6.4 %collective-permute-start.14 = (f32[128,512]{1,0:T(8,128)S(1)}, f32[128,512]{1,0:T(8,128)S(1)}, u32[]{:S(2)}, u32[]{:S(2)}) collective-permute-start(f32[128,512]{1,0:T(8,128)S(1)} %slice_select_fusion.19), channel_id=1, source_target_pairs={{0,8},{2,6},{4,12},{6,2},{8,0},{10,14},{12,4},{14,10},{16,24},{18,... | collective-permute-start | bytes 786440 | tf_op jit(solution)/shard_map/while/body/ppermute | solution.py:510
  110.9 6.0 %collective-permute-start.15 = (f32[64,512]{1,0:T(8,128)S(1)}, f32[64,512]{1,0:T(8,128)S(1)}, u32[]{:S(2)}, u32[]{:S(2)}) collective-permute-start(f32[64,512]{1,0:T(8,128)S(1)} %slice_select_fusion.20), channel_id=1, source_target_pairs={{0,16},{2,10},{4,20},{6,14},{8,24},{10,2},{12,28},{14,6},{16,0},{1... | collective-permute-start | bytes 393224 | tf_op jit(solution)/shard_map/while/body/ppermute | solution.py:510
  117.0 8.1 %collective-permute-start.16 = (f32[64,512]{1,0:T(8,128)S(1)}, f32[64,512]{1,0:T(8,128)S(1)}, u32[]{:S(2)}, u32[]{:S(2)}) collective-permute-start(f32[64,512]{1,0:T(8,128)S(1)} %select_add_fusion.20), channel_id=1, source_target_pairs={{0,5},{2,19},{4,1},{6,23},{8,13},{10,27},{12,9},{14,31},{16,21},{1... | collective-permute-start | bytes 393224 | tf_op jit(solution)/shard_map/while/body/ppermute | solution.py:516
  125.1 5.0 %collective-permute-start.17 = (f32[64,512]{1,0:T(8,128)S(1)}, f32[64,512]{1,0:T(8,128)S(1)}, u32[]{:S(2)}, u32[]{:S(2)}) collective-permute-start(f32[64,512]{1,0:T(8,128)S(1)} %add.111), channel_id=1, source_target_pairs={{0,4},{2,18},{4,0},{6,22},{8,12},{10,26},{12,8},{14,30},{16,20},{1... | collective-permute-start | bytes 393224 | tf_op jit(solution)/shard_map/while/body/ppermute | solution.py:510
  130.2 7.3 %collective-permute-start.18 = (f32[64,512]{1,0:T(8,128)S(1)}, f32[64,512]{1,0:T(8,128)S(1)}, u32[]{:S(2)}, u32[]{:S(2)}) collective-permute-start(f32[64,512]{1,0:T(8,128)S(1)} %add.112), channel_id=1, source_target_pairs={{0,16},{2,10},{4,20},{6,14},{8,24},{10,2},{12,28},{14,6},{16,0},{1... | collective-permute-start | bytes 393224 | tf_op jit(solution)/shard_map/while/body/ppermute | solution.py:510
  137.6 6.4 %collective-permute-start.19 = (f32[128,512]{1,0:T(8,128)S(1)}, f32[128,512]{1,0:T(8,128)S(1)}, u32[]{:S(2)}, u32[]{:S(2)}) collective-permute-start(f32[128,512]{1,0:T(8,128)S(1)} %pad_maximum_fusion.30), channel_id=1, source_target_pairs={{0,8},{2,6},{4,12},{6,2},{8,0},{10,14},{12,4},{14,10},{16,24},{18,... | collective-permute-start | bytes 786440 | tf_op jit(solution)/shard_map/while/body/ppermute | solution.py:510
  144.9 2.1 %collective-permute-start.20 = (f32[256,512]{1,0:T(8,128)}, f32[256,512]{1,0:T(8,128)S(1)}, u32[]{:S(2)}, u32[]{:S(2)}) collective-permute-start(f32[256,512]{1,0:T(8,128)} %pad_maximum_fusion.31), channel_id=1, source_target_pairs={{0,2},{2,0},{4,6},{6,4},{8,10},{10,8},{12,14},{14,12},{16,18},{18,... | collective-permute-start | bytes 1572872 | tf_op jit(solution)/shard_map/while/body/ppermute | solution.py:510
  183.8 1.6 copy-start
  185.4 1.4 copy-start.1

commit v6 on v5

--- a/solution.py
+++ b/solution.py
@@ -209,16 +209,14 @@
         c = GROUP * p
         pa = [jnp.broadcast_to(a[p][k : k + 1, :], shape) for k in range(GROUP)]
         px = [jnp.broadcast_to(x[p][k : k + 1, :], shape) for k in range(GROUP)]
-        s = [
-            [jnp.broadcast_to(pa[k][:, c + l : c + l + 1], shape) if l >= k else None for l in range(GROUP)]
-            for k in range(GROUP)
-        ]
+        corner = [jnp.broadcast_to(a[p][:, c + l : c + l + 1], shape) for l in range(GROUP)]
+        s = [[jnp.broadcast_to(corner[l][k : k + 1, :], shape) for l in range(GROUP)] for k in range(GROUP)]
         reciprocal = []
         for k in range(GROUP):
             reciprocal.append(1.0 / s[k][k])
             for l in range(k + 1, GROUP):
-                m = s[k][l] * reciprocal[k]
-                for t in range(l, GROUP):
+                m = s[l][k] * reciprocal[k]
+                for t in range(k + 1, GROUP):
                     s[l][t] = s[l][t] - m * s[k][t]
                 pa[l] = pa[l] - m * pa[k]
                 px[l] = px[l] - m * px[k]

time: 193 us -> 193 us (level)
  Pallas kernels: 85.9 us -> 88 us
  transfers between devices with their start and end apart: 26 -> 26, of which waited for: 20 -> 20; matrix products, arithmetic and copies ran while one was open for 2% -> 2% of each run, Pallas kernels for 42% -> 43%
where the time goes in v6:
time: 193 us; the launch traced here: 192 us
  Pallas kernels  88 us (46%)
  waiting for transfers between devices  51.9 us (27%)
  starting transfers between devices  43 us (22%)
  local copies, waits for them, and re-layouts  5.19 us (3%)
  other arithmetic  2.89 us (1%)
    ppermute x19, waiting for transfers between devices, flip(): lax.ppermute(x, 'dof', [(i, i ^ order[i % 2][step]) for i in range(count)])  45.8 us
    pallas_call x1, Pallas kernels, finish(): pl.pallas_call(functools.partial(finish_kernel, counts), out_shape=[jax.S...  37.6 us
    ppermute x19, starting transfers between devices, flip(): lax.ppermute(x, 'dof', [(i, i ^ order[i % 2][step]) for i in range(count)])  25.8 us
    pallas_call x1, Pallas kernels, first_factor(): pl.pallas_call(functools.partial(first_factor_kernel, start), out_shape=[...  22.2 us
    pallas_call x1, Pallas kernels, own_gram(): pl.pallas_call(functools.partial(own_gram_kernel, scale, spans), grid_spe...  12.8 us
    pallas_call x2, Pallas kernels, cross_gram(): pl.pallas_call(functools.partial(cross_gram_kernel, scale, before is not...  10.6 us
    ppermute x2, starting transfers between devices, flip_side(): return lax.ppermute(x, ('dof', 'snap'), pairs)  7.36 us
    ppermute x2, starting transfers between devices, one_way(): return lax.ppermute(x, 'snap', [(0, 1)])  5.2 us
  transfers between devices with their start and end apart: 26, of which 20 were waited for; matrix products, arithmetic and copies ran while one was open for 2% of the time, Pallas kernels for 43%

profile of v6, /device:TPU:0, one launch (start us, length us, event | category | flops | bytes accessed | tf_op | source)
XLA Modules:
  0.0 192.2 jit_solution(7790372128629099086)
XLA Ops:
  0.6 2.0 %pick.1 = f32[512,512]{1,0:T(8,128)} custom-call(s32[1]{0:T(128)} %bitcast.side_ref, f32[4096,512]{1,0:T(8,128)} %own_hbm.1), custom_call_target="tpu_custom_call" | custom-call | flops 1 | bytes 1 | tf_op jit(solution)/shard_map/pick/pallas_call | solution.py:65
  2.7 3.0 %collective-permute-start.21 = (f32[512,512]{1,0:T(8,128)}, f32[512,512]{1,0:T(8,128)}, u32[]{:S(2)}, u32[]{:S(2)}) collective-permute-start(f32[512,512]{1,0:T(8,128)} %pick.1), channel_id=1, source_target_pairs={{0,1},{1,0},{2,3},{3,2},{4,5},{5,4},{6,7},{7,6},{8,9},{9,8},{10,11... | collective-permute-start | bytes 3145736 | tf_op jit(solution)/shard_map/ppermute | solution.py:578
  5.7 12.8 %own_gram.1 = (f32[1280,128]{1,0:T(8,128)S(1)}, f32[1024,512]{1,0:T(8,128)}, f32[512,512]{1,0:T(8,128)}) custom-call(s32[1]{0:T(128)} %bitcast.side_ref, f32[4096,512]{1,0:T(8,128)} %own_hbm.1), custom_call_target="tpu_custom_call" | custom-call | flops 1 | bytes 1 | tf_op jit(solution)/shard_map/own_gram/pallas_call | solution.py:123
  19.4 42.9 %while.26 = (s32[]{:T(128)}, f32[1280,128]{1,0:T(8,128)S(1)}, f32[1280,128]{1,0:T(8,128)}, s32[]{:T(128)}, pred[]{:T(512)}, /*index=5*/pred[]{:T(512)}, pred[]{:...) while((s32[]{:T(128)}, f32[1280,128]{1,0:T(8,128)S(1)}, ...), condition=%wide.region_1.2_spmd, body=%wide.region_0.1_spmd.sunk | while | flops 1996802 | bytes 21832332 | solution.py:590
  21.2 2.1 %collective-permute-start.1 = (f32[320,128]{1,0:T(8,128)S(1)}, f32[320,128]{1,0:T(8,128)S(1)}, u32[]{:S(2)}, u32[]{:S(2)}) collective-permute-start(f32[320,128]{1,0:T(8,128)S(1)} %slice_select_fusion.15), channel_id=1, source_target_pairs={{0,8},{2,6},{4,12},{6,2},{8,0},{10,14},{12,4},{14,10},{16,24},{18,... | collective-permute-start | bytes 491528 | tf_op jit(solution)/shard_map/while/body/ppermute | solution.py:508
  23.3 3.3 %collective-permute-done.1 = f32[320,128]{1,0:T(8,128)S(1)} collective-permute-done((f32[320,128]{1,0:T(8,128)S(1)}, f32[320,128]{1,0:T(8,128)S(1)}, u32[]{:S(2)}, u32[]{:S(2)}) %collective-permute-start.1) | collective-permute-done | bytes 163872 | tf_op jit(solution)/shard_map/while/body/ppermute | solution.py:508
  26.6 3.1 %collective-permute-start.2 = (f32[160,128]{1,0:T(8,128)S(1)}, f32[160,128]{1,0:T(8,128)S(1)}, u32[]{:S(2)}, u32[]{:S(2)}) collective-permute-start(f32[160,128]{1,0:T(8,128)S(1)} %slice_select_fusion.16), channel_id=1, source_target_pairs={{0,16},{2,10},{4,20},{6,14},{8,24},{10,2},{12,28},{14,6},{16,0},{1... | collective-permute-start | bytes 245768 | tf_op jit(solution)/shard_map/while/body/ppermute | solution.py:508
  29.7 2.4 %collective-permute-done.2 = f32[160,128]{1,0:T(8,128)S(1)} collective-permute-done((f32[160,128]{1,0:T(8,128)S(1)}, f32[160,128]{1,0:T(8,128)S(1)}, u32[]{:S(2)}, u32[]{:S(2)}) %collective-permute-start.2) | collective-permute-done | bytes 81952 | tf_op jit(solution)/shard_map/while/body/ppermute | solution.py:508
  34.1 2.2 %collective-permute-done.3 = f32[80,128]{1,0:T(8,128)S(1)} collective-permute-done((f32[80,128]{1,0:T(8,128)S(1)}, f32[80,128]{1,0:T(8,128)S(1)}, u32[]{:S(2)}, u32[]{:S(2)}) %collective-permute-start.3) | collective-permute-done | bytes 40992 | tf_op jit(solution)/shard_map/while/body/ppermute | solution.py:508
  36.3 2.8 %collective-permute-start.4 = (f32[80,128]{1,0:T(8,128)S(1)}, f32[80,128]{1,0:T(8,128)S(1)}, u32[]{:S(2)}, u32[]{:S(2)}) collective-permute-start(f32[80,128]{1,0:T(8,128)S(1)} %select_add_fusion.17), channel_id=1, source_target_pairs={{0,5},{1,4},{2,19},{3,18},{4,1},{5,0},{6,23},{7,22},{8,13},{9,12},... | collective-permute-start | bytes 122888 | tf_op jit(solution)/shard_map/while/body/ppermute | solution.py:514
  39.1 2.3 %collective-permute-done.4 = f32[80,128]{1,0:T(8,128)S(1)} collective-permute-done((f32[80,128]{1,0:T(8,128)S(1)}, f32[80,128]{1,0:T(8,128)S(1)}, u32[]{:S(2)}, u32[]{:S(2)}) %collective-permute-start.4) | collective-permute-done | bytes 40992 | tf_op jit(solution)/shard_map/while/body/ppermute | solution.py:514
  45.5 3.1 %collective-permute-start.6 = (f32[160,128]{1,0:T(8,128)S(1)}, f32[160,128]{1,0:T(8,128)S(1)}, u32[]{:S(2)}, u32[]{:S(2)}) collective-permute-start(f32[160,128]{1,0:T(8,128)S(1)} %pad_maximum_fusion.22), channel_id=1, source_target_pairs={{0,16},{2,10},{4,20},{6,14},{8,24},{10,2},{12,28},{14,6},{16,0},{1... | collective-permute-start | bytes 245768 | tf_op jit(solution)/shard_map/while/body/ppermute | solution.py:508
  51.0 2.3 %collective-permute-start.7 = (f32[320,128]{1,0:T(8,128)S(1)}, f32[320,128]{1,0:T(8,128)S(1)}, u32[]{:S(2)}, u32[]{:S(2)}) collective-permute-start(f32[320,128]{1,0:T(8,128)S(1)} %pad_maximum_fusion.23), channel_id=1, source_target_pairs={{0,8},{2,6},{4,12},{6,2},{8,0},{10,14},{12,4},{14,10},{16,24},{18,... | collective-permute-start | bytes 491528 | tf_op jit(solution)/shard_map/while/body/ppermute | solution.py:508
  54.0 2.3 %collective-permute-start.11 = (f32[320,128]{1,0:T(8,128)S(1)}, f32[320,128]{1,0:T(8,128)S(1)}, u32[]{:S(2)}, u32[]{:S(2)}) collective-permute-start(f32[320,128]{1,0:T(8,128)S(1)} %pad_maximum_fusion.27), channel_id=1, source_target_pairs={{0,8},{2,6},{4,12},{6,2},{8,0},{10,14},{12,4},{14,10},{16,24},{18,... | collective-permute-start | bytes 491528 | tf_op jit(solution)/shard_map/while/body/ppermute | solution.py:508
  56.7 2.9 %collective-permute-done.11 = f32[320,128]{1,0:T(8,128)S(1)} collective-permute-done((f32[320,128]{1,0:T(8,128)S(1)}, f32[320,128]{1,0:T(8,128)S(1)}, u32[]{:S(2)}, u32[]{:S(2)}) %collective-permute-start.11) | collective-permute-done | bytes 163872 | tf_op jit(solution)/shard_map/while/body/ppermute | solution.py:508
  63.8 22.2 %first_factor.1 = (f32[512,512]{1,0:T(8,128)}, f32[512,512]{1,0:T(8,128)}, f32[1024,512]{1,0:T(8,128)}, f32[1024,512]{1,0:T(8,128)}) custom-call(f32[1280,128]{1,0:T(8,128)S(1)} %get-tuple-element.212.g_ref, f32[4096,512]{1,0:T(8,128)} %own_hbm.1), custom_call_target="tpu_custom_call" | custom-call | flops 1 | bytes 1 | tf_op jit(solution)/shard_map/first_factor/pallas_call | solution.py:313
  86.0 3.8 %collective-permute-start.25 = (f32[1024,512]{1,0:T(8,128)}, f32[1024,512]{1,0:T(8,128)}, u32[]{:S(2)}, u32[]{:S(2)}) collective-permute-start(f32[1024,512]{1,0:T(8,128)} %get-tuple-element.222), channel_id=1, source_target_pairs={{0,1},{2,3},{4,5},{6,7},{8,9},{10,11},{12,13},{14,15},{16,17},{18,... | collective-permute-start | bytes 6291464 | tf_op jit(solution)/shard_map/ppermute | solution.py:581
  91.1 7.4 %cross_gram.2.refs_1_ = f32[512,512]{1,0:T(8,128)} custom-call(s32[1]{0:T(128)} %bitcast.side_ref, f32[4096,512]{1,0:T(8,128)} %own_hbm.1, f32[512,512]{1,0:T(8,128)} %collective-permute-done.21.refs_0_, f32[1024,512]{1,0:T(8,128)} %copy-done.2, f32[512,512]{1,0:T(8,128)} %get-tuple-element.215.refs_2_.x0_ref, f32[1280,128]{1,0:T(8,128)S(1)} %copy-done.3), custom_call_target="tpu_custom_call" | custom-call | flops 1 | bytes 1 | tf_op jit(solution)/shard_map/cross_gram/pallas_call | solution.py:186
  100.0 3.2 %cross_gram.3 = f32[512,512]{1,0:T(8,128)S(1)} custom-call(s32[1]{0:T(128)} %bitcast.side_ref, f32[4096,512]{1,0:T(8,128)} %own_hbm.1, f32[512,512]{1,0:T(8,128)} %collective-permute-done.24.refs_0_.refs_2_, f32[512,512]{1,0:T(8,128)} %cross_gram.2.refs_1_), custom_call_target="tpu_custom_call" | custom-call | flops 1 | bytes 1 | tf_op jit(solution)/shard_map/cross_gram/pallas_call | solution.py:186
  103.2 44.0 %while.27 = (s32[]{:T(128)}, f32[512,512]{1,0:T(8,128)S(1)}, s32[]{:T(128)}, pred[]{:T(512)}, pred[]{:T(512)}, /*index=5*/pred[]{:T(512)}, s32[]{:T(128)}) while((s32[]{:T(128)}, f32[512,512]{1,0:T(8,128)S(1)}, s32[]{:T(128)}, pred[]{:T(512)}, pred[]{:T(512)}, /*index=5*/pred[]{:T(512)}, s32[]{:T(128)}) %tuple.92), condition=%wide.region_3.4_spmd, body=%wide.region_2.3_spmd.sunk | while | flops 1867778 | bytes 22938004 | solution.py:598
  105.5 2.1 %collective-permute-start.14 = (f32[128,512]{1,0:T(8,128)S(1)}, f32[128,512]{1,0:T(8,128)S(1)}, u32[]{:S(2)}, u32[]{:S(2)}) collective-permute-start(f32[128,512]{1,0:T(8,128)S(1)} %slice_select_fusion.19), channel_id=1, source_target_pairs={{0,8},{2,6},{4,12},{6,2},{8,0},{10,14},{12,4},{14,10},{16,24},{18,... | collective-permute-start | bytes 786440 | tf_op jit(solution)/shard_map/while/body/ppermute | solution.py:508
  107.6 4.4 %collective-permute-done.14 = f32[128,512]{1,0:T(8,128)S(1)} collective-permute-done((f32[128,512]{1,0:T(8,128)S(1)}, f32[128,512]{1,0:T(8,128)S(1)}, u32[]{:S(2)}, u32[]{:S(2)}) %collective-permute-start.14) | collective-permute-done | bytes 262176 | tf_op jit(solution)/shard_map/while/body/ppermute | solution.py:508
  112.0 3.0 %collective-permute-start.15 = (f32[64,512]{1,0:T(8,128)S(1)}, f32[64,512]{1,0:T(8,128)S(1)}, u32[]{:S(2)}, u32[]{:S(2)}) collective-permute-start(f32[64,512]{1,0:T(8,128)S(1)} %slice_select_fusion.20), channel_id=1, source_target_pairs={{0,16},{2,10},{4,20},{6,14},{8,24},{10,2},{12,28},{14,6},{16,0},{1... | collective-permute-start | bytes 393224 | tf_op jit(solution)/shard_map/while/body/ppermute | solution.py:508
  115.0 3.0 %collective-permute-done.15 = f32[64,512]{1,0:T(8,128)S(1)} collective-permute-done((f32[64,512]{1,0:T(8,128)S(1)}, f32[64,512]{1,0:T(8,128)S(1)}, u32[]{:S(2)}, u32[]{:S(2)}) %collective-permute-start.15) | collective-permute-done | bytes 131104 | tf_op jit(solution)/shard_map/while/body/ppermute | solution.py:508
  118.0 4.5 %collective-permute-start.16 = (f32[64,512]{1,0:T(8,128)S(1)}, f32[64,512]{1,0:T(8,128)S(1)}, u32[]{:S(2)}, u32[]{:S(2)}) collective-permute-start(f32[64,512]{1,0:T(8,128)S(1)} %select_add_fusion.20), channel_id=1, source_target_pairs={{0,5},{2,19},{4,1},{6,23},{8,13},{10,27},{12,9},{14,31},{16,21},{1... | collective-permute-start | bytes 393224 | tf_op jit(solution)/shard_map/while/body/ppermute | solution.py:514
  122.6 2.5 %collective-permute-done.16 = f32[64,512]{1,0:T(8,128)S(1)} collective-permute-done((f32[64,512]{1,0:T(8,128)S(1)}, f32[64,512]{1,0:T(8,128)S(1)}, u32[]{:S(2)}, u32[]{:S(2)}) %collective-permute-start.16) | collective-permute-done | bytes 131104 | tf_op jit(solution)/shard_map/while/body/ppermute | solution.py:514
  125.7 4.4 %collective-permute-done.17 = f32[64,512]{1,0:T(8,128)S(1)} collective-permute-done((f32[64,512]{1,0:T(8,128)S(1)}, f32[64,512]{1,0:T(8,128)S(1)}, u32[]{:S(2)}, u32[]{:S(2)}) %collective-permute-start.17) | collective-permute-done | bytes 131104 | tf_op jit(solution)/shard_map/while/body/ppermute | solution.py:508
  131.5 6.0 %collective-permute-done.18 = f32[64,512]{1,0:T(8,128)S(1)} collective-permute-done((f32[64,512]{1,0:T(8,128)S(1)}, f32[64,512]{1,0:T(8,128)S(1)}, u32[]{:S(2)}, u32[]{:S(2)}) %collective-permute-start.18) | collective-permute-done | bytes 131104 | tf_op jit(solution)/shard_map/while/body/ppermute | solution.py:508
  137.6 6.4 %collective-permute-done.19 = f32[128,512]{1,0:T(8,128)S(1)} collective-permute-done((f32[128,512]{1,0:T(8,128)S(1)}, f32[128,512]{1,0:T(8,128)S(1)}, u32[]{:S(2)}, u32[]{:S(2)}) %collective-permute-start.19) | collective-permute-done | bytes 262176 | tf_op jit(solution)/shard_map/while/body/ppermute | solution.py:508
  144.9 2.1 %collective-permute-done.20 = f32[256,512]{1,0:T(8,128)S(1)} collective-permute-done((f32[256,512]{1,0:T(8,128)}, f32[256,512]{1,0:T(8,128)S(1)}, u32[]{:S(2)}, u32[]{:S(2)}) %collective-permute-start.20) | collective-permute-done | bytes 524320 | tf_op jit(solution)/shard_map/while/body/ppermute | solution.py:508
  147.2 37.6 %finish.1 = (f32[1024,512]{1,0:T(8,128)}, bf16[1536,512]{1,0:T(8,128)(2,1)}, f32[1024,512]{1,0:T(8,128)}, f32[4096,512]{1,0:T(8,128)}) custom-call(s32[1]{0:T(128)} %bitcast.side_ref, f32[512,512]{1,0:T(8,128)S(1)} %get-tuple-element.220.cross_ref, f32[1280,128]{1,0:T(8,128)} %get-tuple-element.216.refs_3_.g_ref, f32[512,512]{1,0:T(8,128)} %get-tuple-element.221.r00_ref, ...), custom_call_target="tpu_custom_call" | custom-call | flops 1 | bytes 1 | tf_op jit(solution)/shard_map/finish/pallas_call | solution.py:428
  189.4 2.6 %tail.1 = f32[4096,512]{1,0:T(8,128)} custom-call(f32[1024,512]{1,0:T(8,128)S(1)} %collective-permute-done.23.chunk_ref, bf16[1536,512]{1,0:T(8,128)(2,1)S(1)} %get-tuple-element.225.factor_ref, f32[1024,512]{1,0:T(8,128)S(1)} %get-tuple-element.226.part_ref, f32[4096,512]{1,0:T(8,128)} %get-tuple-element.227.before_hbm), custom_call_target="tpu_custom_call", output_to_operand_aliasing={{}: (3, {})} | custom-call | flops 1 | bytes 1 | tf_op jit(solution)/shard_map/tail/pallas_call | solution.py:493
  (78 shorter events, 29.3 us)
Async XLA Ops:
  2.7 87.1 %collective-permute-start.21 = (f32[512,512]{1,0:T(8,128)}, f32[512,512]{1,0:T(8,128)}, u32[]{:S(2)}, u32[]{:S(2)}) collective-permute-start(f32[512,512]{1,0:T(8,128)} %pick.1), channel_id=1, source_target_pairs={{0,1},{1,0},{2,3},{3,2},{4,5},{5,4},{6,7},{7,6},{8,9},{9,8},{10,11... | collective-permute-start | bytes 3145736 | tf_op jit(solution)/shard_map/ppermute | solution.py:578
  18.5 71.3 %collective-permute-start.22 = (f32[1024,512]{1,0:T(8,128)}, f32[1024,512]{1,0:T(8,128)S(1)}, u32[]{:S(2)}, u32[]{:S(2)}) collective-permute-start(f32[1024,512]{1,0:T(8,128)} %get-tuple-element.214), channel_id=1, source_target_pairs={{0,1},{1,0},{2,3},{3,2},{4,5},{5,4},{6,7},{7,6},{8,9},{9,8},{10,11... | collective-permute-start | bytes 6291464 | tf_op jit(solution)/shard_map/ppermute | solution.py:578
  19.4 1.7 collective-permute-start
  21.2 5.4 %collective-permute-start.1 = (f32[320,128]{1,0:T(8,128)S(1)}, f32[320,128]{1,0:T(8,128)S(1)}, u32[]{:S(2)}, u32[]{:S(2)}) collective-permute-start(f32[320,128]{1,0:T(8,128)S(1)} %slice_select_fusion.15), channel_id=1, source_target_pairs={{0,8},{2,6},{4,12},{6,2},{8,0},{10,14},{12,4},{14,10},{16,24},{18,... | collective-permute-start | bytes 491528 | tf_op jit(solution)/shard_map/while/body/ppermute | solution.py:508
  26.6 5.5 %collective-permute-start.2 = (f32[160,128]{1,0:T(8,128)S(1)}, f32[160,128]{1,0:T(8,128)S(1)}, u32[]{:S(2)}, u32[]{:S(2)}) collective-permute-start(f32[160,128]{1,0:T(8,128)S(1)} %slice_select_fusion.16), channel_id=1, source_target_pairs={{0,16},{2,10},{4,20},{6,14},{8,24},{10,2},{12,28},{14,6},{16,0},{1... | collective-permute-start | bytes 245768 | tf_op jit(solution)/shard_map/while/body/ppermute | solution.py:508
  32.2 4.1 %collective-permute-start.3 = (f32[80,128]{1,0:T(8,128)S(1)}, f32[80,128]{1,0:T(8,128)S(1)}, u32[]{:S(2)}, u32[]{:S(2)}) collective-permute-start(f32[80,128]{1,0:T(8,128)S(1)} %slice_select_fusion.17), channel_id=1, source_target_pairs={{0,4},{2,18},{4,0},{6,22},{8,12},{10,26},{12,8},{14,30},{16,20},{1... | collective-permute-start | bytes 122888 | tf_op jit(solution)/shard_map/while/body/ppermute | solution.py:508
  36.3 5.1 %collective-permute-start.4 = (f32[80,128]{1,0:T(8,128)S(1)}, f32[80,128]{1,0:T(8,128)S(1)}, u32[]{:S(2)}, u32[]{:S(2)}) collective-permute-start(f32[80,128]{1,0:T(8,128)S(1)} %select_add_fusion.17), channel_id=1, source_target_pairs={{0,5},{1,4},{2,19},{3,18},{4,1},{5,0},{6,23},{7,22},{8,13},{9,12},... | collective-permute-start | bytes 122888 | tf_op jit(solution)/shard_map/while/body/ppermute | solution.py:514
  41.4 4.1 %collective-permute-start.5 = (f32[80,128]{1,0:T(8,128)S(1)}, f32[80,128]{1,0:T(8,128)S(1)}, u32[]{:S(2)}, u32[]{:S(2)}) collective-permute-start(f32[80,128]{1,0:T(8,128)S(1)} %get-tuple-element.409), channel_id=1, source_target_pairs={{0,4},{2,18},{4,0},{6,22},{8,12},{10,26},{12,8},{14,30},{16,20},{1... | collective-permute-start | bytes 122888 | tf_op jit(solution)/shard_map/while/body/ppermute | solution.py:508
  43.2 5.3 %collective-permute-start.9 = (f32[80,128]{1,0:T(8,128)S(1)}, f32[80,128]{1,0:T(8,128)S(1)}, u32[]{:S(2)}, u32[]{:S(2)}) collective-permute-start(f32[80,128]{1,0:T(8,128)S(1)} %get-tuple-element.418), channel_id=1, source_target_pairs={{0,4},{2,18},{4,0},{6,22},{8,12},{10,26},{12,8},{14,30},{16,20},{1... | collective-permute-start | bytes 122888 | tf_op jit(solution)/shard_map/while/body/ppermute | solution.py:508
  45.5 5.5 %collective-permute-start.6 = (f32[160,128]{1,0:T(8,128)S(1)}, f32[160,128]{1,0:T(8,128)S(1)}, u32[]{:S(2)}, u32[]{:S(2)}) collective-permute-start(f32[160,128]{1,0:T(8,128)S(1)} %pad_maximum_fusion.22), channel_id=1, source_target_pairs={{0,16},{2,10},{4,20},{6,14},{8,24},{10,2},{12,28},{14,6},{16,0},{1... | collective-permute-start | bytes 245768 | tf_op jit(solution)/shard_map/while/body/ppermute | solution.py:508
  48.6 5.4 %collective-permute-start.10 = (f32[160,128]{1,0:T(8,128)S(1)}, f32[160,128]{1,0:T(8,128)S(1)}, u32[]{:S(2)}, u32[]{:S(2)}) collective-permute-start(f32[160,128]{1,0:T(8,128)S(1)} %pad_maximum_fusion.26), channel_id=1, source_target_pairs={{0,16},{2,10},{4,20},{6,14},{8,24},{10,2},{12,28},{14,6},{16,0},{1... | collective-permute-start | bytes 245768 | tf_op jit(solution)/shard_map/while/body/ppermute | solution.py:508
  51.0 5.6 %collective-permute-start.7 = (f32[320,128]{1,0:T(8,128)S(1)}, f32[320,128]{1,0:T(8,128)S(1)}, u32[]{:S(2)}, u32[]{:S(2)}) collective-permute-start(f32[320,128]{1,0:T(8,128)S(1)} %pad_maximum_fusion.23), channel_id=1, source_target_pairs={{0,8},{2,6},{4,12},{6,2},{8,0},{10,14},{12,4},{14,10},{16,24},{18,... | collective-permute-start | bytes 491528 | tf_op jit(solution)/shard_map/while/body/ppermute | solution.py:508
  54.0 5.6 %collective-permute-start.11 = (f32[320,128]{1,0:T(8,128)S(1)}, f32[320,128]{1,0:T(8,128)S(1)}, u32[]{:S(2)}, u32[]{:S(2)}) collective-permute-start(f32[320,128]{1,0:T(8,128)S(1)} %pad_maximum_fusion.27), channel_id=1, source_target_pairs={{0,8},{2,6},{4,12},{6,2},{8,0},{10,14},{12,4},{14,10},{16,24},{18,... | collective-permute-start | bytes 491528 | tf_op jit(solution)/shard_map/while/body/ppermute | solution.py:508
  56.7 3.1 %collective-permute-start.8 = (f32[640,128]{1,0:T(8,128)S(1)}, f32[640,128]{1,0:T(8,128)S(1)}, u32[]{:S(2)}, u32[]{:S(2)}) collective-permute-start(f32[640,128]{1,0:T(8,128)S(1)} %pad_maximum_fusion.24), channel_id=1, source_target_pairs={{0,2},{2,0},{4,6},{6,4},{8,10},{10,8},{12,14},{14,12},{16,18},{18,... | collective-permute-start | bytes 983048 | tf_op jit(solution)/shard_map/while/body/ppermute | solution.py:508
  59.7 1.7 collective-permute-start.12
  62.3 28.8 %copy-start.3 = (f32[1280,128]{1,0:T(8,128)S(1)}, f32[1280,128]{1,0:T(8,128)}, u32[]{:S(2)}) copy-start(f32[1280,128]{1,0:T(8,128)} %get-tuple-element.216.refs_3_.g_ref) | copy-start | bytes 1966084
  62.3 37.7 %collective-permute-start.24 = (f32[512,512]{1,0:T(8,128)}, f32[512,512]{1,0:T(8,128)}, u32[]{:S(2)}, u32[]{:S(2)}) collective-permute-start(f32[512,512]{1,0:T(8,128)} %get-tuple-element.219), channel_id=1, source_target_pairs={{0,1},{1,0},{2,3},{3,2},{4,5},{5,4},{6,7},{7,6},{8,9},{9,8},{10,11... | collective-permute-start | bytes 3145736 | tf_op jit(solution)/shard_map/ppermute | solution.py:578
  86.0 61.2 %collective-permute-start.25 = (f32[1024,512]{1,0:T(8,128)}, f32[1024,512]{1,0:T(8,128)}, u32[]{:S(2)}, u32[]{:S(2)}) collective-permute-start(f32[1024,512]{1,0:T(8,128)} %get-tuple-element.222), channel_id=1, source_target_pairs={{0,1},{2,3},{4,5},{6,7},{8,9},{10,11},{12,13},{14,15},{16,17},{18,... | collective-permute-start | bytes 6291464 | tf_op jit(solution)/shard_map/ppermute | solution.py:581
  89.8 1.4 copy-start.2
  98.5 90.9 %collective-permute-start.23 = (f32[1024,512]{1,0:T(8,128)}, f32[1024,512]{1,0:T(8,128)S(1)}, u32[]{:S(2)}, u32[]{:S(2)}) collective-permute-start(f32[1024,512]{1,0:T(8,128)} %get-tuple-element.217), channel_id=1, source_target_pairs={{0,1},{2,3},{4,5},{6,7},{8,9},{10,11},{12,13},{14,15},{16,17},{18,... | collective-permute-start | bytes 6291464 | tf_op jit(solution)/shard_map/ppermute | solution.py:581
  103.3 2.0 %collective-permute-start.13 = (f32[256,512]{1,0:T(8,128)S(1)}, f32[256,512]{1,0:T(8,128)S(1)}, u32[]{:S(2)}, u32[]{:S(2)}) collective-permute-start(f32[256,512]{1,0:T(8,128)S(1)} %slice_select_fusion.18), channel_id=1, source_target_pairs={{0,2},{2,0},{4,6},{6,4},{8,10},{10,8},{12,14},{14,12},{16,18},{18,... | collective-permute-start | bytes 1572872 | tf_op jit(solution)/shard_map/while/body/ppermute | solution.py:508
  105.5 6.4 %collective-permute-start.14 = (f32[128,512]{1,0:T(8,128)S(1)}, f32[128,512]{1,0:T(8,128)S(1)}, u32[]{:S(2)}, u32[]{:S(2)}) collective-permute-start(f32[128,512]{1,0:T(8,128)S(1)} %slice_select_fusion.19), channel_id=1, source_target_pairs={{0,8},{2,6},{4,12},{6,2},{8,0},{10,14},{12,4},{14,10},{16,24},{18,... | collective-permute-start | bytes 786440 | tf_op jit(solution)/shard_map/while/body/ppermute | solution.py:508
  112.0 6.0 %collective-permute-start.15 = (f32[64,512]{1,0:T(8,128)S(1)}, f32[64,512]{1,0:T(8,128)S(1)}, u32[]{:S(2)}, u32[]{:S(2)}) collective-permute-start(f32[64,512]{1,0:T(8,128)S(1)} %slice_select_fusion.20), channel_id=1, source_target_pairs={{0,16},{2,10},{4,20},{6,14},{8,24},{10,2},{12,28},{14,6},{16,0},{1... | collective-permute-start | bytes 393224 | tf_op jit(solution)/shard_map/while/body/ppermute | solution.py:508
  118.0 7.1 %collective-permute-start.16 = (f32[64,512]{1,0:T(8,128)S(1)}, f32[64,512]{1,0:T(8,128)S(1)}, u32[]{:S(2)}, u32[]{:S(2)}) collective-permute-start(f32[64,512]{1,0:T(8,128)S(1)} %select_add_fusion.20), channel_id=1, source_target_pairs={{0,5},{2,19},{4,1},{6,23},{8,13},{10,27},{12,9},{14,31},{16,21},{1... | collective-permute-start | bytes 393224 | tf_op jit(solution)/shard_map/while/body/ppermute | solution.py:514
  125.1 5.0 %collective-permute-start.17 = (f32[64,512]{1,0:T(8,128)S(1)}, f32[64,512]{1,0:T(8,128)S(1)}, u32[]{:S(2)}, u32[]{:S(2)}) collective-permute-start(f32[64,512]{1,0:T(8,128)S(1)} %add.111), channel_id=1, source_target_pairs={{0,4},{2,18},{4,0},{6,22},{8,12},{10,26},{12,8},{14,30},{16,20},{1... | collective-permute-start | bytes 393224 | tf_op jit(solution)/shard_map/while/body/ppermute | solution.py:508
  130.2 7.3 %collective-permute-start.18 = (f32[64,512]{1,0:T(8,128)S(1)}, f32[64,512]{1,0:T(8,128)S(1)}, u32[]{:S(2)}, u32[]{:S(2)}) collective-permute-start(f32[64,512]{1,0:T(8,128)S(1)} %add.112), channel_id=1, source_target_pairs={{0,16},{2,10},{4,20},{6,14},{8,24},{10,2},{12,28},{14,6},{16,0},{1... | collective-permute-start | bytes 393224 | tf_op jit(solution)/shard_map/while/body/ppermute | solution.py:508
  137.6 6.4 %collective-permute-start.19 = (f32[128,512]{1,0:T(8,128)S(1)}, f32[128,512]{1,0:T(8,128)S(1)}, u32[]{:S(2)}, u32[]{:S(2)}) collective-permute-start(f32[128,512]{1,0:T(8,128)S(1)} %pad_maximum_fusion.30), channel_id=1, source_target_pairs={{0,8},{2,6},{4,12},{6,2},{8,0},{10,14},{12,4},{14,10},{16,24},{18,... | collective-permute-start | bytes 786440 | tf_op jit(solution)/shard_map/while/body/ppermute | solution.py:508
  144.9 2.1 %collective-permute-start.20 = (f32[256,512]{1,0:T(8,128)}, f32[256,512]{1,0:T(8,128)S(1)}, u32[]{:S(2)}, u32[]{:S(2)}) collective-permute-start(f32[256,512]{1,0:T(8,128)} %pad_maximum_fusion.31), channel_id=1, source_target_pairs={{0,2},{2,0},{4,6},{6,4},{8,10},{10,8},{12,14},{14,12},{16,18},{18,... | collective-permute-start | bytes 1572872 | tf_op jit(solution)/shard_map/while/body/ppermute | solution.py:508
  184.8 1.6 copy-start
  186.4 1.4 copy-start.1
